TPU v7x, 32 devices: a whole 2x2x4 slice. The times are simulated.
32 devices in a mesh: dp: 4 (over z), seq: 2 (over x), mp: 4 (over y, core).
Axes of the slice: x: 2, y: 2, z: 4, core: 2. Of those that a mesh axis runs over, the one named last changes fastest.
Arguments:
- inputs: bfloat16 [2048, 1536], P(('dp', 'seq')), may hold values from -6 to 6
- cotangent: bfloat16 [2048, 1536], P(('dp', 'seq')), may hold values from -6 to 6
- segments: int32 [2048], P('dp'), may hold values from 0 to 4, as said below
- positions: int32 [2048], P(('dp', 'seq')), may hold values from 0 to 255, as said below
- w_query: bfloat16 [1536, 1536], P(('dp', 'seq'), 'mp'), may hold values from -0.15625 to 0.15625
- w_key: bfloat16 [1536, 256], P(('dp', 'seq', 'mp')), may hold values from -0.15625 to 0.15625
- w_value: bfloat16 [1536, 256], P(('dp', 'seq', 'mp')), may hold values from -0.15625 to 0.15625
- bias_query: bfloat16 [1536], P(('dp', 'seq', 'mp')), may hold values from -1.5 to 1.5
- bias_key: bfloat16 [256], P(('dp', 'seq', 'mp')), may hold values from -3 to 3
- bias_value: bfloat16 [256], P(('dp', 'seq', 'mp')), may hold values from -3 to 3
- w_out: bfloat16 [1536, 1536], P('mp', ('dp', 'seq')), may hold values from -1 to 1
- gain_attn: bfloat16 [1536], P(('dp', 'seq', 'mp')), may hold values from 0.5 to 1.5
- gain_ffn: bfloat16 [1536], P(('dp', 'seq', 'mp')), may hold values from 0.5 to 1.5
- w_gate: bfloat16 [1536, 8960], P(('dp', 'seq'), 'mp'), may hold values from -0.15625 to 0.15625
- w_up: bfloat16 [1536, 8960], P(('dp', 'seq'), 'mp'), may hold values from -0.15625 to 0.15625
- w_down: bfloat16 [8960, 1536], P('mp', ('dp', 'seq')), may hold values from -0.5 to 0.5
Outputs:
- output: float32 [2048, 1536], P(('dp', 'seq'))
- input_grad: float32 [2048, 1536], P(('dp', 'seq'))
- grad_query: float32 [1536, 1536], P(('dp', 'seq'), 'mp')
- grad_key: float32 [1536, 256], P(('dp', 'seq', 'mp'))
- grad_value: float32 [1536, 256], P(('dp', 'seq', 'mp'))
- grad_bias_q: float32 [1536], P(('dp', 'seq', 'mp'))
- grad_bias_k: float32 [256], replicated
- grad_bias_v: float32 [256], P(('dp', 'seq', 'mp'))
- grad_out: float32 [1536, 1536], P('mp', ('dp', 'seq'))
- grad_gain_attn: float32 [1536], P(('dp', 'seq', 'mp'))
- grad_gain_ffn: float32 [1536], P(('dp', 'seq', 'mp'))
- grad_gate: float32 [1536, 8960], P(('dp', 'seq'), 'mp')
- grad_up: float32 [1536, 8960], P(('dp', 'seq'), 'mp')
- grad_down: float32 [8960, 1536], P('mp', ('dp', 'seq'))
Inputs may be any that keep to these rules, and one draw needn't show every extreme that they name: `segments`: within each sequence of 512 tokens the ids never fall; a token attends only to tokens with its id; no document is longer than 256 tokens. `positions`: the index of each token within its document.
All inputs are finite; a program needn't handle non-finite values.
Results may differ from a plain program's by a relative error of at most 0.022.
The roundings to bfloat16 on the way count: a program that leaves them out, or rounds other values in their place, can miss the bound.
Values may be sent and summed in bfloat16 or wider, within the bound.
No kernel may reach another device: no remote copies, remote signals or barrier semaphores. Data moves between devices by JAX's collectives and lax.ppermute only.
A program may use at most 192 MiB of HBM per device.

v0:
```python
import math

import jax
import jax.numpy as jnp
from jax import lax
from jax.sharding import PartitionSpec as P

D = 1536
H = 12
KVH = 2
HD = 128


EPSILON = 1e-06
ROPE_BASE = 1000000.0
NEG_BIG = -1e30


def inverse_rms(values):
    return lax.rsqrt(jnp.mean(values * values, axis=-1, keepdims=True) + EPSILON)


def norm_backward(upstream, values, inv_scale, gain_vec):
    scaled = upstream * gain_vec
    return inv_scale * scaled - values * (inv_scale * inv_scale * inv_scale) * jnp.mean(
        scaled * values, axis=-1, keepdims=True
    )


def rope_tables(positions):
    steps_half = jnp.arange(0, HD, 2).astype(jnp.float32)
    frequency = jnp.exp(steps_half * (-math.log(ROPE_BASE) / HD))
    angles = positions.astype(jnp.float32)[:, None] * frequency[None, :]
    angles = jnp.concatenate([angles, angles], axis=-1)
    return (jnp.cos(angles), jnp.sin(angles))


def rotate(values, cosine, sine_table):
    half_width = values.shape[-1] // 2
    turned = jnp.concatenate([-values[..., half_width:], values[..., :half_width]], axis=-1)
    return values * cosine + turned * sine_table


def head_forward(query_rows, key_rows, value_rows, mask_table, score_scale):
    scores = jnp.dot(query_rows, key_rows.T, preferred_element_type=jnp.float32) * score_scale
    scores = jnp.where(mask_table, scores, NEG_BIG)
    row_max = jnp.max(scores, axis=-1, keepdims=True)
    row_total = jnp.sum(
        jnp.where(mask_table, jnp.exp(scores - row_max), 0.0), axis=-1, keepdims=True
    )
    log_total = row_max + jnp.log(row_total)
    prob_cast = jnp.where(mask_table, jnp.exp(scores - log_total), 0.0).astype(jnp.bfloat16)
    attended = jnp.dot(prob_cast, value_rows, preferred_element_type=jnp.float32).astype(
        jnp.bfloat16
    )
    return (attended, log_total)


def head_backward(
    query_rows, key_rows, value_rows, mask_table, score_scale, log_total, attended, diff_attended
):
    scores = jnp.dot(query_rows, key_rows.T, preferred_element_type=jnp.float32) * score_scale
    scores = jnp.where(mask_table, scores, NEG_BIG)
    prob_full = jnp.where(mask_table, jnp.exp(scores - log_total), 0.0)
    prob_cast = prob_full.astype(jnp.bfloat16)
    value_part = jnp.dot(prob_cast.T, diff_attended, preferred_element_type=jnp.float32)
    diff_probs = jnp.dot(diff_attended, value_rows.T, preferred_element_type=jnp.float32)
    row_delta = jnp.sum(
        diff_attended.astype(jnp.float32) * attended.astype(jnp.float32), axis=-1, keepdims=True
    )
    diff_scores = (prob_full * (diff_probs - row_delta) * score_scale).astype(jnp.bfloat16)
    diff_query = jnp.dot(diff_scores, key_rows, preferred_element_type=jnp.float32)
    key_part = jnp.dot(diff_scores.T, query_rows, preferred_element_type=jnp.float32)
    return (diff_query, key_part, value_part)


def local_pieces(small_full, mp_index, heads_local):
    key_full, value_full, bias_q_full, bias_k_full, bias_v_full, gain_one, gain_two = small_full
    group_size = H // KVH
    kv_head = mp_index * heads_local // group_size
    key_local = lax.dynamic_slice_in_dim(key_full, kv_head * HD, HD, 1)
    value_local = lax.dynamic_slice_in_dim(value_full, kv_head * HD, HD, 1)
    bias_q_local = lax.dynamic_slice_in_dim(
        bias_q_full, mp_index * heads_local * HD, heads_local * HD, 0
    )
    bias_k_local = lax.dynamic_slice_in_dim(bias_k_full, kv_head * HD, HD, 0)
    bias_v_local = lax.dynamic_slice_in_dim(bias_v_full, kv_head * HD, HD, 0)
    return (
        kv_head,
        key_local,
        value_local,
        bias_q_local,
        bias_k_local,
        bias_v_local,
        gain_one,
        gain_two,
    )


def on_device(
    inputs,
    cotangent,
    segments,
    positions,
    w_query,
    w_key,
    w_value,
    bias_query,
    bias_key,
    bias_value,
    w_out,
    gain_attn,
    gain_ffn,
    w_gate,
    w_up,
    w_down,
):
    local_rows = inputs.shape[0]
    seq_length = segments.shape[0]
    mp_index = lax.axis_index("mp")
    seq_index = lax.axis_index("seq")
    score_scale = HD ** (-0.5)
    big_full = (
        lax.all_gather(w_query, ("dp", "seq"), axis=0, tiled=True),
        lax.all_gather(w_out, ("dp", "seq"), axis=1, tiled=True),
        lax.all_gather(w_gate, ("dp", "seq"), axis=0, tiled=True),
        lax.all_gather(w_up, ("dp", "seq"), axis=0, tiled=True),
        lax.all_gather(w_down, ("dp", "seq"), axis=1, tiled=True),
    )
    small_full = (
        lax.all_gather(w_key, ("dp", "seq", "mp"), axis=0, tiled=True),
        lax.all_gather(w_value, ("dp", "seq", "mp"), axis=0, tiled=True),
        lax.all_gather(bias_query, ("dp", "seq", "mp"), axis=0, tiled=True),
        lax.all_gather(bias_key, ("dp", "seq", "mp"), axis=0, tiled=True),
        lax.all_gather(bias_value, ("dp", "seq", "mp"), axis=0, tiled=True),
        lax.all_gather(gain_attn, ("dp", "seq", "mp"), axis=0, tiled=True),
        lax.all_gather(gain_ffn, ("dp", "seq", "mp"), axis=0, tiled=True),
    )
    query_full, out_full, gate_full, up_full, down_full = big_full
    heads_local = query_full.shape[1] // HD
    (
        kv_head,
        key_local,
        value_local,
        bias_q_local,
        bias_k_local,
        bias_v_local,
        gain_one,
        gain_two,
    ) = local_pieces(small_full, mp_index, heads_local)
    in_float = inputs.astype(jnp.float32)
    inv_one = inverse_rms(in_float)
    normed_one = (in_float * inv_one * gain_one.astype(jnp.float32)).astype(jnp.bfloat16)
    query_proj = jnp.dot(
        normed_one, query_full, preferred_element_type=jnp.float32
    ) + bias_q_local.astype(jnp.float32)
    key_proj = jnp.dot(
        normed_one, key_local, preferred_element_type=jnp.float32
    ) + bias_k_local.astype(jnp.float32)
    value_proj = jnp.dot(
        normed_one, value_local, preferred_element_type=jnp.float32
    ) + bias_v_local.astype(jnp.float32)
    cosine, sine_table = rope_tables(positions)
    query_rot = rotate(
        query_proj.reshape(local_rows, heads_local, HD), cosine[:, None, :], sine_table[:, None, :]
    ).astype(jnp.bfloat16)
    key_rot = rotate(key_proj, cosine, sine_table).astype(jnp.bfloat16)
    value_cast = value_proj.astype(jnp.bfloat16)
    keys_all, values_all = (
        lax.all_gather(key_rot, "seq", axis=0, tiled=True),
        lax.all_gather(value_cast, "seq", axis=0, tiled=True),
    )
    query_start = seq_index * local_rows
    query_segments = lax.dynamic_slice_in_dim(segments, query_start, local_rows, 0)
    query_order = query_start + jnp.arange(local_rows, dtype=jnp.int32)
    key_order = jnp.arange(seq_length, dtype=jnp.int32)
    mask_table = (query_segments[:, None] == segments[None, :]) & (
        key_order[None, :] <= query_order[:, None]
    )
    attended_list = []
    total_list = []
    for head_number in range(heads_local):
        attended_head, total_head = head_forward(
            query_rot[:, head_number], keys_all, values_all, mask_table, score_scale
        )
        attended_list.append(attended_head)
        total_list.append(total_head)
    attended_flat = jnp.concatenate(attended_list, axis=1)
    attn_branch = lax.psum(
        jnp.dot(attended_flat, out_full, preferred_element_type=jnp.float32), "mp"
    )
    hidden_res = in_float + attn_branch
    inv_two = inverse_rms(hidden_res)
    normed_two = (hidden_res * inv_two * gain_two.astype(jnp.float32)).astype(jnp.bfloat16)
    gate_proj = jnp.dot(normed_two, gate_full, preferred_element_type=jnp.float32)
    up_proj = jnp.dot(normed_two, up_full, preferred_element_type=jnp.float32)
    sigmoid_gate = jax.nn.sigmoid(gate_proj)
    silu_gate = gate_proj * sigmoid_gate
    hidden_act = (silu_gate * up_proj).astype(jnp.bfloat16)
    ffn_branch = lax.psum(
        jnp.dot(hidden_act, down_full, preferred_element_type=jnp.float32).astype(jnp.bfloat16),
        "mp",
    ).astype(jnp.float32)
    output = hidden_res + ffn_branch
    big_back = (
        lax.all_gather(w_query, ("dp", "seq"), axis=0, tiled=True),
        lax.all_gather(w_out, ("dp", "seq"), axis=1, tiled=True),
        lax.all_gather(w_gate, ("dp", "seq"), axis=0, tiled=True),
        lax.all_gather(w_up, ("dp", "seq"), axis=0, tiled=True),
        lax.all_gather(w_down, ("dp", "seq"), axis=1, tiled=True),
    )
    small_back = (
        lax.all_gather(w_key, ("dp", "seq", "mp"), axis=0, tiled=True),
        lax.all_gather(w_value, ("dp", "seq", "mp"), axis=0, tiled=True),
        lax.all_gather(bias_query, ("dp", "seq", "mp"), axis=0, tiled=True),
        lax.all_gather(bias_key, ("dp", "seq", "mp"), axis=0, tiled=True),
        lax.all_gather(bias_value, ("dp", "seq", "mp"), axis=0, tiled=True),
        lax.all_gather(gain_attn, ("dp", "seq", "mp"), axis=0, tiled=True),
        lax.all_gather(gain_ffn, ("dp", "seq", "mp"), axis=0, tiled=True),
    )
    query_full, out_full, gate_full, up_full, down_full = big_back
    (
        kv_head,
        key_local,
        value_local,
        bias_q_local,
        bias_k_local,
        bias_v_local,
        gain_one,
        gain_two,
    ) = local_pieces(small_back, mp_index, heads_local)
    cot_float = cotangent.astype(jnp.float32)
    grad_down = jnp.dot(hidden_act.T, cotangent, preferred_element_type=jnp.float32)
    diff_hidden = jnp.dot(cotangent, down_full.T, preferred_element_type=jnp.float32)
    diff_gate = (
        diff_hidden * up_proj * sigmoid_gate * (1.0 + gate_proj * (1.0 - sigmoid_gate))
    ).astype(jnp.bfloat16)
    diff_up = (diff_hidden * silu_gate).astype(jnp.bfloat16)
    grad_gate = jnp.dot(normed_two.T, diff_gate, preferred_element_type=jnp.float32)
    grad_up = jnp.dot(normed_two.T, diff_up, preferred_element_type=jnp.float32)
    diff_normed_two = lax.psum(
        jnp.dot(diff_gate, gate_full.T, preferred_element_type=jnp.float32)
        + jnp.dot(diff_up, up_full.T, preferred_element_type=jnp.float32),
        "mp",
    )
    first_copy = (mp_index == 0).astype(jnp.float32)
    grad_gain_ffn = jnp.sum(diff_normed_two * hidden_res * inv_two, axis=0) * first_copy
    diff_res = cot_float + norm_backward(
        diff_normed_two, hidden_res, inv_two, gain_two.astype(jnp.float32)
    )
    diff_res_cast = diff_res.astype(jnp.bfloat16)
    grad_out = jnp.dot(attended_flat.T, diff_res_cast, preferred_element_type=jnp.float32)
    diff_attended = jnp.dot(diff_res_cast, out_full.T, preferred_element_type=jnp.float32).astype(
        jnp.bfloat16
    )
    diff_attended = diff_attended.reshape(local_rows, heads_local, HD)
    query_list = []
    key_list = []
    value_list = []
    for head_number in range(heads_local):
        diff_query, key_part, value_part = head_backward(
            query_rot[:, head_number],
            keys_all,
            values_all,
            mask_table,
            score_scale,
            total_list[head_number],
            attended_list[head_number],
            diff_attended[:, head_number],
        )
        query_list.append(diff_query)
        key_list.append(key_part)
        value_list.append(value_part)
    diff_query_all = jnp.stack(query_list, axis=1)
    key_parts = jnp.concatenate(key_list, axis=1)
    value_parts = jnp.concatenate(value_list, axis=1)
    key_mine, value_mine = (
        lax.psum_scatter(key_parts, "seq", scatter_dimension=0, tiled=True),
        lax.psum_scatter(value_parts, "seq", scatter_dimension=0, tiled=True),
    )
    query_pre = rotate(diff_query_all, cosine[:, None, :], -sine_table[:, None, :]).reshape(
        local_rows, heads_local * HD
    )
    key_pre = rotate(
        key_mine.reshape(local_rows, heads_local, HD), cosine[:, None, :], -sine_table[:, None, :]
    ).reshape(local_rows, heads_local * HD)
    grad_bq_local = jnp.sum(query_pre, axis=0)
    grad_bk_local = jnp.sum(key_pre, axis=0).reshape(heads_local, HD).sum(axis=0)
    grad_bv_local = jnp.sum(value_mine, axis=0).reshape(heads_local, HD).sum(axis=0)
    query_cast = query_pre.astype(jnp.bfloat16)
    key_cast = key_pre.astype(jnp.bfloat16)
    value_cast_part = value_mine.astype(jnp.bfloat16)
    grad_query = jnp.dot(normed_one.T, query_cast, preferred_element_type=jnp.float32)
    grad_key_local = (
        jnp.dot(normed_one.T, key_cast, preferred_element_type=jnp.float32)
        .reshape(D, heads_local, HD)
        .sum(axis=1)
    )
    grad_value_local = (
        jnp.dot(normed_one.T, value_cast_part, preferred_element_type=jnp.float32)
        .reshape(D, heads_local, HD)
        .sum(axis=1)
    )
    key_tiled = jnp.tile(key_local, (1, heads_local))
    value_tiled = jnp.tile(value_local, (1, heads_local))
    diff_normed_one = lax.psum(
        (
            jnp.dot(query_cast, query_full.T, preferred_element_type=jnp.float32)
            + jnp.dot(key_cast, key_tiled.T, preferred_element_type=jnp.float32)
            + jnp.dot(value_cast_part, value_tiled.T, preferred_element_type=jnp.float32)
        ).astype(jnp.bfloat16),
        "mp",
    ).astype(jnp.float32)
    grad_gain_attn = jnp.sum(diff_normed_one * in_float * inv_one, axis=0) * first_copy
    input_grad = diff_res + norm_backward(
        diff_normed_one, in_float, inv_one, gain_one.astype(jnp.float32)
    )
    grad_key_full = lax.dynamic_update_slice_in_dim(
        jnp.zeros((D, KVH * HD), jnp.float32), grad_key_local, kv_head * HD, 1
    )
    grad_value_full = lax.dynamic_update_slice_in_dim(
        jnp.zeros((D, KVH * HD), jnp.float32), grad_value_local, kv_head * HD, 1
    )
    grad_bq_full = lax.dynamic_update_slice_in_dim(
        jnp.zeros((H * HD,), jnp.float32), grad_bq_local, mp_index * heads_local * HD, 0
    )
    grad_bk_full = lax.dynamic_update_slice_in_dim(
        jnp.zeros((KVH * HD,), jnp.float32), grad_bk_local, kv_head * HD, 0
    )
    grad_bv_full = lax.dynamic_update_slice_in_dim(
        jnp.zeros((KVH * HD,), jnp.float32), grad_bv_local, kv_head * HD, 0
    )
    big_grads = (
        lax.psum_scatter(
            grad_query.astype(jnp.bfloat16), ("dp", "seq"), scatter_dimension=0, tiled=True
        ).astype(jnp.float32),
        lax.psum_scatter(
            grad_out.astype(jnp.bfloat16), ("dp", "seq"), scatter_dimension=1, tiled=True
        ).astype(jnp.float32),
        lax.psum_scatter(
            grad_gate.astype(jnp.bfloat16), ("dp", "seq"), scatter_dimension=0, tiled=True
        ).astype(jnp.float32),
        lax.psum_scatter(
            grad_up.astype(jnp.bfloat16), ("dp", "seq"), scatter_dimension=0, tiled=True
        ).astype(jnp.float32),
        lax.psum_scatter(
            grad_down.astype(jnp.bfloat16), ("dp", "seq"), scatter_dimension=1, tiled=True
        ).astype(jnp.float32),
    )
    small_grads = (
        lax.psum_scatter(grad_key_full, ("dp", "seq", "mp"), scatter_dimension=0, tiled=True),
        lax.psum_scatter(grad_value_full, ("dp", "seq", "mp"), scatter_dimension=0, tiled=True),
        lax.psum_scatter(grad_bq_full, ("dp", "seq", "mp"), scatter_dimension=0, tiled=True),
        lax.psum_scatter(grad_bv_full, ("dp", "seq", "mp"), scatter_dimension=0, tiled=True),
        lax.psum_scatter(grad_gain_attn, ("dp", "seq", "mp"), scatter_dimension=0, tiled=True),
        lax.psum_scatter(grad_gain_ffn, ("dp", "seq", "mp"), scatter_dimension=0, tiled=True),
    )
    key_bias_total = lax.psum(grad_bk_full, ("dp", "seq", "mp"))
    return (
        output,
        input_grad,
        big_grads[0],
        small_grads[0],
        small_grads[1],
        small_grads[2],
        key_bias_total,
        small_grads[3],
        big_grads[1],
        small_grads[4],
        small_grads[5],
        big_grads[2],
        big_grads[3],
        big_grads[4],
    )


def solution(mesh):
    in_specs = (
        P(("dp", "seq"), None),
        P(("dp", "seq"), None),
        P("dp"),
        P(("dp", "seq")),
        P(("dp", "seq"), "mp"),
        P(("dp", "seq", "mp"), None),
        P(("dp", "seq", "mp"), None),
        P(("dp", "seq", "mp")),
        P(("dp", "seq", "mp")),
        P(("dp", "seq", "mp")),
        P("mp", ("dp", "seq")),
        P(("dp", "seq", "mp")),
        P(("dp", "seq", "mp")),
        P(("dp", "seq"), "mp"),
        P(("dp", "seq"), "mp"),
        P("mp", ("dp", "seq")),
    )
    out_specs = (
        P(("dp", "seq"), None),
        P(("dp", "seq"), None),
        P(("dp", "seq"), "mp"),
        P(("dp", "seq", "mp"), None),
        P(("dp", "seq", "mp"), None),
        P(("dp", "seq", "mp")),
        P(),
        P(("dp", "seq", "mp")),
        P("mp", ("dp", "seq")),
        P(("dp", "seq", "mp")),
        P(("dp", "seq", "mp")),
        P(("dp", "seq"), "mp"),
        P(("dp", "seq"), "mp"),
        P("mp", ("dp", "seq")),
    )
    return jax.shard_map(
        on_device, mesh=mesh, in_specs=in_specs, out_specs=out_specs, check_vma=False
    )
```

profile of v0, /device:TPU:0, one launch (start us, length us, event | category | flops | bytes accessed | tf_op | source)
XLA Modules:
  0.0 1430.2 jit_solution(12653649811309736795)
XLA Ops:
  8.8 47.1 %all_gather.54 = bf16[1536,256]{1,0:T(8,128)(2,1)S(1)} all-gather(bf16[48,256]{1,0:T(8,128)(2,1)} %param.21), channel_id=1, replica_groups=mesh['dp'=4,'seq'=2,'mp'=4] {'dp','seq','mp'}, dimensions={0}, use_global_device_ids=true | all-gather | bytes 811008 | tf_op jit(solution)/shard_map/all_gather | solution.py:131
  60.1 37.4 %all-reduce.10 = (bf16[256]{0:T(256)(128)(2,1)S(1)}, bf16[1536]{0:T(1024)(128)(2,1)S(1)}, bf16[256]{0:T(256)(128)(2,1)S(1)}, bf16[1536]{0:T(1024)(128)(2,1)S(1)}, bf16[1536]{0:T(1024)(128)(2,1)S(1)}) all-reduce(bf16[256]{0:T(256)(128)(2,1)S(1)} %dynamic-update-slice.3, ...), channel_id=1, replica_groups=mesh['dp'=4,'seq'=2,'mp'=4] {'dp','seq','mp'}, use_global_device_ids=true, to_apply=%add.3 | all-reduce | flops 5120 | bytes 20480
  99.1 1.1 fusion.53
  100.2 5.2 all_gather.56
  105.4 41.9 %all_gather.57 = bf16[1536,256]{1,0:T(8,128)(2,1)S(1)} all-gather(bf16[48,256]{1,0:T(8,128)(2,1)S(1)} %copy-done.52), channel_id=1, replica_groups=mesh['dp'=4,'seq'=2,'mp'=4] {'dp','seq','mp'}, dimensions={0}, use_global_device_ids=true | all-gather | bytes 811008 | tf_op jit(solution)/shard_map/all_gather | solution.py:132
  147.8 5.0 all_gather.59
  153.0 1.9 convolution_add_fusion.3
  158.2 3.0 fusion.46
  163.2 37.0 %all-reduce.16.cloned.1.call-done = f32[256,1536]{1,0:T(8,128)} async-done(((f32[256,1536]{1,0:T(8,128)}), f32[256,1536]{1,0:T(8,128)}) %all-reduce.16.cloned.1.call-update) | async-done | bytes 1572880 | tf_op jit(solution)/shard_map/psum | solution.py:189
  200.3 1.7 multiply_reduce_fusion.2
  202.8 108.4 %all-gather.10.cloned.1.call-done = bf16[1536,2240]{1,0:T(8,128)(2,1)} async-done(((bf16[192,2240]{1,0:T(8,128)(2,1)}), bf16[1536,2240]{1,0:T(8,128)(2,1)}) %all-gather.10.cloned.1.call-update) | async-done | bytes 6881296 | tf_op jit(solution)/shard_map/all_gather | solution.py:126
  311.2 7.3 fusion.77
  318.5 101.8 %all-gather.12.cloned.1.call-done = bf16[1536,2240]{1,0:T(8,128)(2,1)} async-done(((bf16[192,2240]{1,0:T(8,128)(2,1)}), bf16[1536,2240]{1,0:T(8,128)(2,1)}) %all-gather.12.cloned.1.call-update) | async-done | bytes 6881296 | tf_op jit(solution)/shard_map/all_gather | solution.py:127
  420.3 7.3 fusion.78
  427.6 101.7 %all-gather.14.cloned.1.call-done = bf16[2240,1536]{0,1:T(8,128)(2,1)} async-done(((bf16[2240,192]{0,1:T(8,128)(2,1)}), bf16[2240,1536]{0,1:T(8,128)(2,1)}) %all-gather.14.cloned.1.call-update) | async-done | bytes 6881296 | tf_op jit(solution)/shard_map/all_gather | solution.py:128
  529.3 8.9 multiply_convert_fusion
  538.2 6.0 fusion.79
  544.2 3.5 convolution_add_fusion.2
  549.6 0.9 copy.49
  550.6 38.4 %all-reduce.18.cloned.1.call-done = f32[256,1536]{1,0:T(8,128)} async-done(((f32[256,1536]{1,0:T(8,128)}), f32[256,1536]{1,0:T(8,128)}) %all-reduce.18.cloned.1.call-update) | async-done | bytes 1572880 | tf_op jit(solution)/shard_map/psum | solution.py:241
  589.0 2.6 multiply_reduce_fusion
  592.8 1.3 convolution_convert_fusion.6
  594.1 1.7 copy.47
  595.9 1.1 multiply_reduce_fusion.5
  597.0 1.5 fusion.23
  600.2 1.0 fusion.49
  602.3 6.4 convolution_convert_fusion.5
  613.4 1.0 pad_maximum_fusion.2
  615.2 4.6 reduce-scatter.10.cloned.1.call-done
  619.8 1.1 slice_negate_fusion
  620.9 2.0 add_reduce_fusion
  625.1 1.7 convolution_add_fusion.1
  626.8 13.4 reduce-scatter.12.cloned.1.call-done
  640.3 1.3 copy-done.3
  641.6 2.5 fusion
  645.0 1.6 convolution_convert_fusion.3
  646.8 2.8 convolution_convert_fusion.4
  649.9 6.4 convolution_convert_fusion.2
  656.4 6.5 convolution_convert_fusion.1
  663.0 6.4 convolution_convert_fusion
  670.4 3.2 fusion.41
  673.6 2.8 reduce_sum.184
  676.5 2.3 copy.51
  678.7 1.3 broadcast.122.clone.1
  680.2 1.0 constant_dynamic-update-slice_fusion
  682.1 1.9 convolution_reduce_fusion
  684.0 1.3 broadcast.122.clone
  685.3 1.0 constant_dynamic-update-slice_fusion.1
  687.4 1.8 fusion.11
  689.2 40.7 %all-reduce.9 = (f32[1536]{0:T(1024)S(1)}, f32[256]{0:T(256)}, f32[256]{0:T(256)S(1)}, f32[1536]{0:T(1024)S(1)}, f32[1536]{0:T(1024)S(1)}) all-reduce(f32[1536]{0:T(1024)S(1)} %bitcast_dynamic-update-slice_fusion, f32[256]{0:T(256)S(1)} %dynamic_update_slice.18, ...), channel_id=7, replica_groups=mesh['dp'=4,'seq'=2,'mp'=4] {'dp','seq','mp'}, use_global_device_ids=true, to_apply=%region_25.26.clone | all-reduce | flops 5120 | bytes 40960
  732.2 23.4 %reduce-scatter.20.cloned.1.call-done = bf16[384,192]{0,1:T(8,128)(2,1)} async-done(((bf16[384,1536]{0,1:T(8,128)(2,1)}), bf16[384,192]{0,1:T(8,128)(2,1)}) %reduce-scatter.20.cloned.1.call-update) | async-done | bytes 147472 | tf_op jit(solution)/shard_map/reduce_scatter | solution.py:337
  755.7 1.6 convert_element_type.209
  757.3 2.6 convert_add_fusion.1
  759.9 1.6 fusion.4
  761.5 61.0 %reduce-scatter.14.cloned.1.call-done = bf16[192,384]{1,0:T(8,128)(2,1)} async-done(((bf16[1536,384]{1,0:T(8,128)(2,1)}), bf16[192,384]{1,0:T(8,128)(2,1)}) %reduce-scatter.14.cloned.1.call-update) | async-done | bytes 147472 | tf_op jit(solution)/shard_map/reduce_scatter | solution.py:334
  822.5 1.6 convert_element_type.207
  824.2 130.1 %reduce-scatter.22.cloned.1.call-done = bf16[192,2240]{1,0:T(8,128)(2,1)} async-done(((bf16[1536,2240]{1,0:T(8,128)(2,1)}), bf16[192,2240]{1,0:T(8,128)(2,1)}) %reduce-scatter.22.cloned.1.call-update) | async-done | bytes 860176 | tf_op jit(solution)/shard_map/reduce_scatter | solution.py:340
  954.3 2.5 convert_element_type.212
  956.8 129.6 %reduce-scatter.24.cloned.1.call-done = bf16[192,2240]{1,0:T(8,128)(2,1)} async-done(((bf16[1536,2240]{1,0:T(8,128)(2,1)}), bf16[192,2240]{1,0:T(8,128)(2,1)}) %reduce-scatter.24.cloned.1.call-update) | async-done | bytes 860176 | tf_op jit(solution)/shard_map/reduce_scatter | solution.py:343
  1086.3 2.5 convert_element_type.214
  1088.8 129.2 %reduce-scatter.26.cloned.1.call-done = bf16[2240,192]{0,1:T(8,128)(2,1)} async-done(((bf16[2240,1536]{0,1:T(8,128)(2,1)}), bf16[2240,192]{0,1:T(8,128)(2,1)}) %reduce-scatter.26.cloned.1.call-update) | async-done | bytes 860176 | tf_op jit(solution)/shard_map/reduce_scatter | solution.py:346
  1218.0 2.5 convert_element_type.216
  1220.5 100.2 %reduce-scatter.18.cloned.1.call-done = f32[48,256]{1,0:T(8,128)} async-done(((f32[1536,256]{1,0:T(8,128)}), f32[48,256]{1,0:T(8,128)}) %reduce-scatter.18.cloned.1.call-update) | async-done | bytes 49168 | tf_op jit(solution)/shard_map/reduce_scatter | solution.py:352
  1320.7 102.6 %reduce-scatter.16.cloned.1.call-done = f32[48,256]{1,0:T(8,128)} async-done(((f32[1536,256]{1,0:T(8,128)}), f32[48,256]{1,0:T(8,128)}) %reduce-scatter.16.cloned.1.call-update) | async-done | bytes 49168 | tf_op jit(solution)/shard_map/reduce_scatter | solution.py:351
  (273 shorter events, 33.9 us)
Async XLA Ops:
  7.2 90.5 %copy-start = (bf16[256,1536]{1,0:T(8,128)(2,1)S(1)}, bf16[256,1536]{1,0:T(8,128)(2,1)}, u32[]{:S(2)}) copy-start(bf16[256,1536]{1,0:T(8,128)(2,1)} %param.16) | copy-start | bytes 2359300
  7.2 145.8 %all-gather.6.cloned.1.call-start = ((), (), s32[]{:S(2)}) async-start(), calls=%async_computation.9 | async-start | bytes 1327104 | tf_op jit(solution)/shard_map/all_gather | solution.py:124
  7.9 150.3 %all-gather.8.cloned.1.call-start = ((), (), s32[]{:S(2)}) async-start(), calls=%async_computation.10 | async-start | bytes 1327104 | tf_op jit(solution)/shard_map/all_gather | solution.py:125
  8.7 191.6 %all-reduce.16.cloned.1.call-start = ((), (), s32[]{:S(2)}) async-start(), calls=%async_computation.11 | async-start | bytes 3145728 | tf_op jit(solution)/shard_map/psum | solution.py:189
  8.8 148.9 %copy-start.67 = (s32[256]{0:T(256)}, s32[256]{0:T(256)S(1)}, u32[]{:S(2)}) copy-start(s32[256]{0:T(256)S(1)} %iota_add_fusion) | copy-start | bytes 3076
  97.6 2.6 copy-start.14
  97.9 7.5 copy-start.52
  98.5 54.5 %copy-start.53 = (f32[256]{0:T(256)}, f32[256]{0:T(256)S(1)}, u32[]{:S(2)}) copy-start(f32[256]{0:T(256)S(1)} %get-tuple-element.60) | copy-start | bytes 3076
  100.2 54.9 %copy-start.11 = (f32[256,128]{0,1:T(8,128)}, f32[256,128]{0,1:T(8,128)S(1)}, u32[]{:S(2)}) copy-start(f32[256,128]{0,1:T(8,128)S(1)} %get-tuple-element.58) | copy-start | bytes 393220
  147.3 5.6 copy-start.61
  147.3 5.6 copy-start.16
  152.8 4.9 copy-start.48
  153.0 4.8 copy-start.64
  155.2 443.9 %copy-start.29 = (bf16[256,3,128]{0,2,1:T(8,128)(2,1)}, bf16[256,3,128]{0,2,1:T(8,128)(2,1)S(1)}, u32[]{:S(2)}) copy-start(bf16[256,3,128]{0,2,1:T(8,128)(2,1)S(1)} %fusion.31) | copy-start | bytes 589828
  157.3 438.5 %copy-start.34 = (bf16[256,128]{0,1:T(8,128)(2,1)}, bf16[256,128]{0,1:T(8,128)(2,1)S(1)}, u32[]{:S(2)}) copy-start(bf16[256,128]{0,1:T(8,128)(2,1)S(1)} %convolution_convert_fusion.9) | copy-start | bytes 196612
  157.7 3.5 copy-start.36
  158.2 3.1 copy-start.38
  161.3 149.9 %all-gather.10.cloned.1.call-start = ((), (), s32[]{:S(2)}) async-start(), calls=%async_computation.12 | async-start | bytes 7962624 | tf_op jit(solution)/shard_map/all_gather | solution.py:126
  161.9 258.4 %all-gather.12.cloned.1.call-start = ((), (), s32[]{:S(2)}) async-start(), calls=%async_computation.13 | async-start | bytes 7962624 | tf_op jit(solution)/shard_map/all_gather | solution.py:127
  162.4 366.9 %all-gather.14.cloned.1.call-start = ((), (), s32[]{:S(2)}) async-start(), calls=%async_computation.14 | async-start | bytes 7962624 | tf_op jit(solution)/shard_map/all_gather | solution.py:128
  163.0 425.9 %all-reduce.18.cloned.1.call-start = ((), (), s32[]{:S(2)}) async-start(), calls=%async_computation.15 | async-start | bytes 3145728 | tf_op jit(solution)/shard_map/psum | solution.py:241
  202.6 108.7 %copy-start.56 = (f32[256]{0:T(256)}, f32[256]{0:T(256)S(1)}, u32[]{:S(2)}) copy-start(f32[256]{0:T(256)S(1)} %get-tuple-element.62) | copy-start | bytes 3076
  202.8 217.5 %copy-start.2 = (bf16[256,1536]{1,0:T(8,128)(2,1)}, bf16[256,1536]{1,0:T(8,128)(2,1)S(1)}, u32[]{:S(2)}) copy-start(bf16[256,1536]{1,0:T(8,128)(2,1)S(1)} %multiply_convert_fusion.3) | copy-start | bytes 2359300
  318.5 210.8 %copy-start.9 = (bf16[256,1536]{1,0:T(8,128)(2,1)S(1)}, bf16[256,1536]{1,0:T(8,128)(2,1)}, u32[]{:S(2)}) copy-start(bf16[256,1536]{1,0:T(8,128)(2,1)} %param.17) | copy-start | bytes 2359300
  538.2 6.0 copy-start.23
  538.2 6.0 copy-start.22
  538.2 6.0 copy-start.79
  547.7 41.2 %copy-start.57 = (f32[256]{0:T(256)S(1)}, f32[256]{0:T(256)}, u32[]{:S(2)}) copy-start(f32[256]{0:T(256)} %copy-done.56) | copy-start | bytes 3076
  547.7 72.1 %reduce-scatter.10.cloned.1.call-start = ((), (), s32[]{:S(2)}) async-start(), calls=%async_computation.16 | async-start | bytes 1179648 | tf_op jit(solution)/shard_map/reduce_scatter | solution.py:278
  589.0 2.6 copy-start.4
  589.0 2.6 copy-start.10
  589.0 2.6 copy-start.58
  589.0 2.6 copy-start.66
  592.8 4.1 copy-start.62
  592.8 4.2 copy-start.65
  595.8 2.9 copy-start.32
  595.8 2.9 copy-start.41
  595.8 2.9 copy-start.49
  595.8 2.9 copy-start.68
  595.9 2.9 copy-start.77
  602.2 38.0 %reduce-scatter.12.cloned.1.call-start = ((), (), s32[]{:S(2)}) async-start(), calls=%async_computation.17 | async-start | bytes 1179648 | tf_op jit(solution)/shard_map/reduce_scatter | solution.py:279
  602.2 6.5 copy-start.25
  602.3 7.4 copy-start.27
  602.3 8.2 copy-start.33
  602.3 8.2 copy-start.47
  602.3 8.2 copy-start.69
  602.3 8.2 copy-start.71
  612.5 74.9 %all-reduce.20.cloned.1.call-start = ((), (), s32[]{:S(2)}) async-start(), calls=%async_computation.25 | async-start | bytes 3145728 | tf_op jit(solution)/shard_map/psum | solution.py:200
  619.8 3.1 copy-start.12
  619.8 3.1 copy-start.13
  625.1 15.2 %copy-start.18 = (bf16[1536,128]{0,1:T(8,128)(2,1)S(1)}, bf16[1536,128]{0,1:T(8,128)(2,1)}, u32[]{:S(2)}) copy-start(bf16[1536,128]{0,1:T(8,128)(2,1)} %copy.49) | copy-start | bytes 1179652
  644.2 2.6 copy-start.31
  644.2 2.6 copy-start.54
  644.2 111.5 %reduce-scatter.20.cloned.1.call-start = ((), (), s32[]{:S(2)}) async-start(), calls=%async_computation.21 | async-start | bytes 1327104 | tf_op jit(solution)/shard_map/reduce_scatter | solution.py:337
  646.7 175.8 %reduce-scatter.14.cloned.1.call-start = ((), (), s32[]{:S(2)}) async-start(), calls=%async_computation.18 | async-start | bytes 1327104 | tf_op jit(solution)/shard_map/reduce_scatter | solution.py:334
  649.6 304.7 %reduce-scatter.22.cloned.1.call-start = ((), (), s32[]{:S(2)}) async-start(), calls=%async_computation.22 | async-start | bytes 7962624 | tf_op jit(solution)/shard_map/reduce_scatter | solution.py:340
  656.4 430.0 %reduce-scatter.24.cloned.1.call-start = ((), (), s32[]{:S(2)}) async-start(), calls=%async_computation.23 | async-start | bytes 7962624 | tf_op jit(solution)/shard_map/reduce_scatter | solution.py:343
  663.0 555.0 %reduce-scatter.26.cloned.1.call-start = ((), (), s32[]{:S(2)}) async-start(), calls=%async_computation.24 | async-start | bytes 7962624 | tf_op jit(solution)/shard_map/reduce_scatter | solution.py:346
  669.5 651.2 %reduce-scatter.18.cloned.1.call-start = ((), (), s32[]{:S(2)}) async-start(), calls=%async_computation.20 | async-start | bytes 1622016 | tf_op jit(solution)/shard_map/reduce_scatter | solution.py:352
  681.2 742.0 %reduce-scatter.16.cloned.1.call-start = ((), (), s32[]{:S(2)}) async-start(), calls=%async_computation.19 | async-start | bytes 1622016 | tf_op jit(solution)/shard_map/reduce_scatter | solution.py:351
  686.3 3.0 copy-start.51
  757.3 2.6 copy-start.1
  757.3 2.6 copy-start.7
  757.3 2.6 copy-start.63
  (33 other events, 46.2 us)
Sparse Core Ops, SparseCore 0:
  10.2 44.5 all-gather.5
  57.0 39.8 all-gather.7
  161.4 38.8 all-reduce.15
  202.3 108.8 all-gather.9
  313.2 106.9 all-gather.11
  422.3 106.9 all-gather.13
  547.9 41.0 all-reduce.17
  602.3 17.4 reduce-scatter.9
  622.7 17.4 reduce-scatter.11
  644.3 43.0 all-reduce.19
  691.4 64.2 reduce-scatter.19
  759.5 62.9 reduce-scatter.13
  826.2 128.0 reduce-scatter.21
  958.3 128.0 reduce-scatter.23
  1089.9 128.0 reduce-scatter.25
  1224.5 96.1 reduce-scatter.17
  1327.2 96.0 reduce-scatter.15
where the time goes:
time: 1440 us; the launch traced here: 1430 us
  waiting for transfers between devices  1090 us (76%)
  blocking collectives  177 us (12%)
  matrix products  88.9 us (6%)
  other arithmetic  37.5 us (3%)
  local copies, waits for them, and re-layouts  25 us (2%)
  between operations  15.4 us (1%)
    reduce_scatter x1, waiting for transfers between devices, on_device(): lax.psum_scatter(grad_gate.astype(jnp.bfloat16), ('dp', 'seq'), scatter_d...  130 us
    reduce_scatter x1, waiting for transfers between devices, on_device(): lax.psum_scatter(grad_up.astype(jnp.bfloat16), ('dp', 'seq'), scatter_dim...  130 us
    reduce_scatter x1, waiting for transfers between devices, on_device(): lax.psum_scatter(grad_down.astype(jnp.bfloat16), ('dp', 'seq'), scatter_d...  129 us
    all_gather x1, waiting for transfers between devices, on_device(): lax.all_gather(w_gate, ('dp', 'seq'), axis=0, tiled=True)  108 us
    reduce_scatter x1, waiting for transfers between devices, on_device(): lax.psum_scatter(grad_key_full, ('dp', 'seq', 'mp'), scatter_dimension=0,...  103 us
    all_gather x1, waiting for transfers between devices, on_device(): lax.all_gather(w_up, ('dp', 'seq'), axis=0, tiled=True)  102 us
    all_gather x1, waiting for transfers between devices, on_device(): lax.all_gather(w_down, ('dp', 'seq'), axis=1, tiled=True)  102 us
    reduce_scatter x1, waiting for transfers between devices, on_device(): lax.psum_scatter(grad_value_full, ('dp', 'seq', 'mp'), scatter_dimension=...  100 us
  transfers between devices with their start and end apart: 17, of which 15 were waited for; matrix products, arithmetic and copies ran while one was open for 8% of the time, Pallas kernels for 0%

commit v1 on v0

v1 whole, which is shorter than its diff:
```python
import math

import jax
import jax.numpy as jnp
from jax import lax
from jax.experimental import pallas as pl
from jax.experimental.pallas import tpu as pltpu
from jax.sharding import PartitionSpec as P

D = 1536
H = 12
KVH = 2
HD = 128

EPSILON = 1e-06
ROPE_BASE = 1000000.0
NEG_BIG = -1e30
SMALL = 16
CHEAP = pl.CostEstimate(flops=0, bytes_accessed=0, transcendentals=0)
BF = jnp.bfloat16
F32 = jnp.float32


def dot(a, b):
    return jnp.dot(a, b, preferred_element_type=F32)


def dot_nt(a, b):
    return lax.dot_general(a, b, (((1,), (1,)), ((), ())), preferred_element_type=F32)


def dot_tn(a, b):
    return lax.dot_general(a, b, (((0,), (0,)), ((), ())), preferred_element_type=F32)


def inverse_rms(values):
    return lax.rsqrt(jnp.mean(values * values, axis=-1, keepdims=True) + EPSILON)


def norm_backward(upstream, values, inv_scale, gain_vec):
    scaled = upstream * gain_vec
    return inv_scale * scaled - values * (inv_scale * inv_scale * inv_scale) * jnp.mean(
        scaled * values, axis=-1, keepdims=True
    )


def rope_tables(positions):
    steps_half = jnp.arange(0, HD, 2).astype(F32)
    frequency = jnp.exp(steps_half * (-math.log(ROPE_BASE) / HD))
    angles = positions.astype(F32)[:, None] * frequency[None, :]
    angles = jnp.concatenate([angles, angles], axis=-1)
    return (jnp.cos(angles), jnp.sin(angles))


def head_backward(
    query_rows, key_rows, value_rows, mask_table, score_scale, log_total, attended, diff_attended
):
    scores = dot_nt(query_rows, key_rows) * score_scale + mask_table
    prob_full = jnp.exp(scores - log_total)
    prob_cast = prob_full.astype(BF)
    value_part = dot_tn(prob_cast, diff_attended)
    diff_probs = dot_nt(diff_attended, value_rows)
    row_delta = jnp.sum(
        diff_attended.astype(F32) * attended.astype(F32), axis=-1, keepdims=True
    )
    diff_scores = (prob_full * (diff_probs - row_delta) * score_scale).astype(BF)
    diff_query = dot(diff_scores, key_rows)
    key_part = dot_tn(diff_scores, query_rows)
    return (diff_query, key_part, value_part)


(
    ATTENDED,
    AWAY,
    BLOCKS,
    BOTH,
    BRANCH,
    BRANCH_C,
    BRANCH_HALF,
    BRANCH_Y,
    C,
    COT,
    COT_QUARTER,
    DIFF_NORMED,
    DIFF_RES,
    DN,
    DN1,
    DONE,
    DRES,
    FEED_AWAY,
    FEED_OWN,
    FFN,
    GRAD,
    GRADS_DONE,
    GRADS_FAR,
    GRADS_NEAR,
    G_SUM,
    G_X,
    G_Z,
    HALF,
    HEADS,
    HEADS_BACK,
    HIDDEN_AWAY,
    HIDDEN_OWN,
    HIDDEN_RES,
    INPUTS,
    INPUT_DIFF,
    INV_ONE,
    INV_QUARTER,
    INV_TWO,
    IN_FLOAT,
    IN_QUARTER,
    KV,
    KV_ACT_C,
    KV_ACT_X,
    KV_DONE_C,
    KV_DONE_HEADS,
    KV_DONE_Y,
    KV_GRADS,
    KV_GRAD_C,
    KV_GRAD_X,
    KV_PAIRS,
    KV_PRE,
    KV_ROT,
    KV_ROWS,
    KV_SEEN,
    KV_SLOTS,
    KV_SUM,
    KV_SUMS,
    LEFT,
    MASK,
    MASK_TABLE,
    N2,
    NORMED_ONE,
    NORMED_TWO,
    OUT,
    OUT_FULL,
    OWN,
    O_ALL,
    PAIR,
    PART,
    PAY,
    POSITIONS,
    PROJ,
    PROJECT,
    PROJECTED,
    QKV_CAST,
    QUERY,
    QUERY_PRE,
    QUERY_ROT,
    RESULTS,
    ROPE,
    SUMS,
    TOTAL,
    VECTOR,
    W_PREP,
    W_X,
    W_Z,
    X,
    X01,
    X10,
    XA,
    XB,
    XF,
    XN,
    Y,
    YA,
    YB,
    Z,
) = range(97)

AFTER = {
    (W_X, (0, 0)): [(O_ALL, X)],
    (O_ALL, (Z, 2)): [(QUERY, (Z, 2))],
    (QUERY, XB): [(O_ALL, (Z, 2))],
    (W_Z, (2, 0)): [(QUERY, (Z, 1))],
    (O_ALL, (Z, 1)): [(QUERY, (Z, 1))],
    PROJECT: [(W_Z, (2, 0)), (O_ALL, (Z, 1))],
    (COT, (Z, 2)): [(QUERY, XB)],
    (O_ALL, X): [(QUERY, XB)],
    KV_ACT_C: [(COT, (Z, 2))],
    (W_Z, (2, 1)): [KV_ACT_X],
    (COT, (Z, 1)): [KV_ACT_X],
    (W_X, (2, 0)): [BRANCH_Y],
    BRANCH_C: [(W_Z, (2, 1)), (COT, (Z, 1))],
    (W_Z, (2, 2)): [ATTENDED],
    (W_Z, (1, 0)): [ATTENDED],
    (W_X, (2, 1)): [(W_X, (2, 0))],
    (COT, YA): [ATTENDED],
    NORMED_TWO: [(W_Z, (2, 2)), (W_X, (0, 0)), (COT, YA)],
    (W_X, (2, 2)): [(W_X, (2, 1))],
    (COT, YB): [BRANCH_Y],
    (N2, (Z, 1)): [(W_Z, (1, 0)), (W_X, (2, 1)), (COT, YB)],
    (W_Z, (3, 0)): [(N2, (Z, 2))],
    (W_X, (1, 0)): [(N2, (Z, 2))],
    (N2, YB): [(W_Z, (3, 0))],
    (W_Z, (3, 1)): [(N2, (Z, 1))],
    (W_X, (3, 0)): [(W_X, (1, 0))],
    (COT, C): [(N2, (Z, 1))],
    (N2, C): [(W_Z, (3, 1)), (W_X, (1, 0))],
    (W_Z, (3, 2)): [(N2, YB)],
    (W_X, (3, 1)): [(W_X, (3, 0))],
    (W_X, (3, 2)): [(W_X, (3, 1))],
    INPUTS: [(QUERY, (Z, 2))],
    POSITIONS: [(QUERY, (Z, 2))],
    MASK: [(QUERY, (Z, 1))],
    W_PREP: [(KV, C)],
    GRADS_FAR: [(DN, OWN)],
    (DN, (Z, 1)): [GRADS_FAR],
    GRADS_NEAR: [(DN, YB)],
    (DN, (Z, 2)): [GRADS_NEAR],
    (G_X, 2): [(G_X, 3)],
    (DRES, Y): [(G_X, 3)],
    (FFN, AWAY): [(DN, (Z, 2))],
    (FFN, OWN): [(DN, (Z, 2))],
    (DRES, C): [(FFN, OWN), (FFN, AWAY)],
    (G_Z, (3, 0)): [(DN, (Z, 2))],
    HEADS_BACK: [(G_Z, (3, 0))],
    (G_X, 1): [(G_X, 2)],
    KV_GRAD_C: [(G_X, 2)],
    (G_Z, (3, 1)): [(DRES, C)],
    KV_GRAD_X: [(G_Z, (3, 1)), (FFN, C)],
    (FFN, C): [(DRES, C)],
    (G_Z, (3, 2)): [KV_GRAD_C],
    (PROJ, XF): [(G_X, 1)],
    (DN1, C): [(PROJ, GRAD)],
    (G_Z, (2, 0)): [(PROJ, GRAD)],
    (PROJ, (Z, 1)): [(G_Z, (3, 2)), (G_Z, (2, 0)), (FFN, YB), (DN1, Y)],
    (G_Z, (2, 1)): [(PROJ, XF)],
    (PROJ, (Z, 2)): [(G_Z, (2, 1)), (FFN, (Z, 1))],
    (VECTOR, C): [(PROJ, XF)],
    (OUT, X): [(PROJ, XF)],
    (G_Z, (2, 2)): [(PROJ, (Z, 1))],
    (G_Z, (1, 0)): [(G_Z, (3, 2))],
    KV_DONE_Y: [(G_Z, (2, 2)), (OUT, X), (VECTOR, Y), (G_Z, (1, 0))],
    (G_X, 0): [(OUT, X)],
    (OUT, GRAD): [KV_GRAD_C],
}


def after(x, *tokens):
    return lax.optimization_barrier((x, *tokens))[0] if tokens else x


def index(x, i, axis=0):
    return lax.dynamic_index_in_dim(x, i, axis, keepdims=False)


def split_columns(weights, n, pieces):
    rows, columns = weights[0].shape
    part, count = columns // n, len(weights)
    flat = [(j, cut) for j in range(n) for cut in pieces[j]]

    def kernel(*refs):
        ins, outs, held = refs[:count], refs[count:-1], refs[-1]
        d = lax.axis_index("dp")
        for i in range(count):
            for t in range(n):
                held[t] = ins[i][:, t * part : (t + 1) * part]
            for out, (j, (low, high)) in zip(outs, flat):
                out[i] = held[d ^ j, low:high]

    outs = pl.pallas_call(
        kernel,
        cost_estimate=CHEAP,
        out_shape=[
            jax.ShapeDtypeStruct((count, high - low, part), BF) for _, (low, high) in flat
        ],
        scratch_shapes=[pltpu.VMEM((n, rows, part), BF)],
        compiler_params=pltpu.CompilerParams(vmem_limit_bytes=48 << 20),
    )(*weights)
    return dict(zip(flat, outs))


def join_columns(blocks, n, rows):
    keys = list(blocks)
    count, _, part = blocks[keys[0]].shape

    def kernel(*refs):
        ins, outs, held = refs[: len(keys)], refs[len(keys) : -1], refs[-1]
        d = lax.axis_index("dp")
        for i in range(count):
            for ref, (j, (low, high)) in zip(ins, keys):
                held[d ^ j, low:high] = ref[i]
            for t in range(n):
                outs[i][:, t * part : (t + 1) * part] = held[t].astype(F32)

    return pl.pallas_call(
        kernel,
        cost_estimate=CHEAP,
        out_shape=[jax.ShapeDtypeStruct((rows, n * part), F32)] * count,
        scratch_shapes=[pltpu.VMEM((n, rows, part), BF)],
        compiler_params=pltpu.CompilerParams(vmem_limit_bytes=48 << 20),
    )(*blocks.values())


def key_value_slots(w_key, w_value, vectors):
    rows = w_key.shape[0]

    def kernel(key_ref, value_ref, *refs):
        ins, outs = refs[:-2], refs[-2:]
        head = lax.axis_index("mp") // (lax.axis_size("mp") // KVH)
        for i, ref in enumerate((key_ref, value_ref)):
            parts = [ref[:, k * HD : (k + 1) * HD] for k in range(KVH)]
            outs[0][i, :rows] = jnp.where(head == 0, parts[0], parts[1])
            outs[1][i, :rows] = jnp.where(head == 0, parts[1], parts[0])
            for out in outs:
                out[i, rows:] = jnp.zeros((SMALL, HD), BF)
                for j, vector in enumerate(ins):
                    out[i, rows + j : rows + j + 1, : vector.shape[1]] = vector[...]

    return pl.pallas_call(
        kernel, cost_estimate=CHEAP, out_shape=[jax.ShapeDtypeStruct((2, rows + SMALL, HD), BF)] * 2
    )(w_key, w_value, *[v[None] for v in vectors])


def join_rows(own, other, n_dp, n_seq, rows, lens):
    parts = [(a, o, 0) for a, o in own] + [(a, o, 1) for a, o in other]
    width = parts[0][0].shape[2]
    total = sum(len(o) for _, o, _ in parts)
    slots = n_dp * n_seq
    small = parts[0][0].shape[1] - rows

    def kernel(*refs):
        ins, out, vectors = refs[: len(parts)], refs[len(parts)], refs[len(parts) + 1 : -2]
        held, sem = refs[-2:]
        d = lax.axis_index("dp")
        s = lax.axis_index("seq")
        copies = []
        for ref, (_, offsets, side) in zip(ins, parts):
            for i, offset in enumerate(offsets):
                slot = (d ^ offset) * n_seq + (s ^ side)
                start = pl.multiple_of(slot * rows, rows)
                pairs = [(ref.at[i, pl.ds(0, rows)], out.at[pl.ds(start, rows)])]
                if lens:
                    pairs.append((ref.at[i, pl.ds(rows, small)], held.at[slot]))
                for pair in pairs:
                    copies.append(pltpu.make_async_copy(*pair, sem.at[len(copies)]))
        for copy in copies:
            copy.start()
        for copy in copies:
            copy.wait()
        for i, size in enumerate(lens):
            for t in range(slots):
                for k in range(small // SMALL):
                    at = (t * (small // SMALL) + k) * size
                    x = held[t, k * SMALL : (k + 1) * SMALL, :size].astype(F32)
                    vectors[i][:, at : at + size] = x[i : i + 1]

    return pl.pallas_call(
        kernel,
        cost_estimate=CHEAP,
        out_shape=[jax.ShapeDtypeStruct((slots * rows, width), BF)]
        + [jax.ShapeDtypeStruct((1, slots * (small // SMALL) * size), F32) for size in lens],
        in_specs=[pl.BlockSpec(memory_space=pl.ANY)] * len(parts),
        scratch_shapes=[
            pltpu.VMEM((slots, max(small, SMALL), width), BF),
            pltpu.SemaphoreType.DMA((2 * total,)),
        ],
    )(*[a for a, _, _ in parts])


def turn(x, cosine, sine_signed):
    return x * cosine + pltpu.roll(x, HD // 2, 1) * sine_signed


def project(x, vectors, w_q, w_kv, cosine, sine_signed):
    tokens = x.shape[0]
    wide = w_q.shape[1]

    def kernel(x_ref, bq, bk, bv, gain, _, w_ref, wkv_ref, cos_ref, sin_ref, *outs):
        normed, inv_ref, q_ref, kv_ref = outs
        m = lax.axis_index("mp")
        value = x_ref[...].astype(F32)
        inv = inverse_rms(value)
        inv_ref[...] = inv
        norm = (value * inv * gain[...]).astype(BF)
        normed[...] = norm
        proj = dot(norm, w_ref[...])
        cosine, sine = cos_ref[...], sin_ref[...]
        bias = bq[:, pl.ds(pl.multiple_of(m * wide, HD), wide)]
        for j in range(wide // HD):
            cut = slice(j * HD, (j + 1) * HD)
            q_ref[:, cut] = turn(proj[:, cut] + bias[:, cut], cosine, sine).astype(BF)
        head = pl.ds(pl.multiple_of((m // 2) * HD, HD), HD)
        last = dot(norm, wkv_ref[...]) + jnp.where(m % 2 == 0, bk[:, head], bv[:, head])
        kv_ref[...] = jnp.where(m % 2 == 0, turn(last, cosine, sine), last).astype(BF)

    return pl.pallas_call(
        kernel,
        cost_estimate=CHEAP,
        out_shape=[
            jax.ShapeDtypeStruct(x.shape, BF),
            jax.ShapeDtypeStruct((tokens, 1), F32),
            jax.ShapeDtypeStruct((tokens, wide), BF),
            jax.ShapeDtypeStruct((tokens, HD), BF),
        ],
    )(x, *vectors, w_q, w_kv, cosine, sine_signed)


def attend(query, seen, other, mask, out_t, quarter):
    tokens, wide = query.shape
    heads = wide // HD
    width = out_t.shape[0]

    def kernel(q_ref, seen_ref, other_ref, mask_ref, o_ref, att, log_ref, near, away, held):
        c = lax.axis_index("mp") % 2
        keys = jnp.where(c == 0, seen_ref[...], other_ref[...])
        vals = jnp.where(c == 0, other_ref[...], seen_ref[...])
        for j in range(heads):
            cut = slice(j * HD, (j + 1) * HD)
            scores = dot_nt(q_ref[:, cut], keys) * HD ** (-0.5) + mask_ref[...]
            top = jnp.max(scores, axis=-1, keepdims=True)
            total = jnp.sum(jnp.exp(scores - top), axis=-1, keepdims=True)
            log_total = top + jnp.log(total)
            log_ref[:, j : j + 1] = log_total
            att[:, cut] = dot(jnp.exp(scores - log_total).astype(BF), vals).astype(BF)
        held[...] = dot_nt(att[...], o_ref[...])
        for i in range(2):
            rows = pl.ds(pl.multiple_of((2 * i + c) * quarter, quarter), quarter)
            near[i] = held[rows]
            rows = pl.ds(pl.multiple_of((2 * i + 1 - c) * quarter, quarter), quarter)
            away[i] = held[rows].astype(BF)

    return pl.pallas_call(
        kernel,
        cost_estimate=CHEAP,
        out_shape=[
            jax.ShapeDtypeStruct((tokens, wide), BF),
            jax.ShapeDtypeStruct((tokens, heads), F32),
            jax.ShapeDtypeStruct((2, quarter, width), F32),
            jax.ShapeDtypeStruct((2, quarter, width), BF),
        ],
        scratch_shapes=[pltpu.VMEM((tokens, width), F32)],
    )(query, seen, other, mask, out_t)


def feed_rows(n2, cot, gate_ref, up_ref, down_ref, outs, waits):
    act, diff_gate_ref, diff_up_ref, dn = outs
    size = min(256, n2.shape[0])
    for i in range(n2.shape[0] // size):
        rows = slice(i * size, (i + 1) * size)
        if i == 0:
            waits[0]()
        gate_proj = dot(n2[rows], gate_ref[...])
        if i == 0:
            waits[1]()
        up_proj = dot(n2[rows], up_ref[...])
        if i == 0:
            waits[2]()
        diff_hidden = dot(cot[rows], down_ref[...])
        sigmoid_gate = 1.0 / (1.0 + jnp.exp(-gate_proj))
        silu_gate = gate_proj * sigmoid_gate
        act[rows] = (silu_gate * up_proj).astype(BF)
        diff_gate = (
            diff_hidden * up_proj * sigmoid_gate * (1.0 + gate_proj * (1.0 - sigmoid_gate))
        ).astype(BF)
        diff_up = (diff_hidden * silu_gate).astype(BF)
        diff_gate_ref[rows] = diff_gate
        diff_up_ref[rows] = diff_up
        dn[rows] = (dot_nt(diff_gate, gate_ref[...]) + dot_nt(diff_up, up_ref[...])).astype(dn.dtype)


def feed_shapes(n2, part, kind):
    shape = jax.ShapeDtypeStruct((n2.shape[0], part), BF)
    return [shape] * 3 + [jax.ShapeDtypeStruct(n2.shape, kind)]


def feed_limit(n2, part):
    part = -(-part // HD) * HD
    return min(60 << 20, (10 << 20) + 8 * n2.size + 12 * sum(n2.shape) * part)


def feed_first(n2, cot, blocks, rows, n_dp, n_seq):
    keys = list(blocks)
    part = blocks[keys[0]].shape[2]
    full = n_dp * n_seq * rows

    def kernel(n2_ref, cot_ref, *refs):
        ins, copies_out, outs = refs[: len(keys)], refs[len(keys) :][:3], refs[len(keys) + 3 :][:4]
        weights, sem = refs[-4:-1], refs[-1]
        d = lax.axis_index("dp")
        s = lax.axis_index("seq")
        back = [
            pltpu.make_async_copy(weights[w], copies_out[w], sem.at[w]) for w in range(3)
        ]

        def place(which):
            for ref, (side, j, (low, high)) in zip(ins, keys):
                size = high - low
                start = ((d ^ j) * n_seq + (s ^ side)) * rows + low
                weights[which][pl.ds(pl.multiple_of(start, size), size)] = ref[which]
            back[which].start()

        waits = [lambda w=w: place(w) for w in range(3)]
        feed_rows(n2_ref, cot_ref, *weights, outs, waits)
        for copy in back:
            copy.wait()

    whole = pl.BlockSpec(memory_space=pltpu.VMEM)
    return pl.pallas_call(
        kernel,
        cost_estimate=CHEAP,
        out_shape=[pltpu.HBM((full, part), BF)] * 3 + feed_shapes(n2, part, BF),
        out_specs=[pl.BlockSpec(memory_space=pltpu.HBM)] * 3 + [whole] * 4,
        scratch_shapes=[pltpu.VMEM((full, part), BF)] * 3
        + [pltpu.SemaphoreType.DMA((3,))],
        compiler_params=pltpu.CompilerParams(vmem_limit_bytes=feed_limit(n2, part)),
    )(n2, cot, *blocks.values())


def feed_second(n2, cot, gate, up, down):
    part = gate.shape[1]

    def kernel(n2_ref, cot_ref, gate_ref, up_ref, down_ref, *outs):
        feed_rows(n2_ref, cot_ref, gate_ref, up_ref, down_ref, outs, [lambda: None] * 3)

    return pl.pallas_call(
        kernel,
        cost_estimate=CHEAP,
        out_shape=feed_shapes(n2, part, F32),
        compiler_params=pltpu.CompilerParams(vmem_limit_bytes=feed_limit(n2, part)),
    )(n2, cot, gate, up, down)


def weight_grads(rows, which, diffs, n_dp, n_seq, far):
    count, half, n = len(diffs), n_dp // 2, 2 * len(rows)
    wide = rows[0][0].shape[1] // n_dp
    size, width = wide // n_seq, diffs[0][0].shape[1]
    operands = [a for pair in rows for a in pair] + [a for pair in diffs for a in pair]

    def kernel(*refs):
        ins, outs, held = refs[: len(operands)], refs[len(operands) : -1], refs[-1]
        d = lax.axis_index("dp")
        s = lax.axis_index("seq")
        upper = (d // half) ^ int(far)

        def columns(ref, t):
            if wide % HD == 0:
                start = upper * (half * wide) + t * wide
                return ref[:, pl.ds(pl.multiple_of(start, HD), wide)]
            low = ref[:, t * wide : (t + 1) * wide]
            high = ref[:, (half + t) * wide : (half + t + 1) * wide]
            return jnp.where(upper == 0, low, high)

        for i in range(count):
            for t in range(half):
                k = 2 * which[i]
                x = dot_tn(columns(ins[k], t), ins[n + 2 * i][...])
                x = x + dot_tn(columns(ins[k + 1], t), ins[n + 2 * i + 1][...])
                x = x.astype(BF)
                held[t, 0] = x[:size]
                held[t, 1] = x[size:]
            for j in range(half):
                outs[j][i] = held[(d % half) ^ j, s]
                outs[half + j][i] = held[(d % half) ^ j, 1 - s]

    total = sum(a.size for a in operands)
    need = (6 << 20) + (2 if total < 8 << 20 else 4) * total
    outs = pl.pallas_call(
        kernel,
        cost_estimate=CHEAP,
        out_shape=[jax.ShapeDtypeStruct((count, size, width), BF)] * n_dp,
        scratch_shapes=[pltpu.VMEM((half, n_seq, size, width), BF)],
        compiler_params=pltpu.CompilerParams(vmem_limit_bytes=min(60 << 20, need)),
    )(*operands)
    return outs[:half], outs[half:]


def token_grads(rows, diff, n_dp, n_seq, groups):
    wide = rows.shape[1] // n_dp
    size, width = wide // n_seq, diff.shape[1]

    def kernel(rows_ref, diff_ref, *refs):
        outs, held = refs[:-1], refs[-1]
        d = lax.axis_index("dp")
        s = lax.axis_index("seq")
        for t in range(n_dp):
            x = dot_tn(rows_ref[:, t * wide : (t + 1) * wide], diff_ref[...]).astype(BF)
            held[t, 0] = x[:size]
            held[t, 1] = x[size:]
        for side in range(2):
            for out, group in zip(outs[side * len(groups) :], groups):
                for i, offset in enumerate(group):
                    out[i] = held[d ^ offset, s ^ side]

    outs = pl.pallas_call(
        kernel,
        cost_estimate=CHEAP,
        out_shape=[jax.ShapeDtypeStruct((len(g), size, width), BF) for g in groups] * 2,
        scratch_shapes=[pltpu.VMEM((n_dp, n_seq, size, width), BF)],
    )(rows, diff)
    return outs[: len(groups)], outs[len(groups) :]


def solution(mesh):
    n_dp = mesh.shape["dp"]
    n_seq = mesh.shape["seq"]
    n_mp = mesh.shape["mp"]
    bits = [1 << i for i in reversed(range(n_dp.bit_length() - 1))]

    def on_device(
        inputs,
        cotangent,
        segments,
        positions,
        w_query,
        w_key,
        w_value,
        bias_query,
        bias_key,
        bias_value,
        w_out,
        gain_attn,
        gain_ffn,
        w_gate,
        w_up,
        w_down,
    ):
        d = lax.axis_index("dp")
        s = lax.axis_index("seq")
        m = lax.axis_index("mp")
        y, c = m // 2, m % 2
        tokens = inputs.shape[0]
        quarter = tokens // n_mp
        score_scale = HD ** (-0.5)
        wide = w_query.shape[1]
        heads_local = wide // HD
        rows_kv = w_key.shape[0]

        values, makers = {}, {}

        def get(name):
            if name not in values:
                values[name] = makers[name]()
            return values[name]

        def task(name):
            def add(maker):
                makers[name] = maker

            return add

        def tied(name, x):
            tokens = [jax.tree.leaves(get(o))[0] for o in AFTER.get(name, ()) if o in makers]
            return after(x, *tokens)

        links = {X: ("seq", [(0, 1), (1, 0)]), X01: ("seq", [(0, 1)]), X10: ("seq", [(1, 0)])}
        for k in range(1, n_dp):
            links[(Z, k)] = ("dp", [(j, j ^ k) for j in range(n_dp)])
        for k, name in ((1, C), (2, Y)):
            links[name] = ("mp", [(j, j ^ k) for j in range(n_mp)])

        def move(name, link, maker):
            makers[name] = lambda: lax.ppermute(tied(name, maker()), *links[link])

        def of(name):
            return lambda: get(name)

        def gather(name, maker, size, lens, split):
            makers[(name, PAY)] = lambda: maker()[None]
            pay, offsets = (name, PAY), [0]
            for k in bits[:-1]:
                recv = (name, (Z, k))
                move(recv, (Z, k), of(pay))
                makers[(recv, PAY)] = lambda a=pay, b=recv: jnp.concatenate([get(a), get(b)])
                pay, offsets = (recv, PAY), offsets + [o ^ k for o in offsets]
            k = bits[-1]
            recv = (name, (Z, k))
            move(recv, (Z, k), of(pay))
            there = [o ^ k for o in offsets]
            if split:
                move((name, XA), X, of(pay))
                move((name, XB), X, of(recv))
                own = lambda: [(get(pay), offsets), (get(recv), there)]
                other = lambda: [(get((name, XA)), offsets), (get((name, XB)), there)]
            else:
                makers[(name, BOTH)] = lambda: jnp.concatenate([get(pay), get(recv)])
                move((name, X), X, of((name, BOTH)))
                own = lambda: [(get((name, BOTH)), offsets + there)]
                other = lambda: [(get((name, X)), offsets + there)]
            makers[name] = lambda: join_rows(own(), other(), n_dp, n_seq, size, lens)

        w_rows = w_gate.shape[0]
        whole_cut = [(0, w_rows)]
        third = w_rows // 3
        third_cuts = [(i * third, (i + 1) * third) for i in range(3)]
        pieces = [whole_cut if k < n_dp // 2 else third_cuts for k in range(n_dp)]
        tails = [(k, cut, (k, i)) for k in range(n_dp) for i, cut in enumerate(pieces[k])]
        makers[W_PREP] = lambda: split_columns(
            [tied(W_PREP, w_gate), w_up, w_down.T], n_dp, pieces
        )
        for k, cut, tail in tails:
            if k:
                move((W_Z, tail), (Z, k), lambda k=k, cut=cut: get(W_PREP)[k, cut])
            else:
                makers[(W_Z, tail)] = lambda cut=cut: get(W_PREP)[0, cut]
            move((W_X, tail), X, of((W_Z, tail)))

        def rows_gather(name, maker):
            makers[(name, PAY)] = maker
            pay = (name, PAY)
            for k in bits[:-1]:
                recv = (name, (Z, k))
                move(recv, (Z, k), of(pay))
                makers[(recv, PAY)] = lambda a=pay, b=recv: jnp.concatenate([get(a), get(b)])
                pay = (recv, PAY)
            recv = (name, (Z, bits[-1]))
            move(recv, (Z, bits[-1]), of(pay))
            move((name, YA), Y, of(pay))
            move((name, YB), Y, of(recv))
            makers[(name, OWN)] = lambda: jnp.concatenate(
                [get(pay), get(recv), get((name, YA)), get((name, YB))]
            )
            move((name, C), C, of((name, OWN)))

        def rows_sum(name):
            move((name, C), C, of((name, AWAY)))
            last = (name, (Z, bits[-1]))

            def part(i):
                size = get((name, OWN)).shape[0] // 4
                cut = slice(i * size, (i + 1) * size)
                return get((name, OWN))[cut] + get((name, C))[cut].astype(F32)

            for i in range(4):
                makers[(name, PART, i)] = lambda i=i: part(i)
            move((name, YB), Y, lambda: get((name, PART, 3)).astype(BF))
            move((name, YA), Y, lambda: get((name, PART, 2)).astype(BF))
            move(
                last,
                (Z, bits[-1]),
                lambda: (get((name, PART, 1)) + get((name, YB)).astype(F32)).astype(BF),
            )
            makers[(name, LEFT, 0)] = (
                lambda: get((name, PART, 0)) + get((name, YA)).astype(F32) + get(last).astype(F32)
            )
            left = (name, LEFT, 0)
            for i, k in enumerate(reversed(bits[:-1])):
                recv = (name, (Z, k))

                def far(left=left):
                    return get(left)[get(left).shape[0] // 2 :].astype(BF)

                def near(left=left, recv=recv):
                    return get(left)[: get(left).shape[0] // 2] + get(recv).astype(F32)

                move(recv, (Z, k), far)
                left = (name, LEFT, i + 1)
                makers[left] = near
            makers[name] = of(left)

        def weight_grad_ways(name, far):
            own, away = get(HIDDEN_OWN), get(HIDDEN_AWAY)
            n2 = [tied(name, get((N2, OWN))), get((N2, C))]
            cot = [get((COT, OWN)), get((COT, C))]
            return weight_grads(
                [n2, cot],
                [0, 0, 1],
                [[own[1], away[1]], [own[2], away[2]], [own[0], away[0]]],
                n_dp,
                n_seq,
                far,
            )

        makers[GRADS_FAR] = lambda: weight_grad_ways(GRADS_FAR, True)
        makers[GRADS_NEAR] = lambda: weight_grad_ways(GRADS_NEAR, False)

        def grad_piece(k, side):
            return get(GRADS_NEAR if k < n_dp // 2 else GRADS_FAR)[side][k % (n_dp // 2)]

        for k in range(n_dp):
            move((G_X, k), X, lambda k=k: grad_piece(k, 1))
        for k, cut, tail in tails:

            def summed(k=k, cut=cut, tail=tail):
                low, high = cut
                own = tied((G_SUM, tail), grad_piece(k, 0)[:, low:high]).astype(F32)
                return (own + get((G_X, k))[:, low:high].astype(F32)).astype(BF)

            makers[(G_SUM, tail)] = summed
            if k:
                move((G_Z, tail), (Z, k), of((G_SUM, tail)))
            else:
                makers[(G_Z, tail)] = of((G_SUM, tail))
        makers[GRADS_DONE] = lambda: join_columns(
            {(k, cut): get((G_Z, tail)) for k, cut, tail in tails}, n_dp, w_rows
        )

        def gather_grad(name, rows, diff, split):
            near = [0]
            for k in bits[:-1]:
                near = near + [o ^ k for o in near]
            far = [o ^ bits[-1] for o in near]
            n_near = len(near)
            groups = [near, far] if split else [near + far]
            makers[(name, GRAD)] = lambda: token_grads(rows(), diff(), n_dp, n_seq, groups)
            if split:
                move((name, XF), X, lambda: get((name, GRAD))[1][1])
                move((name, XN), X, lambda: get((name, GRAD))[1][0])
                own = lambda i: get((name, GRAD))[0][i]
            else:
                move((name, X), X, lambda: get((name, GRAD))[1][0])
                makers[(name, XN)] = lambda: get((name, X))[:n_near]
                makers[(name, XF)] = lambda: get((name, X))[n_near:]
                own = lambda i: get((name, GRAD))[0][0][i * n_near : (i + 1) * n_near]

            def both(i, recv):
                return own(i).astype(F32) + get(recv).astype(F32)

            last = (name, (Z, bits[-1]))
            move(last, (Z, bits[-1]), lambda: both(1, (name, XF)).astype(BF))
            makers[(name, LEFT, 0)] = lambda: both(0, (name, XN)) + get(last).astype(F32)
            left = (name, LEFT, 0)
            for i, k in enumerate(reversed(bits[:-1])):
                recv = (name, (Z, k))

                def far_half(left=left):
                    return get(left)[get(left).shape[0] // 2 :].astype(BF)

                def near_half(left=left, recv=recv):
                    return get(left)[: get(left).shape[0] // 2] + get(recv).astype(F32)

                move(recv, (Z, k), far_half)
                left = (name, LEFT, i + 1)
                makers[left] = near_half
            makers[(name, DONE)] = lambda: get(left)[0]

        def mp_gather(name, maker):
            move((name, Y), Y, maker)

            def pair():
                a, b = maker(), get((name, Y))
                return jnp.where(y == 0, jnp.stack([a, b]), jnp.stack([b, a]))

            makers[(name, PAIR)] = pair
            move((name, C), C, of((name, PAIR)))

            def whole():
                a, b = get((name, PAIR)), get((name, C))
                both = jnp.where(c == 0, jnp.stack([a, b], axis=1), jnp.stack([b, a], axis=1))
                return both.reshape(-1, both.shape[-1])

            makers[name] = whole

        def mp_sum(name, maker):
            def blocks():
                x = maker()
                return x.reshape(2, 2, -1, x.shape[-1])

            makers[(name, BLOCKS)] = blocks
            move((name, C), C, lambda: index(get((name, BLOCKS)), 1 - c, 1).astype(BF))
            makers[(name, HALF)] = lambda: index(get((name, BLOCKS)), c, 1) + get(
                (name, C)
            ).astype(F32)
            move((name, Y), Y, lambda: index(get((name, HALF)), 1 - y).astype(BF))
            makers[name] = lambda: index(get((name, HALF)), y) + get((name, Y)).astype(F32)

        gather(QUERY, lambda: w_query, w_query.shape[0], [], True)
        gather(O_ALL, lambda: tied(O_ALL, w_out).T, w_query.shape[0], [], False)
        makers[OUT_FULL] = lambda: get(O_ALL)[0]

        vectors = (bias_query, bias_key, bias_value, gain_attn, gain_ffn)

        makers[KV_SLOTS] = lambda: key_value_slots(w_key, w_value, vectors)
        move((KV, Y), Y, lambda: get(KV_SLOTS)[1])

        @task(KV_PAIRS)
        def kv_pairs():
            return jnp.stack([get(KV_SLOTS)[0], get((KV, Y))])

        move((KV, C), C, lambda: index(get(KV_PAIRS), 1 - c, 1))

        @task(KV_ROWS)
        def kv_rows():
            own, got = index(get(KV_PAIRS), c, 1), get((KV, C))
            by_core = jnp.where(
                c == 0, jnp.stack([own, got], axis=1), jnp.stack([got, own], axis=1)
            )
            whole = jnp.where(y == 0, by_core, by_core[::-1])
            parts = [whole[:, :, :rows_kv], whole[:, :, rows_kv:]]
            return jnp.concatenate([x.reshape(-1, HD) for x in parts])

        gather(
            KV, of(KV_ROWS), n_mp * rows_kv, [v.shape[0] for v in vectors], False
        )

        @task(IN_FLOAT)
        def in_float():
            return tied(INPUTS, inputs).astype(F32)

        @task(ROPE)
        def rope():
            cosine, sine_table = rope_tables(tied(POSITIONS, positions))
            first = jnp.arange(HD) < HD // 2
            return cosine, jnp.where(first, -sine_table, sine_table)

        @task(PROJECTED)
        def projected():
            weights, *small = get(KV)
            x = tied(PROJECT, inputs)
            return project(x, small, get(QUERY)[0], weights, *get(ROPE))

        makers[NORMED_ONE] = lambda: get(PROJECTED)[0]
        makers[INV_ONE] = lambda: get(PROJECTED)[1]
        makers[QUERY_ROT] = lambda: get(PROJECTED)[2]
        makers[KV_ROT] = lambda: tied(KV_ROT, get(PROJECTED)[3])

        move(KV_ACT_X, X01, of(KV_ROT))

        @task(KV_SEEN)
        def kv_seen():
            return jnp.concatenate([get(KV_ACT_X), get(KV_ROT)], axis=0)

        move(KV_ACT_C, C, of(KV_SEEN))

        @task(MASK_TABLE)
        def mask_table():
            where = tied(MASK, segments)
            seg_before = where[:tokens]
            seg_own = lax.dynamic_slice_in_dim(where, s * tokens, tokens, 0)
            order = jnp.arange(tokens, dtype=jnp.int32)
            before = (seg_own[:, None] == seg_before[None, :]) & (s > 0)
            own = (seg_own[:, None] == seg_own[None, :]) & (order[None, :] <= order[:, None])
            return jnp.where(jnp.concatenate([before, own], axis=1), 0.0, NEG_BIG)

        @task(HEADS)
        def heads():
            return attend(
                get(QUERY_ROT),
                get(KV_SEEN),
                tied(HEADS, get(KV_ACT_C)),
                get(MASK_TABLE),
                get(OUT_FULL),
                quarter,
            )

        makers[ATTENDED] = lambda: get(HEADS)[0]

        move(BRANCH_C, C, lambda: get(HEADS)[3])
        makers[BRANCH_HALF] = lambda: get(HEADS)[2] + get(BRANCH_C).astype(F32)
        move(BRANCH_Y, Y, lambda: index(get(BRANCH_HALF), 1 - y).astype(BF))
        makers[BRANCH] = lambda: index(get(BRANCH_HALF), y) + get(BRANCH_Y).astype(F32)

        @task(IN_QUARTER)
        def in_quarter():
            return lax.dynamic_slice_in_dim(get(IN_FLOAT), m * quarter, quarter, 0)

        @task(HIDDEN_RES)
        def hidden_res():
            return get(IN_QUARTER) + get(BRANCH)

        @task(INV_TWO)
        def inv_two():
            return inverse_rms(get(HIDDEN_RES))

        @task(NORMED_TWO)
        def normed_two():
            return tied(
                NORMED_TWO, (get(HIDDEN_RES) * get(INV_TWO) * get(KV)[5]).astype(BF)
            )

        @task(COT_QUARTER)
        def cot_quarter():
            return lax.dynamic_slice_in_dim(cotangent, m * quarter, quarter, 0)

        rows_gather(N2, of(NORMED_TWO))
        rows_gather(COT, of(COT_QUARTER))

        @task(FEED_AWAY)
        def feed_away():
            blocks = {(0, k, cut): get((W_Z, tail)) for k, cut, tail in tails}
            blocks.update({(1, k, cut): get((W_X, tail)) for k, cut, tail in tails})
            return feed_first(
                tied(FEED_AWAY, get((N2, C))), get((COT, C)), blocks, w_rows, n_dp, n_seq
            )

        @task(FEED_OWN)
        def feed_own():
            weights = get(FEED_AWAY)[:3]
            return feed_second(tied(FEED_OWN, get((N2, OWN))), get((COT, OWN)), *weights)

        makers[HIDDEN_AWAY] = lambda: get(FEED_AWAY)[3:6]
        makers[HIDDEN_OWN] = lambda: get(FEED_OWN)[:3]
        makers[(DN, AWAY)] = lambda: get(FEED_AWAY)[6]
        makers[(DN, OWN)] = lambda: get(FEED_OWN)[3]
        makers[(FFN, OWN)] = lambda: dot_nt(
            tied((FFN, OWN), get(HIDDEN_OWN)[0]), get(FEED_AWAY)[2]
        )
        makers[(FFN, AWAY)] = lambda: dot_nt(
            tied((FFN, AWAY), get(HIDDEN_AWAY)[0]), get(FEED_AWAY)[2]
        ).astype(BF)
        rows_sum(DN)

        rows_sum(FFN)

        @task(DIFF_RES)
        def diff_res():
            return get(COT_QUARTER).astype(F32) + norm_backward(
                get(DN), get(HIDDEN_RES), get(INV_TWO), get(KV)[5]
            )

        mp_gather(DRES, lambda: get(DIFF_RES).astype(BF))

        @task(HEADS_BACK)
        def heads_back():
            seen, other = get(KV_SEEN), get(KV_ACT_C)
            keys, vals = jnp.where(c == 0, seen, other), jnp.where(c == 0, other, seen)
            queries, logs = get(QUERY_ROT), get(HEADS)[1]
            diff_attended = tied(HEADS_BACK, dot(get(DRES), get(OUT_FULL)).astype(BF))
            return [
                head_backward(
                    queries[:, j * HD : (j + 1) * HD],
                    keys,
                    vals,
                    get(MASK_TABLE),
                    score_scale,
                    logs[:, j : j + 1],
                    get(ATTENDED)[:, j * HD : (j + 1) * HD],
                    diff_attended[:, j * HD : (j + 1) * HD],
                )
                for j in range(heads_local)
            ]

        @task(KV_SUMS)
        def kv_sums():
            return [sum(head[i] for head in get(HEADS_BACK)) for i in (1, 2)]

        move(KV_GRAD_C, C, lambda: jnp.where(c == 0, *reversed(get(KV_SUMS))))

        @task(KV_SUM)
        def kv_sum():
            return jnp.where(c == 0, *get(KV_SUMS)) + get(KV_GRAD_C)

        move(KV_GRAD_X, X10, lambda: get(KV_SUM)[:tokens])

        def turn_back(x):
            cosine, sine_signed = get(ROPE)
            return x * cosine - jnp.roll(x, HD // 2, axis=1) * sine_signed

        @task(KV_PRE)
        def kv_pre():
            mine = get(KV_SUM)[tokens:] + get(KV_GRAD_X)
            return jnp.where(c == 0, turn_back(mine), mine)

        @task(QUERY_PRE)
        def query_pre():
            return jnp.concatenate([turn_back(head[0]) for head in get(HEADS_BACK)], axis=1)

        @task(QKV_CAST)
        def qkv_cast():
            return jnp.concatenate([get(QUERY_PRE), get(KV_PRE)], axis=1).astype(BF)

        gather_grad(PROJ, of(NORMED_ONE), of(QKV_CAST), True)
        gather_grad(OUT, lambda: tied((OUT, GRAD), get(DRES)), of(ATTENDED), False)

        @task(DIFF_NORMED)
        def diff_normed():
            cast = get(QKV_CAST)
            return dot_nt(cast[:, :wide], get(QUERY)[0]) + dot_nt(cast[:, wide:], get(KV)[0])

        mp_sum(DN1, of(DIFF_NORMED))

        @task((KV, DONE))
        def kv_done():
            return get((PROJ, DONE))[:, wide:].reshape(2, 2, rows_kv, HD).astype(BF)

        move(KV_DONE_Y, Y, lambda: index(get((KV, DONE)), 1 - y))

        @task(KV_DONE_HEADS)
        def kv_done_heads():
            mine, got = index(get((KV, DONE)), y), get(KV_DONE_Y)
            return jnp.where(y == 0, jnp.stack([mine, got]), jnp.stack([got, mine]))

        move(KV_DONE_C, C, lambda: index(get(KV_DONE_HEADS), 1 - c, 1))

        @task(KV_GRADS)
        def kv_grads():
            mine, got = index(get(KV_DONE_HEADS), c, 1), get(KV_DONE_C)
            return [
                jnp.where(c == 0, a, b)
                .transpose(1, 0, 2)
                .reshape(rows_kv, KVH * HD)
                .astype(F32)
                for a, b in ((mine, got), (got, mine))
            ]

        @task(INV_QUARTER)
        def inv_quarter():
            return lax.dynamic_slice_in_dim(get(INV_ONE), m * quarter, quarter, 0)

        @task(INPUT_DIFF)
        def input_diff():
            return get(DIFF_RES) + norm_backward(
                get(DN1), get(IN_QUARTER), get(INV_QUARTER), get(KV)[4]
            )

        mp_gather(
            RESULTS,
            lambda: jnp.concatenate(
                [get(HIDDEN_RES) + get(FFN), get(INPUT_DIFF)], axis=1
            ).astype(BF),
        )

        @task(VECTOR)
        def vector():
            grad_gain_ffn = jnp.sum(get(DN) * get(HIDDEN_RES) * get(INV_TWO), axis=0)
            grad_gain_attn = jnp.sum(get(DN1) * get(IN_QUARTER) * get(INV_QUARTER), axis=0)
            grad_bq = jnp.sum(get(QUERY_PRE), axis=0)
            grad_bkv = jnp.sum(get(KV_PRE), axis=0)
            zeros_kv = jnp.zeros((2, KVH, HD), F32)
            return jnp.concatenate(
                [
                    lax.dynamic_update_slice_in_dim(
                        jnp.zeros((H * HD,), F32), grad_bq, m * wide, 0
                    ),
                    grad_gain_attn,
                    grad_gain_ffn,
                    lax.dynamic_update_slice(zeros_kv, grad_bkv[None, None], (c, y, 0)).reshape(-1),
                ]
            ).reshape(-1, HD)

        total = VECTOR
        for link in [C, Y, X] + [(Z, k) for k in bits]:
            move((VECTOR, link), link, of(total))
            makers[(TOTAL, link)] = lambda a=total, b=(VECTOR, link): get(a) + get(b)
            total = (TOTAL, link)

        makers[SUMS] = lambda: get(total).reshape(-1)
        device = (d * n_seq + s) * n_mp + m

        def own(start, length):
            width = length // (n_dp * n_seq * n_mp)
            return lax.dynamic_slice_in_dim(
                get(SUMS)[start : start + length], device * width, width, 0
            )

        return (
            get(RESULTS)[:, :D].astype(F32),
            get(RESULTS)[:, D:].astype(F32),
            get((PROJ, DONE))[:, :wide],
            get(KV_GRADS)[0],
            get(KV_GRADS)[1],
            own(0, H * HD),
            get(SUMS)[3 * D : 3 * D + KVH * HD],
            own(3 * D + KVH * HD, KVH * HD),
            get((OUT, DONE)).T,
            own(D, D),
            own(2 * D, D),
            get(GRADS_DONE)[0],
            get(GRADS_DONE)[1],
            get(GRADS_DONE)[2].T,
        )

    in_specs = (
        P(("dp", "seq"), None),
        P(("dp", "seq"), None),
        P("dp"),
        P(("dp", "seq")),
        P(("dp", "seq"), "mp"),
        P(("dp", "seq", "mp"), None),
        P(("dp", "seq", "mp"), None),
        P(("dp", "seq", "mp")),
        P(("dp", "seq", "mp")),
        P(("dp", "seq", "mp")),
        P("mp", ("dp", "seq")),
        P(("dp", "seq", "mp")),
        P(("dp", "seq", "mp")),
        P(("dp", "seq"), "mp"),
        P(("dp", "seq"), "mp"),
        P("mp", ("dp", "seq")),
    )
    out_specs = (
        P(("dp", "seq"), None),
        P(("dp", "seq"), None),
        P(("dp", "seq"), "mp"),
        P(("dp", "seq", "mp"), None),
        P(("dp", "seq", "mp"), None),
        P(("dp", "seq", "mp")),
        P(),
        P(("dp", "seq", "mp")),
        P("mp", ("dp", "seq")),
        P(("dp", "seq", "mp")),
        P(("dp", "seq", "mp")),
        P(("dp", "seq"), "mp"),
        P(("dp", "seq"), "mp"),
        P("mp", ("dp", "seq")),
    )
    return jax.shard_map(
        on_device, mesh=mesh, in_specs=in_specs, out_specs=out_specs, check_vma=False
    )
```

time: 1440 us -> 418 us (0.29)
  waiting for transfers between devices: 1090 us -> 181 us
  blocking collectives: 177 us -> 0 us
  starting transfers between devices: 1.11 us -> 103 us
  matrix products: 88.9 us -> 9.81 us
  Pallas kernels: 0 us -> 53.8 us
    reduce_scatter x9 -> x0, waiting for transfers between devices: 694 us -> none  [the longest x1 130 us: on_device(): lax.psum_scatter(grad_gate.astype(jnp.bfloat16), ('dp', 'seq'), scatter_d...]
    all_gather x5 -> x0, waiting for transfers between devices: 312 us -> none  [the longest x1 108 us: on_device(): lax.all_gather(w_gate, ('dp', 'seq'), axis=0, tiled=True)]
    ppermute x0 -> x84, waiting for transfers between devices: none -> 181 us  [move(): makers[name] = lambda: lax.ppermute(tied(name, maker()), *links[link])]
    ppermute x0 -> x84, starting transfers between devices: none -> 103 us  [move(): makers[name] = lambda: lax.ppermute(tied(name, maker()), *links[link])]
    all_gather x4 -> x0, blocking collectives: 99.1 us -> none  [the longest x1 47.1 us: on_device(): lax.all_gather(w_key, ('dp', 'seq', 'mp'), axis=0, tiled=True)]
    dot_general x39 -> x20, matrix products: 88.9 us -> 9.81 us  [the longest x10 7.01 us: dot_nt(): lax.dot_general(a, b, (((1,), (1,)), ((), ())), preferred_element_type=F32)]
    unnamed x2 -> x0, blocking collectives: 78.1 us -> none
    psum x3 -> x0, waiting for transfers between devices: 75.9 us -> none  [the longest x1 38.4 us: on_device(): lax.psum(jnp.dot(diff_gate, gate_full.T, preferred_element_type=jnp.float...]
  transfers between devices with their start and end apart: 17 -> 84, of which waited for: 15 -> 41; matrix products, arithmetic and copies ran while one was open for 8% -> 14% of each run, Pallas kernels for 0% -> 9%
where the time goes in v1:
time: 418 us; the launch traced here: 413 us
  waiting for transfers between devices  181 us (43%)
  starting transfers between devices  103 us (25%)
  Pallas kernels  53.8 us (13%)
  other arithmetic  41.5 us (10%)
  local copies, waits for them, and re-layouts  21.4 us (5%)
  matrix products  9.81 us (2%)
    ppermute x84, waiting for transfers between devices, move(): makers[name] = lambda: lax.ppermute(tied(name, maker()), *links[link])  181 us
    ppermute x84, starting transfers between devices, move(): makers[name] = lambda: lax.ppermute(tied(name, maker()), *links[link])  103 us
    unnamed x179, local copies, waits for them, and re-layouts  13.6 us
    pallas_call x2, Pallas kernels, weight_grads(): pl.pallas_call(kernel, cost_estimate=CHEAP, out_shape=[jax.ShapeDtypeStru...  9.5 us
    pallas_call x1, Pallas kernels, feed_first(): pl.pallas_call(kernel, cost_estimate=CHEAP, out_shape=[pltpu.HBM((full, p...  9.42 us
  transfers between devices with their start and end apart: 84, of which 41 were waited for; matrix products, arithmetic and copies ran while one was open for 14% of the time, Pallas kernels for 9%

profile of v1, /device:TPU:0, one launch (start us, length us, event | category | flops | bytes accessed | tf_op | source)
XLA Modules:
  0.0 412.8 jit_solution(13853980891687009424)
XLA Ops:
  2.2 3.0 collective-permute-start.1
  5.2 2.6 collective-permute-start
  14.8 2.0 shard_map.264
  26.4 3.0 collective-permute-start.9
  29.4 2.4 collective-permute-done.5
  33.6 3.0 collective-permute-start.6
  41.0 2.0 shard_map.265
  43.0 9.1 %collective-permute-done.4.refs_2_ = bf16[3,64,560]{2,1,0:T(8,128)(2,1)S(1)} collective-permute-done((bf16[3,64,560]{2,1,0:T(8,128)(2,1)}, bf16[3,64,560]{2,1,0:T(8,128)(2,1)S(1)}, u32[]{:S(2)}, u32[]{:S(2)}) %collective-permute-start.4) | collective-permute-done | bytes 215072 | tf_op jit(solution)/shard_map/ppermute | solution.py:655
  52.1 2.5 shard_map.266.w_ref
  54.7 3.7 shard_map.267
  58.4 2.8 collective-permute-start.12
  63.8 5.3 %collective-permute-done.13 = bf16[64,1536]{1,0:T(8,128)(2,1)S(1)} collective-permute-done((bf16[64,1536]{1,0:T(8,128)(2,1)S(1)}, bf16[64,1536]{1,0:T(8,128)(2,1)S(1)}, u32[]{:S(2)}, u32[]{:S(2)}) %collective-permute-start.13) | collective-permute-done | bytes 196640 | tf_op jit(solution)/shard_map/ppermute | solution.py:655
  70.0 2.3 collective-permute-start.16
  73.3 2.5 collective-permute-done.15.refs_1_
  75.8 2.5 shard_map.268.o_ref
  78.4 4.8 %shard_map.269 = (bf16[256,384]{1,0:T(8,128)(2,1)}, f32[256,3]{1,0:T(8,128)}, f32[2,64,1536]{2,1,0:T(8,128)}, bf16[2,64,1536]{2,1,0:T(8,128)(2,1)}) custom-call(bf16[256,384]{1,0:T(8,128)(2,1)} %get-tuple-element.148.q_ref, bf16[512,128]{1,0:T(8,128)(2,1)} %copy-done.56, bf16[512,128]{1,0:T(8,128)(2,1)} %collective-permute-done.14.other_ref, ...), custom_call_target="tpu_custom_call" | custom-call | tf_op jit(solution)/shard_map/pallas_call | solution.py:425
  83.3 2.3 collective-permute-done.17
  92.1 11.1 %collective-permute-done.19 = bf16[64,1536]{1,0:T(8,128)(2,1)S(1)} collective-permute-done((bf16[64,1536]{1,0:T(8,128)(2,1)S(1)}, bf16[64,1536]{1,0:T(8,128)(2,1)S(1)}, u32[]{:S(2)}, u32[]{:S(2)}) %collective-permute-start.19) | collective-permute-done | bytes 196640 | tf_op jit(solution)/shard_map/ppermute | solution.py:655
  109.3 2.1 collective-permute-done.25.refs_10_
  111.8 6.0 %collective-permute-done.23 = bf16[64,1536]{1,0:T(8,128)(2,1)S(1)} collective-permute-done((bf16[64,1536]{1,0:T(8,128)(2,1)S(1)}, bf16[64,1536]{1,0:T(8,128)(2,1)S(1)}, u32[]{:S(2)}, u32[]{:S(2)}) %collective-permute-start.23) | collective-permute-done | bytes 196640 | tf_op jit(solution)/shard_map/ppermute | solution.py:655
  119.4 3.3 collective-permute-start.30
  123.0 11.8 %collective-permute-done.30.refs_5_ = bf16[3,64,560]{2,1,0:T(8,128)(2,1)S(1)} collective-permute-done((bf16[3,64,560]{2,1,0:T(8,128)(2,1)S(1)}, bf16[3,64,560]{2,1,0:T(8,128)(2,1)S(1)}, u32[]{:S(2)}, u32[]{:S(2)}) %collective-permute-start.30) | collective-permute-done | bytes 215072 | tf_op jit(solution)/shard_map/ppermute | solution.py:655
  137.5 5.9 %collective-permute-done.31 = bf16[128,1536]{1,0:T(8,128)(2,1)S(1)} collective-permute-done((bf16[128,1536]{1,0:T(8,128)(2,1)S(1)}, bf16[128,1536]{1,0:T(8,128)(2,1)S(1)}, u32[]{:S(2)}, u32[]{:S(2)}) %collective-permute-start.31) | collective-permute-done | bytes 393248 | tf_op jit(solution)/shard_map/ppermute | solution.py:655
  143.7 8.3 %collective-permute-done.38.refs_13_ = bf16[3,64,560]{2,1,0:T(8,128)(2,1)S(1)} collective-permute-done((bf16[3,64,560]{2,1,0:T(8,128)(2,1)S(1)}, bf16[3,64,560]{2,1,0:T(8,128)(2,1)S(1)}, u32[]{:S(2)}, u32[]{:S(2)}) %collective-permute-start.38) | collective-permute-done | bytes 215072 | tf_op jit(solution)/shard_map/ppermute | solution.py:655
  152.2 2.2 collective-permute-start.36
  156.2 4.6 %collective-permute-done.39.refs_14_ = bf16[3,64,560]{2,1,0:T(8,128)(2,1)S(1)} collective-permute-done((bf16[3,64,560]{2,1,0:T(8,128)(2,1)S(1)}, bf16[3,64,560]{2,1,0:T(8,128)(2,1)S(1)}, u32[]{:S(2)}, u32[]{:S(2)}) %collective-permute-start.39) | collective-permute-done | bytes 215072 | tf_op jit(solution)/shard_map/ppermute | solution.py:655
  163.2 2.9 collective-permute-done.37.refs_12_
  166.1 4.0 collective-permute-done.40.refs_15_
  170.1 9.4 %shard_map.270 = (bf16[1536,560]{1,0:T(8,128)(2,1)}, bf16[1536,560]{1,0:T(8,128)(2,1)}, bf16[1536,560]{1,0:T(8,128)(2,1)}, bf16[512,560]{1,0:T(8,128)(2,1)S(1)},...) custom-call(bf16[512,1536]{1,0:T(8,128)(2,1)S(1)} %collective-permute-done.34.n2_ref.refs_1_, ...), custom_call_target="tpu_custom_call" | custom-call | tf_op jit(solution)/shard_map/pallas_call | solution.py:501
  187.6 6.8 %shard_map.271 = (bf16[512,560]{1,0:T(8,128)(2,1)S(1)}, bf16[512,560]{1,0:T(8,128)(2,1)S(1)}, bf16[512,560]{1,0:T(8,128)(2,1)S(1)}, f32[512,1536]{1,0:T(8,128)S(1)}) custom-call(bf16[512,1536]{1,0:T(8,128)(2,1)S(1)} %constant_dynamic-update-slice_fusion.4.n2_ref.refs_0_, bf16[512,1536]{1,0:T(8,128)(2,1)S(1)} %constant_dynamic-update-slice_fusion.9.cot_ref.refs_2_, ...), custom_call_target="tpu_custom_call" | custom-call | tf_op jit(solution)/shard_map/pallas_call | solution.py:518
  198.9 4.1 %shard_map.272 = (bf16[3,192,560]{2,1,0:T(8,128)(2,1)S(1)}, bf16[3,192,560]{2,1,0:T(8,128)(2,1)S(1)}, bf16[3,192,560]{2,1,0:T(8,128)(2,1)S(1)}, bf16[3,192,560]{2,1,0:T(8,128)(2,1)S(1)}) custom-call(bf16[512,1536]{1,0:T(8,128)(2,1)S(1)} %constant_dynamic-update-slice_fusion.4.n2_ref.refs_0_, bf16[512,1536]{1,0:T(8,128)(2,1)S(1)} %copy-done.3, ...), custom_call_target="tpu_custom_call" | custom-call | tf_op jit(solution)/shard_map/pallas_call | solution.py:560
  204.2 3.7 collective-permute-done.43
  209.0 4.0 collective-permute-start.44
  213.6 8.2 %collective-permute-done.46 = bf16[3,192,560]{2,1,0:T(8,128)(2,1)S(1)} collective-permute-done((bf16[3,192,560]{2,1,0:T(8,128)(2,1)S(1)}, bf16[3,192,560]{2,1,0:T(8,128)(2,1)S(1)}, u32[]{:S(2)}, u32[]{:S(2)}) %collective-permute-start.46) | collective-permute-done | bytes 645152 | tf_op jit(solution)/shard_map/ppermute | solution.py:655
  222.2 5.4 %shard_map.273 = (bf16[3,192,560]{2,1,0:T(8,128)(2,1)S(1)}, bf16[3,192,560]{2,1,0:T(8,128)(2,1)S(1)}, bf16[3,192,560]{2,1,0:T(8,128)(2,1)S(1)}, bf16[3,192,560]{2,1,0:T(8,128)(2,1)}) custom-call(bf16[512,1536]{1,0:T(8,128)(2,1)S(1)} %constant_dynamic-update-slice_fusion.4.n2_ref.refs_0_, bf16[512,1536]{1,0:T(8,128)(2,1)S(1)} %copy-done.3, ...), custom_call_target="tpu_custom_call" | custom-call | tf_op jit(solution)/shard_map/pallas_call | solution.py:560
  229.2 4.3 %collective-permute-start.45 = (bf16[64,1536]{1,0:T(8,128)(2,1)S(1)}, bf16[64,1536]{1,0:T(8,128)(2,1)S(1)}, u32[]{:S(2)}, u32[]{:S(2)}) collective-permute-start(bf16[64,1536]{1,0:T(8,128)(2,1)S(1)} %slice.488), channel_id=1, source_target_pairs={{0,16},{8,24},{16,0},{24,8},{1,17},{9,25},{17,1},{25,9},{2,18},{10... | collective-permute-start | bytes 589832 | tf_op jit(solution)/shard_map/ppermute | solution.py:655
  234.3 7.5 %collective-permute-done.45 = bf16[64,1536]{1,0:T(8,128)(2,1)S(1)} collective-permute-done((bf16[64,1536]{1,0:T(8,128)(2,1)S(1)}, bf16[64,1536]{1,0:T(8,128)(2,1)S(1)}, u32[]{:S(2)}, u32[]{:S(2)}) %collective-permute-start.45) | collective-permute-done | bytes 196640 | tf_op jit(solution)/shard_map/ppermute | solution.py:655
  243.8 3.1 fusion.86
  250.5 2.5 collective-permute-start.54
  253.8 6.7 %collective-permute-done.54.refs_5_ = bf16[3,64,560]{2,1,0:T(8,128)(2,1)S(1)} collective-permute-done((bf16[3,64,560]{2,1,0:T(8,128)(2,1)S(1)}, bf16[3,64,560]{2,1,0:T(8,128)(2,1)S(1)}, u32[]{:S(2)}, u32[]{:S(2)}) %collective-permute-start.54) | collective-permute-done | bytes 215072 | tf_op jit(solution)/shard_map/ppermute | solution.py:655
  263.7 2.5 collective-permute-start.57
  267.2 6.3 %collective-permute-done.57.refs_6_ = bf16[3,64,560]{2,1,0:T(8,128)(2,1)S(1)} collective-permute-done((bf16[3,64,560]{2,1,0:T(8,128)(2,1)S(1)}, bf16[3,64,560]{2,1,0:T(8,128)(2,1)S(1)}, u32[]{:S(2)}, u32[]{:S(2)}) %collective-permute-start.57) | collective-permute-done | bytes 215072 | tf_op jit(solution)/shard_map/ppermute | solution.py:655
  276.0 2.5 collective-permute-start.66
  283.7 3.0 shard_map.274
  286.9 2.7 fusion.21
  294.1 2.3 add_convert_fusion.1
  296.4 2.8 shard_map.275
  299.2 5.5 %collective-permute-start.75 = (bf16[3,192,560]{2,1,0:T(8,128)(2,1)}, bf16[3,192,560]{2,1,0:T(8,128)(2,1)S(1)}, u32[]{:S(2)}, u32[]{:S(2)}) collective-permute-start(bf16[3,192,560]{2,1,0:T(8,128)(2,1)} %add_convert_fusion.1), channel_id=1, source_target_pairs={{0,8},{8,0},{16,24},{24,16},{1,9},{9,1},{17,25},{25,17},{2,10},{10... | collective-permute-start | bytes 1935368 | tf_op jit(solution)/shard_map/ppermute | solution.py:655
  307.2 5.1 %collective-permute-start.67 = (bf16[3,64,560]{2,1,0:T(8,128)(2,1)}, bf16[3,64,560]{2,1,0:T(8,128)(2,1)S(1)}, u32[]{:S(2)}, u32[]{:S(2)}) collective-permute-start(bf16[3,64,560]{2,1,0:T(8,128)(2,1)} %get-tuple-element.230), channel_id=1, source_target_pairs={{0,16},{8,24},{16,0},{24,8},{1,17},{9,25},{17,1},{25,9},{2,18},{10... | collective-permute-start | bytes 645128 | tf_op jit(solution)/shard_map/ppermute | solution.py:655
  319.2 3.8 collective-permute-done.78
  322.9 2.8 collective-permute-start.79
  329.1 5.8 %collective-permute-done.79 = f32[40,128]{1,0:T(8,128)S(1)} collective-permute-done((f32[40,128]{1,0:T(8,128)S(1)}, f32[40,128]{1,0:T(8,128)S(1)}, u32[]{:S(2)}, u32[]{:S(2)}) %collective-permute-start.79) | collective-permute-done | bytes 20512 | tf_op jit(solution)/shard_map/ppermute | solution.py:655
  335.0 3.4 collective-permute-start.69
  341.6 2.2 collective-permute-done.80
  348.2 8.8 %collective-permute-done.53 = bf16[64,1536]{1,0:T(8,128)(2,1)S(1)} collective-permute-done((bf16[64,1536]{1,0:T(8,128)(2,1)S(1)}, bf16[64,1536]{1,0:T(8,128)(2,1)S(1)}, u32[]{:S(2)}, u32[]{:S(2)}) %collective-permute-start.53) | collective-permute-done | bytes 196640 | tf_op jit(solution)/shard_map/ppermute | solution.py:655
  358.0 8.9 %collective-permute-done.68 = bf16[2,192,512]{2,1,0:T(8,128)(2,1)S(1)} collective-permute-done((bf16[2,192,512]{2,1,0:T(8,128)(2,1)S(1)}, bf16[2,192,512]{2,1,0:T(8,128)(2,1)S(1)}, u32[]{:S(2)}, u32[]{:S(2)}) %collective-permute-start.68) | collective-permute-done | bytes 393248 | tf_op jit(solution)/shard_map/ppermute | solution.py:655
  367.3 3.0 collective-permute-start.71
  370.2 12.3 %collective-permute-done.70 = bf16[1,192,512]{2,1,0:T(8,128)(2,1)S(1)} collective-permute-done((bf16[1,192,512]{2,1,0:T(8,128)(2,1)S(1)}, bf16[1,192,512]{2,1,0:T(8,128)(2,1)S(1)}, u32[]{:S(2)}, u32[]{:S(2)}) %collective-permute-start.70) | collective-permute-done | bytes 196640 | tf_op jit(solution)/shard_map/ppermute | solution.py:655
  382.7 5.1 %collective-permute-done.71.refs_4_ = bf16[3,64,560]{2,1,0:T(8,128)(2,1)S(1)} collective-permute-done((bf16[3,64,560]{2,1,0:T(8,128)(2,1)S(1)}, bf16[3,64,560]{2,1,0:T(8,128)(2,1)S(1)}, u32[]{:S(2)}, u32[]{:S(2)}) %collective-permute-start.71) | collective-permute-done | bytes 215072 | tf_op jit(solution)/shard_map/ppermute | solution.py:655
  389.5 2.0 collective-permute-done.76
  392.5 4.3 %collective-permute-done.81 = bf16[2,192,384]{2,1,0:T(8,128)(2,1)S(1)} collective-permute-done((bf16[2,192,384]{2,1,0:T(8,128)(2,1)S(1)}, bf16[2,192,384]{2,1,0:T(8,128)(2,1)S(1)}, u32[]{:S(2)}, u32[]{:S(2)}) %collective-permute-start.81) | collective-permute-done | bytes 294944 | tf_op jit(solution)/shard_map/ppermute | solution.py:655
  399.3 6.7 %collective-permute-done.82 = bf16[1,192,384]{2,1,0:T(8,128)(2,1)S(1)} collective-permute-done((bf16[1,192,384]{2,1,0:T(8,128)(2,1)S(1)}, bf16[1,192,384]{2,1,0:T(8,128)(2,1)S(1)}, u32[]{:S(2)}, u32[]{:S(2)}) %collective-permute-start.82) | collective-permute-done | bytes 147488 | tf_op jit(solution)/shard_map/ppermute | solution.py:655
  406.9 3.3 shard_map.276
  410.6 2.1 slice_convert_fusion
  (425 shorter events, 119.8 us)
Async XLA Ops:
  5.2 14.3 %collective-permute-start = (bf16[1,192,384]{2,1,0:T(8,128)(2,1)}, bf16[1,192,384]{2,1,0:T(8,128)(2,1)}, u32[]{:S(2)}, u32[]{:S(2)}) collective-permute-start(bf16[1,192,384]{2,1,0:T(8,128)(2,1)} %bitcast.158), channel_id=1, source_target_pairs={{0,16},{8,24},{16,0},{24,8},{1,17},{9,25},{17,1},{25,9},{2,18},{10... | collective-permute-start | bytes 442376 | tf_op jit(solution)/shard_map/ppermute | solution.py:655
  20.5 13.0 %collective-permute-start.3 = (bf16[2,192,384]{2,1,0:T(8,128)(2,1)S(1)}, bf16[2,192,384]{2,1,0:T(8,128)(2,1)S(1)}, u32[]{:S(2)}, u32[]{:S(2)}) collective-permute-start(bf16[2,192,384]{2,1,0:T(8,128)(2,1)S(1)} %pad_maximum_fusion.3.refs_0_), channel_id=1, source_target_pairs={{0,8},{8,0},{16,24},{24,16},{1,9},{9,1},{17,25},{25,17},{2,10},{10... | collective-permute-start | bytes 884744 | tf_op jit(solution)/shard_map/ppermute | solution.py:655
  22.2 29.9 %collective-permute-start.10 = (bf16[2,192,384]{2,1,0:T(8,128)(2,1)S(1)}, bf16[2,192,384]{2,1,0:T(8,128)(2,1)}, u32[]{:S(2)}, u32[]{:S(2)}) collective-permute-start(bf16[2,192,384]{2,1,0:T(8,128)(2,1)S(1)} %pad_maximum_fusion.3.refs_0_), channel_id=1, source_target_pairs={{0,4},{4,0},{1,5},{5,1},{2,6},{6,2},{3,7},{7,3},{8,12},{12,8},{9,1... | collective-permute-start | bytes 884744 | tf_op jit(solution)/shard_map/ppermute | solution.py:655
  23.7 8.0 %collective-permute-start.5 = (bf16[1,192,384]{2,1,0:T(8,128)(2,1)S(1)}, bf16[1,192,384]{2,1,0:T(8,128)(2,1)S(1)}, u32[]{:S(2)}, u32[]{:S(2)}) collective-permute-start(bf16[1,192,384]{2,1,0:T(8,128)(2,1)S(1)} %bitcast.152), channel_id=1, source_target_pairs={{0,16},{8,24},{16,0},{24,8},{1,17},{9,25},{17,1},{25,9},{2,18},{10... | collective-permute-start | bytes 442376 | tf_op jit(solution)/shard_map/ppermute | solution.py:655
  26.4 14.6 %collective-permute-start.9 = (bf16[4,256,128]{2,1,0:T(8,128)(2,1)S(1)}, bf16[4,256,128]{2,1,0:T(8,128)(2,1)}, u32[]{:S(2)}, u32[]{:S(2)}) collective-permute-start(bf16[4,256,128]{2,1,0:T(8,128)(2,1)S(1)} %pad_maximum_fusion.5.refs_0_), channel_id=1, source_target_pairs={{0,4},{4,0},{1,5},{5,1},{2,6},{6,2},{3,7},{7,3},{8,12},{12,8},{9,1... | collective-permute-start | bytes 786440 | tf_op jit(solution)/shard_map/ppermute | solution.py:655
  33.6 18.5 %collective-permute-start.6 = (bf16[2,192,384]{2,1,0:T(8,128)(2,1)}, bf16[2,192,384]{2,1,0:T(8,128)(2,1)}, u32[]{:S(2)}, u32[]{:S(2)}) collective-permute-start(bf16[2,192,384]{2,1,0:T(8,128)(2,1)} %pad_maximum_fusion.4), channel_id=1, source_target_pairs={{0,8},{8,0},{16,24},{24,16},{1,9},{9,1},{17,25},{25,17},{2,10},{10... | collective-permute-start | bytes 884744 | tf_op jit(solution)/shard_map/ppermute | solution.py:655
  36.5 15.6 %collective-permute-start.11 = (bf16[2,192,384]{2,1,0:T(8,128)(2,1)S(1)}, bf16[2,192,384]{2,1,0:T(8,128)(2,1)}, u32[]{:S(2)}, u32[]{:S(2)}) collective-permute-start(bf16[2,192,384]{2,1,0:T(8,128)(2,1)S(1)} %collective-permute-done.3.refs_1_), channel_id=1, source_target_pairs={{0,4},{4,0},{1,5},{5,1},{2,6},{6,2},{3,7},{7,3},{8,12},{12,8},{9,1... | collective-permute-start | bytes 884744 | tf_op jit(solution)/shard_map/ppermute | solution.py:655
  39.3 12.8 %collective-permute-start.4 = (bf16[3,64,560]{2,1,0:T(8,128)(2,1)}, bf16[3,64,560]{2,1,0:T(8,128)(2,1)S(1)}, u32[]{:S(2)}, u32[]{:S(2)}) collective-permute-start(bf16[3,64,560]{2,1,0:T(8,128)(2,1)} %get-tuple-element.136), channel_id=1, source_target_pairs={{0,16},{8,24},{16,0},{24,8},{1,17},{9,25},{17,1},{25,9},{2,18},{10... | collective-permute-start | bytes 645128 | tf_op jit(solution)/shard_map/ppermute | solution.py:655
  62.4 13.4 %collective-permute-start.15 = (bf16[4,192,384]{2,1,0:T(8,128)(2,1)S(1)}, bf16[4,192,384]{2,1,0:T(8,128)(2,1)}, u32[]{:S(2)}, u32[]{:S(2)}) collective-permute-start(bf16[4,192,384]{2,1,0:T(8,128)(2,1)S(1)} %pad_maximum_fusion.refs_0_), channel_id=1, source_target_pairs={{0,4},{4,0},{1,5},{5,1},{2,6},{6,2},{3,7},{7,3},{8,12},{12,8},{9,1... | collective-permute-start | bytes 1769480 | tf_op jit(solution)/shard_map/ppermute | solution.py:655
  69.9 15.7 %collective-permute-start.17 = (bf16[128,1536]{1,0:T(8,128)(2,1)}, bf16[128,1536]{1,0:T(8,128)(2,1)}, u32[]{:S(2)}, u32[]{:S(2)}) collective-permute-start(bf16[128,1536]{1,0:T(8,128)(2,1)} %pad_maximum_fusion.1), channel_id=1, source_target_pairs={{0,8},{8,0},{16,24},{24,16},{1,9},{9,1},{17,25},{25,17},{2,10},{10... | collective-permute-start | bytes 1179656 | tf_op jit(solution)/shard_map/ppermute | solution.py:655
  70.0 13.3 %collective-permute-start.16 = (bf16[3,64,560]{2,1,0:T(8,128)(2,1)S(1)}, bf16[3,64,560]{2,1,0:T(8,128)(2,1)S(1)}, u32[]{:S(2)}, u32[]{:S(2)}) collective-permute-start(bf16[3,64,560]{2,1,0:T(8,128)(2,1)S(1)} %copy-done.35), channel_id=1, source_target_pairs={{0,16},{8,24},{16,0},{24,8},{1,17},{9,25},{17,1},{25,9},{2,18},{10... | collective-permute-start | bytes 645128 | tf_op jit(solution)/shard_map/ppermute | solution.py:655
  86.4 20.4 %collective-permute-start.20 = (bf16[3,64,560]{2,1,0:T(8,128)(2,1)S(1)}, bf16[3,64,560]{2,1,0:T(8,128)(2,1)S(1)}, u32[]{:S(2)}, u32[]{:S(2)}) collective-permute-start(bf16[3,64,560]{2,1,0:T(8,128)(2,1)S(1)} %copy-done.33), channel_id=1, source_target_pairs={{0,16},{8,24},{16,0},{24,8},{1,17},{9,25},{17,1},{25,9},{2,18},{10... | collective-permute-start | bytes 645128 | tf_op jit(solution)/shard_map/ppermute | solution.py:655
  87.6 19.9 %collective-permute-start.21 = (bf16[3,192,560]{2,1,0:T(8,128)(2,1)S(1)}, bf16[3,192,560]{2,1,0:T(8,128)(2,1)S(1)}, u32[]{:S(2)}, u32[]{:S(2)}) collective-permute-start(bf16[3,192,560]{2,1,0:T(8,128)(2,1)S(1)} %get-tuple-element.164.refs_0_), channel_id=1, source_target_pairs={{0,4},{4,0},{1,5},{5,1},{2,6},{6,2},{3,7},{7,3},{8,12},{12,8},{9,1... | collective-permute-start | bytes 1935368 | tf_op jit(solution)/shard_map/ppermute | solution.py:655
  87.6 19.9 %collective-permute-start.22 = (bf16[128,1536]{1,0:T(8,128)(2,1)}, bf16[128,1536]{1,0:T(8,128)(2,1)S(1)}, u32[]{:S(2)}, u32[]{:S(2)}) collective-permute-start(bf16[128,1536]{1,0:T(8,128)(2,1)} %pad_maximum_fusion.1), channel_id=1, source_target_pairs={{0,2},{1,3},{2,0},{3,1},{4,6},{5,7},{6,4},{7,5},{8,10},{9,11},{10,... | collective-permute-start | bytes 1179656 | tf_op jit(solution)/shard_map/ppermute | solution.py:655
  88.2 29.6 %collective-permute-start.24 = (bf16[3,192,560]{2,1,0:T(8,128)(2,1)}, bf16[3,192,560]{2,1,0:T(8,128)(2,1)S(1)}, u32[]{:S(2)}, u32[]{:S(2)}) collective-permute-start(bf16[3,192,560]{2,1,0:T(8,128)(2,1)} %get-tuple-element.168), channel_id=1, source_target_pairs={{0,8},{8,0},{16,24},{24,16},{1,9},{9,1},{17,25},{25,17},{2,10},{10... | collective-permute-start | bytes 1935368 | tf_op jit(solution)/shard_map/ppermute | solution.py:655
  89.6 13.6 %collective-permute-start.19 = (bf16[64,1536]{1,0:T(8,128)(2,1)S(1)}, bf16[64,1536]{1,0:T(8,128)(2,1)S(1)}, u32[]{:S(2)}, u32[]{:S(2)}) collective-permute-start(bf16[64,1536]{1,0:T(8,128)(2,1)S(1)} %fusion.41), channel_id=1, source_target_pairs={{0,2},{1,3},{2,0},{3,1},{4,6},{5,7},{6,4},{7,5},{8,10},{9,11},{10,... | collective-permute-start | bytes 589832 | tf_op jit(solution)/shard_map/ppermute | solution.py:655
  103.2 8.2 %collective-permute-start.25 = (bf16[3,64,560]{2,1,0:T(8,128)(2,1)S(1)}, bf16[3,64,560]{2,1,0:T(8,128)(2,1)S(1)}, u32[]{:S(2)}, u32[]{:S(2)}) collective-permute-start(bf16[3,64,560]{2,1,0:T(8,128)(2,1)S(1)} %collective-permute-done.4.refs_2_), channel_id=1, source_target_pairs={{0,4},{4,0},{1,5},{5,1},{2,6},{6,2},{3,7},{7,3},{8,12},{12,8},{9,1... | collective-permute-start | bytes 645128 | tf_op jit(solution)/shard_map/ppermute | solution.py:655
  106.7 11.1 %collective-permute-start.27 = (bf16[128,1536]{1,0:T(8,128)(2,1)}, bf16[128,1536]{1,0:T(8,128)(2,1)S(1)}, u32[]{:S(2)}, u32[]{:S(2)}) collective-permute-start(bf16[128,1536]{1,0:T(8,128)(2,1)} %collective-permute-done.17), channel_id=1, source_target_pairs={{0,2},{1,3},{2,0},{3,1},{4,6},{5,7},{6,4},{7,5},{8,10},{9,11},{10,... | collective-permute-start | bytes 1179656 | tf_op jit(solution)/shard_map/ppermute | solution.py:655
  107.4 10.4 %collective-permute-start.23 = (bf16[64,1536]{1,0:T(8,128)(2,1)S(1)}, bf16[64,1536]{1,0:T(8,128)(2,1)S(1)}, u32[]{:S(2)}, u32[]{:S(2)}) collective-permute-start(bf16[64,1536]{1,0:T(8,128)(2,1)S(1)} %multiply_convert_fusion), channel_id=1, source_target_pairs={{0,16},{8,24},{16,0},{24,8},{1,17},{9,25},{17,1},{25,9},{2,18},{10... | collective-permute-start | bytes 589832 | tf_op jit(solution)/shard_map/ppermute | solution.py:655
  118.6 16.2 %collective-permute-start.28 = (bf16[128,1536]{1,0:T(8,128)(2,1)S(1)}, bf16[128,1536]{1,0:T(8,128)(2,1)S(1)}, u32[]{:S(2)}, u32[]{:S(2)}) collective-permute-start(bf16[128,1536]{1,0:T(8,128)(2,1)S(1)} %get-tuple-element.172), channel_id=1, source_target_pairs={{0,8},{8,0},{16,24},{24,16},{1,9},{9,1},{17,25},{25,17},{2,10},{10... | collective-permute-start | bytes 1179656 | tf_op jit(solution)/shard_map/ppermute | solution.py:655
  118.6 18.8 %collective-permute-start.29 = (bf16[128,1536]{1,0:T(8,128)(2,1)S(1)}, bf16[128,1536]{1,0:T(8,128)(2,1)S(1)}, u32[]{:S(2)}, u32[]{:S(2)}) collective-permute-start(bf16[128,1536]{1,0:T(8,128)(2,1)S(1)} %get-tuple-element.172), channel_id=1, source_target_pairs={{0,2},{1,3},{2,0},{3,1},{4,6},{5,7},{6,4},{7,5},{8,10},{9,11},{10,... | collective-permute-start | bytes 1179656 | tf_op jit(solution)/shard_map/ppermute | solution.py:655
  119.4 15.4 %collective-permute-start.30 = (bf16[3,64,560]{2,1,0:T(8,128)(2,1)S(1)}, bf16[3,64,560]{2,1,0:T(8,128)(2,1)S(1)}, u32[]{:S(2)}, u32[]{:S(2)}) collective-permute-start(bf16[3,64,560]{2,1,0:T(8,128)(2,1)S(1)} %copy-done.31), channel_id=1, source_target_pairs={{0,24},{8,16},{16,8},{24,0},{1,25},{9,17},{17,9},{25,1},{2,26},{10... | collective-permute-start | bytes 645128 | tf_op jit(solution)/shard_map/ppermute | solution.py:655
  122.7 20.6 %collective-permute-start.33 = (bf16[3,192,560]{2,1,0:T(8,128)(2,1)S(1)}, bf16[3,192,560]{2,1,0:T(8,128)(2,1)S(1)}, u32[]{:S(2)}, u32[]{:S(2)}) collective-permute-start(bf16[3,192,560]{2,1,0:T(8,128)(2,1)S(1)} %collective-permute-done.24.refs_1_), channel_id=1, source_target_pairs={{0,4},{4,0},{1,5},{5,1},{2,6},{6,2},{3,7},{7,3},{8,12},{12,8},{9,1... | collective-permute-start | bytes 1935368 | tf_op jit(solution)/shard_map/ppermute | solution.py:655
  134.8 8.5 %collective-permute-start.31 = (bf16[128,1536]{1,0:T(8,128)(2,1)S(1)}, bf16[128,1536]{1,0:T(8,128)(2,1)S(1)}, u32[]{:S(2)}, u32[]{:S(2)}) collective-permute-start(bf16[128,1536]{1,0:T(8,128)(2,1)S(1)} %collective-permute-done.28), channel_id=1, source_target_pairs={{0,2},{1,3},{2,0},{3,1},{4,6},{5,7},{6,4},{7,5},{8,10},{9,11},{10,... | collective-permute-start | bytes 1179656 | tf_op jit(solution)/shard_map/ppermute | solution.py:655
  135.5 8.1 %collective-permute-start.32 = (bf16[3,64,560]{2,1,0:T(8,128)(2,1)S(1)}, bf16[3,64,560]{2,1,0:T(8,128)(2,1)S(1)}, u32[]{:S(2)}, u32[]{:S(2)}) collective-permute-start(bf16[3,64,560]{2,1,0:T(8,128)(2,1)S(1)} %copy-done.29), channel_id=1, source_target_pairs={{0,24},{8,16},{16,8},{24,0},{1,25},{9,17},{17,9},{25,1},{2,26},{10... | collective-permute-start | bytes 645128 | tf_op jit(solution)/shard_map/ppermute | solution.py:655
  137.4 32.7 %collective-permute-start.35 = (bf16[512,1536]{1,0:T(8,128)(2,1)S(1)}, bf16[512,1536]{1,0:T(8,128)(2,1)S(1)}, u32[]{:S(2)}, u32[]{:S(2)}) collective-permute-start(bf16[512,1536]{1,0:T(8,128)(2,1)S(1)} %constant_dynamic-update-slice_fusion.9.cot_ref.refs_2_), channel_id=1, source_target_pairs={{0,1},{1,0},{2,3},{3,2},{4,5},{5,4},{6,7},{7,6},{8,9},{9,8},{10,11... | collective-permute-start | bytes 4718600 | tf_op jit(solution)/shard_map/ppermute | solution.py:655
  143.6 26.5 %collective-permute-start.34 = (bf16[512,1536]{1,0:T(8,128)(2,1)S(1)}, bf16[512,1536]{1,0:T(8,128)(2,1)S(1)}, u32[]{:S(2)}, u32[]{:S(2)}) collective-permute-start(bf16[512,1536]{1,0:T(8,128)(2,1)S(1)} %constant_dynamic-update-slice_fusion.4.n2_ref.refs_0_), channel_id=1, source_target_pairs={{0,1},{1,0},{2,3},{3,2},{4,5},{5,4},{6,7},{7,6},{8,9},{9,8},{10,11... | collective-permute-start | bytes 4718600 | tf_op jit(solution)/shard_map/ppermute | solution.py:655
  143.6 8.4 %collective-permute-start.38 = (bf16[3,64,560]{2,1,0:T(8,128)(2,1)S(1)}, bf16[3,64,560]{2,1,0:T(8,128)(2,1)S(1)}, u32[]{:S(2)}, u32[]{:S(2)}) collective-permute-start(bf16[3,64,560]{2,1,0:T(8,128)(2,1)S(1)} %collective-permute-done.30.refs_5_), channel_id=1, source_target_pairs={{0,4},{4,0},{1,5},{5,1},{2,6},{6,2},{3,7},{7,3},{8,12},{12,8},{9,1... | collective-permute-start | bytes 645128 | tf_op jit(solution)/shard_map/ppermute | solution.py:655
  151.9 8.9 %collective-permute-start.39 = (bf16[3,64,560]{2,1,0:T(8,128)(2,1)S(1)}, bf16[3,64,560]{2,1,0:T(8,128)(2,1)S(1)}, u32[]{:S(2)}, u32[]{:S(2)}) collective-permute-start(bf16[3,64,560]{2,1,0:T(8,128)(2,1)S(1)} %collective-permute-done.32.refs_6_), channel_id=1, source_target_pairs={{0,4},{4,0},{1,5},{5,1},{2,6},{6,2},{3,7},{7,3},{8,12},{12,8},{9,1... | collective-permute-start | bytes 645128 | tf_op jit(solution)/shard_map/ppermute | solution.py:655
  152.2 9.3 %collective-permute-start.36 = (bf16[3,64,560]{2,1,0:T(8,128)(2,1)S(1)}, bf16[3,64,560]{2,1,0:T(8,128)(2,1)S(1)}, u32[]{:S(2)}, u32[]{:S(2)}) collective-permute-start(bf16[3,64,560]{2,1,0:T(8,128)(2,1)S(1)} %copy-done.27), channel_id=1, source_target_pairs={{0,24},{8,16},{16,8},{24,0},{1,25},{9,17},{17,9},{25,1},{2,26},{10... | collective-permute-start | bytes 645128 | tf_op jit(solution)/shard_map/ppermute | solution.py:655
  154.4 11.7 %collective-permute-start.37 = (bf16[3,64,560]{2,1,0:T(8,128)(2,1)S(1)}, bf16[3,64,560]{2,1,0:T(8,128)(2,1)S(1)}, u32[]{:S(2)}, u32[]{:S(2)}) collective-permute-start(bf16[3,64,560]{2,1,0:T(8,128)(2,1)S(1)} %collective-permute-done.20.refs_4_), channel_id=1, source_target_pairs={{0,4},{4,0},{1,5},{5,1},{2,6},{6,2},{3,7},{7,3},{8,12},{12,8},{9,1... | collective-permute-start | bytes 645128 | tf_op jit(solution)/shard_map/ppermute | solution.py:655
  161.6 8.5 %collective-permute-start.40 = (bf16[3,64,560]{2,1,0:T(8,128)(2,1)S(1)}, bf16[3,64,560]{2,1,0:T(8,128)(2,1)S(1)}, u32[]{:S(2)}, u32[]{:S(2)}) collective-permute-start(bf16[3,64,560]{2,1,0:T(8,128)(2,1)S(1)} %collective-permute-done.36.refs_7_), channel_id=1, source_target_pairs={{0,4},{4,0},{1,5},{5,1},{2,6},{6,2},{3,7},{7,3},{8,12},{12,8},{9,1... | collective-permute-start | bytes 645128 | tf_op jit(solution)/shard_map/ppermute | solution.py:655
  182.1 12.3 %collective-permute-start.41 = (bf16[512,1536]{1,0:T(8,128)(2,1)}, bf16[512,1536]{1,0:T(8,128)(2,1)}, u32[]{:S(2)}, u32[]{:S(2)}) collective-permute-start(bf16[512,1536]{1,0:T(8,128)(2,1)} %get-tuple-element.192), channel_id=1, source_target_pairs={{0,1},{1,0},{2,3},{3,2},{4,5},{5,4},{6,7},{7,6},{8,9},{9,8},{10,11... | collective-permute-start | bytes 4718600 | tf_op jit(solution)/shard_map/ppermute | solution.py:655
  195.9 12.0 %collective-permute-start.43 = (bf16[128,1536]{1,0:T(8,128)(2,1)S(1)}, bf16[128,1536]{1,0:T(8,128)(2,1)S(1)}, u32[]{:S(2)}, u32[]{:S(2)}) collective-permute-start(bf16[128,1536]{1,0:T(8,128)(2,1)S(1)} %get-tuple-element.277), channel_id=1, source_target_pairs={{0,2},{1,3},{2,0},{3,1},{4,6},{5,7},{6,4},{7,5},{8,10},{9,11},{10,... | collective-permute-start | bytes 1179656 | tf_op jit(solution)/shard_map/ppermute | solution.py:655
  203.1 18.7 %collective-permute-start.46 = (bf16[3,192,560]{2,1,0:T(8,128)(2,1)S(1)}, bf16[3,192,560]{2,1,0:T(8,128)(2,1)S(1)}, u32[]{:S(2)}, u32[]{:S(2)}) collective-permute-start(bf16[3,192,560]{2,1,0:T(8,128)(2,1)S(1)} %get-tuple-element.206), channel_id=1, source_target_pairs={{0,4},{4,0},{1,5},{5,1},{2,6},{6,2},{3,7},{7,3},{8,12},{12,8},{9,1... | collective-permute-start | bytes 1935368 | tf_op jit(solution)/shard_map/ppermute | solution.py:655
  203.6 24.0 %collective-permute-start.42 = (bf16[128,1536]{1,0:T(8,128)(2,1)S(1)}, bf16[128,1536]{1,0:T(8,128)(2,1)S(1)}, u32[]{:S(2)}, u32[]{:S(2)}) collective-permute-start(bf16[128,1536]{1,0:T(8,128)(2,1)S(1)} %get-tuple-element.276), channel_id=1, source_target_pairs={{0,2},{1,3},{2,0},{3,1},{4,6},{5,7},{6,4},{7,5},{8,10},{9,11},{10,... | collective-permute-start | bytes 1179656 | tf_op jit(solution)/shard_map/ppermute | solution.py:655
  209.0 18.5 %collective-permute-start.44 = (bf16[128,1536]{1,0:T(8,128)(2,1)S(1)}, bf16[128,1536]{1,0:T(8,128)(2,1)S(1)}, u32[]{:S(2)}, u32[]{:S(2)}) collective-permute-start(bf16[128,1536]{1,0:T(8,128)(2,1)S(1)} %add_convert_fusion.3), channel_id=1, source_target_pairs={{0,8},{8,0},{16,24},{24,16},{1,9},{9,1},{17,25},{25,17},{2,10},{10... | collective-permute-start | bytes 1179656 | tf_op jit(solution)/shard_map/ppermute | solution.py:655
  221.8 27.0 %collective-permute-start.55 = (bf16[3,192,560]{2,1,0:T(8,128)(2,1)S(1)}, bf16[3,192,560]{2,1,0:T(8,128)(2,1)S(1)}, u32[]{:S(2)}, u32[]{:S(2)}) collective-permute-start(bf16[3,192,560]{2,1,0:T(8,128)(2,1)S(1)} %get-tuple-element.216), channel_id=1, source_target_pairs={{0,4},{4,0},{1,5},{5,1},{2,6},{6,2},{3,7},{7,3},{8,12},{12,8},{9,1... | collective-permute-start | bytes 1935368 | tf_op jit(solution)/shard_map/ppermute | solution.py:655
  229.2 12.7 %collective-permute-start.45 = (bf16[64,1536]{1,0:T(8,128)(2,1)S(1)}, bf16[64,1536]{1,0:T(8,128)(2,1)S(1)}, u32[]{:S(2)}, u32[]{:S(2)}) collective-permute-start(bf16[64,1536]{1,0:T(8,128)(2,1)S(1)} %slice.488), channel_id=1, source_target_pairs={{0,16},{8,24},{16,0},{24,8},{1,17},{9,25},{17,1},{25,9},{2,18},{10... | collective-permute-start | bytes 589832 | tf_op jit(solution)/shard_map/ppermute | solution.py:655
  249.8 40.7 %collective-permute-start.64 = (bf16[3,192,560]{2,1,0:T(8,128)(2,1)}, bf16[3,192,560]{2,1,0:T(8,128)(2,1)S(1)}, u32[]{:S(2)}, u32[]{:S(2)}) collective-permute-start(bf16[3,192,560]{2,1,0:T(8,128)(2,1)} %get-tuple-element.227), channel_id=1, source_target_pairs={{0,4},{4,0},{1,5},{5,1},{2,6},{6,2},{3,7},{7,3},{8,12},{12,8},{9,1... | collective-permute-start | bytes 1935368 | tf_op jit(solution)/shard_map/ppermute | solution.py:655
  250.5 10.0 %collective-permute-start.54 = (bf16[3,64,560]{2,1,0:T(8,128)(2,1)S(1)}, bf16[3,64,560]{2,1,0:T(8,128)(2,1)S(1)}, u32[]{:S(2)}, u32[]{:S(2)}) collective-permute-start(bf16[3,64,560]{2,1,0:T(8,128)(2,1)S(1)} %get-tuple-element.213), channel_id=1, source_target_pairs={{0,24},{8,16},{16,8},{24,0},{1,25},{9,17},{17,9},{25,1},{2,26},{10... | collective-permute-start | bytes 645128 | tf_op jit(solution)/shard_map/ppermute | solution.py:655
  262.0 11.6 %collective-permute-start.49 = (bf16[512,1536]{1,0:T(8,128)(2,1)S(1)}, bf16[512,1536]{1,0:T(8,128)(2,1)S(1)}, u32[]{:S(2)}, u32[]{:S(2)}) collective-permute-start(bf16[512,1536]{1,0:T(8,128)(2,1)S(1)} %convolution_convert_fusion), channel_id=1, source_target_pairs={{0,1},{1,0},{2,3},{3,2},{4,5},{5,4},{6,7},{7,6},{8,9},{9,8},{10,11... | collective-permute-start | bytes 4718600 | tf_op jit(solution)/shard_map/ppermute | solution.py:655
  263.7 9.8 %collective-permute-start.57 = (bf16[3,64,560]{2,1,0:T(8,128)(2,1)S(1)}, bf16[3,64,560]{2,1,0:T(8,128)(2,1)S(1)}, u32[]{:S(2)}, u32[]{:S(2)}) collective-permute-start(bf16[3,64,560]{2,1,0:T(8,128)(2,1)S(1)} %get-tuple-element.218), channel_id=1, source_target_pairs={{0,24},{8,16},{16,8},{24,0},{1,25},{9,17},{17,9},{25,1},{2,26},{10... | collective-permute-start | bytes 645128 | tf_op jit(solution)/shard_map/ppermute | solution.py:655
  276.0 23.2 %collective-permute-start.66 = (bf16[3,64,560]{2,1,0:T(8,128)(2,1)}, bf16[3,64,560]{2,1,0:T(8,128)(2,1)S(1)}, u32[]{:S(2)}, u32[]{:S(2)}) collective-permute-start(bf16[3,64,560]{2,1,0:T(8,128)(2,1)} %get-tuple-element.229), channel_id=1, source_target_pairs={{0,24},{8,16},{16,8},{24,0},{1,25},{9,17},{17,9},{25,1},{2,26},{10... | collective-permute-start | bytes 645128 | tf_op jit(solution)/shard_map/ppermute | solution.py:655
  289.6 24.0 %collective-permute-start.51 = (bf16[128,1536]{1,0:T(8,128)(2,1)}, bf16[128,1536]{1,0:T(8,128)(2,1)}, u32[]{:S(2)}, u32[]{:S(2)}) collective-permute-start(bf16[128,1536]{1,0:T(8,128)(2,1)} %get-tuple-element.275), channel_id=1, source_target_pairs={{0,2},{1,3},{2,0},{3,1},{4,6},{5,7},{6,4},{7,5},{8,10},{9,11},{10,... | collective-permute-start | bytes 1179656 | tf_op jit(solution)/shard_map/ppermute | solution.py:655
  290.5 23.0 %collective-permute-start.65 = (bf16[2,192,512]{2,1,0:T(8,128)(2,1)}, bf16[2,192,512]{2,1,0:T(8,128)(2,1)}, u32[]{:S(2)}, u32[]{:S(2)}) collective-permute-start(bf16[2,192,512]{2,1,0:T(8,128)(2,1)} %get-tuple-element.228), channel_id=1, source_target_pairs={{0,4},{4,0},{1,5},{5,1},{2,6},{6,2},{3,7},{7,3},{8,12},{12,8},{9,1... | collective-permute-start | bytes 1179656 | tf_op jit(solution)/shard_map/ppermute | solution.py:655
  293.8 13.4 %collective-permute-start.60 = (bf16[64,1536]{1,0:T(8,128)(2,1)}, bf16[64,1536]{1,0:T(8,128)(2,1)}, u32[]{:S(2)}, u32[]{:S(2)}) collective-permute-start(bf16[64,1536]{1,0:T(8,128)(2,1)} %fusion.42), channel_id=1, source_target_pairs={{0,2},{1,3},{2,0},{3,1},{4,6},{5,7},{6,4},{7,5},{8,10},{9,11},{10,... | collective-permute-start | bytes 589832 | tf_op jit(solution)/shard_map/ppermute | solution.py:655
  299.2 83.4 %collective-permute-start.75 = (bf16[3,192,560]{2,1,0:T(8,128)(2,1)}, bf16[3,192,560]{2,1,0:T(8,128)(2,1)S(1)}, u32[]{:S(2)}, u32[]{:S(2)}) collective-permute-start(bf16[3,192,560]{2,1,0:T(8,128)(2,1)} %add_convert_fusion.1), channel_id=1, source_target_pairs={{0,8},{8,0},{16,24},{24,16},{1,9},{9,1},{17,25},{25,17},{2,10},{10... | collective-permute-start | bytes 1935368 | tf_op jit(solution)/shard_map/ppermute | solution.py:655
  304.7 33.6 %collective-permute-start.50 = (bf16[128,1536]{1,0:T(8,128)(2,1)}, bf16[128,1536]{1,0:T(8,128)(2,1)}, u32[]{:S(2)}, u32[]{:S(2)}) collective-permute-start(bf16[128,1536]{1,0:T(8,128)(2,1)} %get-tuple-element.274), channel_id=1, source_target_pairs={{0,2},{1,3},{2,0},{3,1},{4,6},{5,7},{6,4},{7,5},{8,10},{9,11},{10,... | collective-permute-start | bytes 1179656 | tf_op jit(solution)/shard_map/ppermute | solution.py:655
  307.2 20.0 %collective-permute-start.67 = (bf16[3,64,560]{2,1,0:T(8,128)(2,1)}, bf16[3,64,560]{2,1,0:T(8,128)(2,1)S(1)}, u32[]{:S(2)}, u32[]{:S(2)}) collective-permute-start(bf16[3,64,560]{2,1,0:T(8,128)(2,1)} %get-tuple-element.230), channel_id=1, source_target_pairs={{0,16},{8,24},{16,0},{24,8},{1,17},{9,25},{17,1},{25,9},{2,18},{10... | collective-permute-start | bytes 645128 | tf_op jit(solution)/shard_map/ppermute | solution.py:655
  315.1 24.9 %collective-permute-start.52 = (bf16[128,1536]{1,0:T(8,128)(2,1)S(1)}, bf16[128,1536]{1,0:T(8,128)(2,1)S(1)}, u32[]{:S(2)}, u32[]{:S(2)}) collective-permute-start(bf16[128,1536]{1,0:T(8,128)(2,1)S(1)} %fusion.20), channel_id=1, source_target_pairs={{0,8},{8,0},{16,24},{24,16},{1,9},{9,1},{17,25},{25,17},{2,10},{10... | collective-permute-start | bytes 1179656 | tf_op jit(solution)/shard_map/ppermute | solution.py:655
  322.9 12.0 %collective-permute-start.79 = (f32[40,128]{1,0:T(8,128)S(1)}, f32[40,128]{1,0:T(8,128)S(1)}, u32[]{:S(2)}, u32[]{:S(2)}) collective-permute-start(f32[40,128]{1,0:T(8,128)S(1)} %add.296), channel_id=1, source_target_pairs={{0,16},{8,24},{16,0},{24,8},{1,17},{9,25},{17,1},{25,9},{2,18},{10... | collective-permute-start | bytes 61448 | tf_op jit(solution)/shard_map/ppermute | solution.py:655
  327.2 29.8 %collective-permute-start.63 = (bf16[2,192,512]{2,1,0:T(8,128)(2,1)S(1)}, bf16[2,192,512]{2,1,0:T(8,128)(2,1)S(1)}, u32[]{:S(2)}, u32[]{:S(2)}) collective-permute-start(bf16[2,192,512]{2,1,0:T(8,128)(2,1)S(1)} %copy-done.84), channel_id=1, source_target_pairs={{0,4},{4,0},{1,5},{5,1},{2,6},{6,2},{3,7},{7,3},{8,12},{12,8},{9,1... | collective-permute-start | bytes 1179656 | tf_op jit(solution)/shard_map/ppermute | solution.py:655
  335.0 32.2 %collective-permute-start.69 = (bf16[3,64,560]{2,1,0:T(8,128)(2,1)S(1)}, bf16[3,64,560]{2,1,0:T(8,128)(2,1)S(1)}, u32[]{:S(2)}, u32[]{:S(2)}) collective-permute-start(bf16[3,64,560]{2,1,0:T(8,128)(2,1)S(1)} %copy-done.73), channel_id=1, source_target_pairs={{0,16},{8,24},{16,0},{24,8},{1,17},{9,25},{17,1},{25,9},{2,18},{10... | collective-permute-start | bytes 645128 | tf_op jit(solution)/shard_map/ppermute | solution.py:655
  338.4 44.3 %collective-permute-start.72 = (bf16[4,192,384]{2,1,0:T(8,128)(2,1)S(1)}, bf16[4,192,384]{2,1,0:T(8,128)(2,1)S(1)}, u32[]{:S(2)}, u32[]{:S(2)}) collective-permute-start(bf16[4,192,384]{2,1,0:T(8,128)(2,1)S(1)} %copy-done.83), channel_id=1, source_target_pairs={{0,4},{4,0},{1,5},{5,1},{2,6},{6,2},{3,7},{7,3},{8,12},{12,8},{9,1... | collective-permute-start | bytes 1769480 | tf_op jit(solution)/shard_map/ppermute | solution.py:655
  343.8 13.1 %collective-permute-start.53 = (bf16[64,1536]{1,0:T(8,128)(2,1)S(1)}, bf16[64,1536]{1,0:T(8,128)(2,1)S(1)}, u32[]{:S(2)}, u32[]{:S(2)}) collective-permute-start(bf16[64,1536]{1,0:T(8,128)(2,1)S(1)} %slice.487), channel_id=1, source_target_pairs={{0,16},{8,24},{16,0},{24,8},{1,17},{9,25},{17,1},{25,9},{2,18},{10... | collective-permute-start | bytes 589832 | tf_op jit(solution)/shard_map/ppermute | solution.py:655
  356.9 10.0 %collective-permute-start.68 = (bf16[2,192,512]{2,1,0:T(8,128)(2,1)S(1)}, bf16[2,192,512]{2,1,0:T(8,128)(2,1)S(1)}, u32[]{:S(2)}, u32[]{:S(2)}) collective-permute-start(bf16[2,192,512]{2,1,0:T(8,128)(2,1)S(1)} %add_convert_fusion.2), channel_id=1, source_target_pairs={{0,8},{8,0},{16,24},{24,16},{1,9},{9,1},{17,25},{25,17},{2,10},{10... | collective-permute-start | bytes 1179656 | tf_op jit(solution)/shard_map/ppermute | solution.py:655
  357.1 34.6 %collective-permute-start.61 = (bf16[64,3072]{1,0:T(8,128)(2,1)S(1)}, bf16[64,3072]{1,0:T(8,128)(2,1)S(1)}, u32[]{:S(2)}, u32[]{:S(2)}) collective-permute-start(bf16[64,3072]{1,0:T(8,128)(2,1)S(1)} %pad_maximum_fusion.2), channel_id=1, source_target_pairs={{0,2},{1,3},{2,0},{3,1},{4,6},{5,7},{6,4},{7,5},{8,10},{9,11},{10,... | collective-permute-start | bytes 1179656 | tf_op jit(solution)/shard_map/ppermute | solution.py:655
  367.2 15.4 %collective-permute-start.70 = (bf16[1,192,512]{2,1,0:T(8,128)(2,1)S(1)}, bf16[1,192,512]{2,1,0:T(8,128)(2,1)S(1)}, u32[]{:S(2)}, u32[]{:S(2)}) collective-permute-start(bf16[1,192,512]{2,1,0:T(8,128)(2,1)S(1)} %slice.486), channel_id=1, source_target_pairs={{0,16},{8,24},{16,0},{24,8},{1,17},{9,25},{17,1},{25,9},{2,18},{10... | collective-permute-start | bytes 589832 | tf_op jit(solution)/shard_map/ppermute | solution.py:655
  367.3 20.4 %collective-permute-start.71 = (bf16[3,64,560]{2,1,0:T(8,128)(2,1)S(1)}, bf16[3,64,560]{2,1,0:T(8,128)(2,1)S(1)}, u32[]{:S(2)}, u32[]{:S(2)}) collective-permute-start(bf16[3,64,560]{2,1,0:T(8,128)(2,1)S(1)} %copy-done.72), channel_id=1, source_target_pairs={{0,16},{8,24},{16,0},{24,8},{1,17},{9,25},{17,1},{25,9},{2,18},{10... | collective-permute-start | bytes 645128 | tf_op jit(solution)/shard_map/ppermute | solution.py:655
  387.8 9.0 %collective-permute-start.81 = (bf16[2,192,384]{2,1,0:T(8,128)(2,1)S(1)}, bf16[2,192,384]{2,1,0:T(8,128)(2,1)S(1)}, u32[]{:S(2)}, u32[]{:S(2)}) collective-permute-start(bf16[2,192,384]{2,1,0:T(8,128)(2,1)S(1)} %add_convert_fusion.6), channel_id=1, source_target_pairs={{0,8},{8,0},{16,24},{24,16},{1,9},{9,1},{17,25},{25,17},{2,10},{10... | collective-permute-start | bytes 884744 | tf_op jit(solution)/shard_map/ppermute | solution.py:655
  387.9 18.8 %collective-permute-start.83 = (bf16[3,192,560]{2,1,0:T(8,128)(2,1)S(1)}, bf16[3,192,560]{2,1,0:T(8,128)(2,1)S(1)}, u32[]{:S(2)}, u32[]{:S(2)}) collective-permute-start(bf16[3,192,560]{2,1,0:T(8,128)(2,1)S(1)} %copy-done.25), channel_id=1, source_target_pairs={{0,4},{4,0},{1,5},{5,1},{2,6},{6,2},{3,7},{7,3},{8,12},{12,8},{9,1... | collective-permute-start | bytes 1935368 | tf_op jit(solution)/shard_map/ppermute | solution.py:655
  391.8 18.4 %collective-permute-start.62 = (bf16[2,64,3072]{2,1,0:T(8,128)(2,1)S(1)}, bf16[2,64,3072]{2,1,0:T(8,128)(2,1)S(1)}, u32[]{:S(2)}, u32[]{:S(2)}) collective-permute-start(bf16[2,64,3072]{2,1,0:T(8,128)(2,1)S(1)} %maximum_select_fusion.3), channel_id=1, source_target_pairs={{0,1},{1,0},{2,3},{3,2},{4,5},{5,4},{6,7},{7,6},{8,9},{9,8},{10,11... | collective-permute-start | bytes 2359304 | tf_op jit(solution)/shard_map/ppermute | solution.py:655
  396.9 9.0 %collective-permute-start.82 = (bf16[1,192,384]{2,1,0:T(8,128)(2,1)S(1)}, bf16[1,192,384]{2,1,0:T(8,128)(2,1)S(1)}, u32[]{:S(2)}, u32[]{:S(2)}) collective-permute-start(bf16[1,192,384]{2,1,0:T(8,128)(2,1)S(1)} %slice.489), channel_id=1, source_target_pairs={{0,16},{8,24},{16,0},{24,8},{1,17},{9,25},{17,1},{25,9},{2,18},{10... | collective-permute-start | bytes 442376 | tf_op jit(solution)/shard_map/ppermute | solution.py:655
  (105 other events, 1129.5 us)

commit v2 on v1

--- a/solution.py
+++ b/solution.py
@@ -214,27 +214,24 @@
     (FFN, AWAY): [(DN, (Z, 2))],
     (FFN, OWN): [(DN, (Z, 2))],
     (DRES, C): [(FFN, OWN), (FFN, AWAY)],
-    (G_Z, (3, 0)): [(DN, (Z, 2))],
-    HEADS_BACK: [(G_Z, (3, 0))],
+    (G_Z, 3): [(DN, (Z, 2))],
     (G_X, 1): [(G_X, 2)],
     KV_GRAD_C: [(G_X, 2)],
-    (G_Z, (3, 1)): [(DRES, C)],
-    KV_GRAD_X: [(G_Z, (3, 1)), (FFN, C)],
     (FFN, C): [(DRES, C)],
-    (G_Z, (3, 2)): [KV_GRAD_C],
-    (PROJ, XF): [(G_X, 1)],
+    KV_GRAD_X: [(FFN, C)],
+    (PROJ, XF): [(G_X, 1), (G_Z, 3)],
+    (FFN, Y): [KV_GRAD_C],
     (DN1, C): [(PROJ, GRAD)],
-    (G_Z, (2, 0)): [(PROJ, GRAD)],
-    (PROJ, (Z, 1)): [(G_Z, (3, 2)), (G_Z, (2, 0)), (FFN, YB), (DN1, Y)],
-    (G_Z, (2, 1)): [(PROJ, XF)],
-    (PROJ, (Z, 2)): [(G_Z, (2, 1)), (FFN, (Z, 1))],
-    (VECTOR, C): [(PROJ, XF)],
-    (OUT, X): [(PROJ, XF)],
-    (G_Z, (2, 2)): [(PROJ, (Z, 1))],
-    (G_Z, (1, 0)): [(G_Z, (3, 2))],
-    KV_DONE_Y: [(G_Z, (2, 2)), (OUT, X), (VECTOR, Y), (G_Z, (1, 0))],
+    (G_Z, 2): [(G_Z, 3)],
+    (G_Z, 1): [KV_GRAD_X],
+    (PROJ, (Z, 1)): [(FFN, Y), (G_Z, 1)],
+    (PROJ, (Z, 2)): [(DN1, Y), (FFN, (Z, 1))],
+    (VECTOR, C): [(PROJ, XN)],
+    (OUT, X): [(PROJ, XN)],
+    (FFN, (Z, 1)): [(FFN, Y)],
     (G_X, 0): [(OUT, X)],
     (OUT, GRAD): [KV_GRAD_C],
+    KV_DONE_Y: [(G_Z, 2)],
 }
 
 
@@ -272,16 +269,16 @@
     return dict(zip(flat, outs))
 
 
-def join_columns(blocks, n, rows):
-    keys = list(blocks)
-    count, _, part = blocks[keys[0]].shape
+def join_columns(blocks):
+    n = len(blocks)
+    count, rows, part = blocks[0].shape
 
     def kernel(*refs):
-        ins, outs, held = refs[: len(keys)], refs[len(keys) : -1], refs[-1]
+        ins, outs, held = refs[:n], refs[n:-1], refs[-1]
         d = lax.axis_index("dp")
         for i in range(count):
-            for ref, (j, (low, high)) in zip(ins, keys):
-                held[d ^ j, low:high] = ref[i]
+            for j, ref in enumerate(ins):
+                held[d ^ j] = ref[i]
             for t in range(n):
                 outs[i][:, t * part : (t + 1) * part] = held[t].astype(F32)
 
@@ -291,7 +288,7 @@
         out_shape=[jax.ShapeDtypeStruct((rows, n * part), F32)] * count,
         scratch_shapes=[pltpu.VMEM((n, rows, part), BF)],
         compiler_params=pltpu.CompilerParams(vmem_limit_bytes=48 << 20),
-    )(*blocks.values())
+    )(*blocks)
 
 
 def key_value_slots(w_key, w_value, vectors):
@@ -714,7 +711,7 @@
             )
             move((name, C), C, of((name, OWN)))
 
-        def rows_sum(name):
+        def rows_sum(name, split):
             move((name, C), C, of((name, AWAY)))
             last = (name, (Z, bits[-1]))
 
@@ -725,8 +722,17 @@
 
             for i in range(4):
                 makers[(name, PART, i)] = lambda i=i: part(i)
-            move((name, YB), Y, lambda: get((name, PART, 3)).astype(BF))
-            move((name, YA), Y, lambda: get((name, PART, 2)).astype(BF))
+            if split:
+                move((name, YB), Y, lambda: get((name, PART, 3)).astype(BF))
+                move((name, YA), Y, lambda: get((name, PART, 2)).astype(BF))
+            else:
+
+                def parts():
+                    return jnp.concatenate([get((name, PART, 2)), get((name, PART, 3))]).astype(BF)
+
+                move((name, Y), Y, parts)
+                makers[(name, YA)] = lambda: get((name, Y))[: get((name, PART, 2)).shape[0]]
+                makers[(name, YB)] = lambda: get((name, Y))[get((name, PART, 2)).shape[0] :]
             move(
                 last,
                 (Z, bits[-1]),
@@ -771,20 +777,19 @@
 
         for k in range(n_dp):
             move((G_X, k), X, lambda k=k: grad_piece(k, 1))
-        for k, cut, tail in tails:
-
-            def summed(k=k, cut=cut, tail=tail):
-                low, high = cut
-                own = tied((G_SUM, tail), grad_piece(k, 0)[:, low:high]).astype(F32)
-                return (own + get((G_X, k))[:, low:high].astype(F32)).astype(BF)
-
-            makers[(G_SUM, tail)] = summed
+        for k in range(n_dp):
+
+            def summed(k=k):
+                own = tied((G_SUM, k), grad_piece(k, 0)).astype(F32)
+                return (own + get((G_X, k)).astype(F32)).astype(BF)
+
+            makers[(G_SUM, k)] = summed
             if k:
-                move((G_Z, tail), (Z, k), of((G_SUM, tail)))
+                move((G_Z, k), (Z, k), of((G_SUM, k)))
             else:
-                makers[(G_Z, tail)] = of((G_SUM, tail))
+                makers[(G_Z, k)] = of((G_SUM, k))
         makers[GRADS_DONE] = lambda: join_columns(
-            {(k, cut): get((G_Z, tail)) for k, cut, tail in tails}, n_dp, w_rows
+            [get((G_Z, k)) for k in range(n_dp)]
         )
 
         def gather_grad(name, rows, diff, split):
@@ -990,9 +995,9 @@
         makers[(FFN, AWAY)] = lambda: dot_nt(
             tied((FFN, AWAY), get(HIDDEN_AWAY)[0]), get(FEED_AWAY)[2]
         ).astype(BF)
-        rows_sum(DN)
-
-        rows_sum(FFN)
+        rows_sum(DN, True)
+
+        rows_sum(FFN, False)
 
         @task(DIFF_RES)
         def diff_res():

time: 418 us -> 400 us (0.957)
  starting transfers between devices: 103 us -> 81.6 us
  local copies, waits for them, and re-layouts: 21.4 us -> 36.9 us
  waiting for transfers between devices: 181 us -> 171 us
    ppermute x84 -> x79, starting transfers between devices: 103 us -> 81.6 us  [move(): makers[name] = lambda: lax.ppermute(tied(name, maker()), *links[link])]
    unnamed x179 -> x189, local copies, waits for them, and re-layouts: 13.6 us -> 27.3 us
    ppermute x84 -> x79, waiting for transfers between devices: 181 us -> 171 us  [move(): makers[name] = lambda: lax.ppermute(tied(name, maker()), *links[link])]
  transfers between devices with their start and end apart: 84 -> 79, of which waited for: 41 -> 42; matrix products, arithmetic and copies ran while one was open for 14% -> 16% of each run, Pallas kernels for 9% -> 9%
where the time goes in v2:
time: 400 us; the launch traced here: 394 us
  waiting for transfers between devices  171 us (43%)
  starting transfers between devices  81.6 us (20%)
  Pallas kernels  51.5 us (13%)
  other arithmetic  41.1 us (10%)
  local copies, waits for them, and re-layouts  36.9 us (9%)
  matrix products  9.84 us (2%)
    ppermute x79, waiting for transfers between devices, move(): makers[name] = lambda: lax.ppermute(tied(name, maker()), *links[link])  171 us
    ppermute x79, starting transfers between devices, move(): makers[name] = lambda: lax.ppermute(tied(name, maker()), *links[link])  81.6 us
    unnamed x189, local copies, waits for them, and re-layouts  27.3 us
    pallas_call x2, Pallas kernels, weight_grads(): pl.pallas_call(kernel, cost_estimate=CHEAP, out_shape=[jax.ShapeDtypeStru...  9.5 us
  transfers between devices with their start and end apart: 79, of which 42 were waited for; matrix products, arithmetic and copies ran while one was open for 16% of the time, Pallas kernels for 9%

profile of v2, /device:TPU:0, one launch (start us, length us, event | category | flops | bytes accessed | tf_op | source)
XLA Modules:
  0.0 394.4 jit_solution(8087663164162148677)
XLA Ops:
  2.2 3.0 collective-permute-start.1
  5.2 2.6 collective-permute-start
  7.7 1.6 constant_dynamic-update-slice_fusion.13
  14.9 2.0 shard_map.264
  20.5 1.7 collective-permute-start.3
  23.8 1.5 collective-permute-start.5
  26.3 3.1 collective-permute-start.9
  29.4 2.4 collective-permute-done.5
  33.7 2.9 collective-permute-start.6
  40.5 2.0 shard_map.265
  42.5 9.6 %collective-permute-done.4.refs_2_ = bf16[3,64,560]{2,1,0:T(8,128)(2,1)S(1)} collective-permute-done((bf16[3,64,560]{2,1,0:T(8,128)(2,1)}, bf16[3,64,560]{2,1,0:T(8,128)(2,1)S(1)}, u32[]{:S(2)}, u32[]{:S(2)}) %collective-permute-start.4) | collective-permute-done | bytes 215072 | tf_op jit(solution)/shard_map/ppermute | solution.py:652
  52.1 2.5 shard_map.266.w_ref
  54.6 3.7 shard_map.267
  58.3 2.8 collective-permute-start.12
  64.4 4.6 %collective-permute-done.13 = bf16[64,1536]{1,0:T(8,128)(2,1)S(1)} collective-permute-done((bf16[64,1536]{1,0:T(8,128)(2,1)S(1)}, bf16[64,1536]{1,0:T(8,128)(2,1)S(1)}, u32[]{:S(2)}, u32[]{:S(2)}) %collective-permute-start.13) | collective-permute-done | bytes 196640 | tf_op jit(solution)/shard_map/ppermute | solution.py:652
  70.5 2.3 collective-permute-start.16
  73.8 2.0 collective-permute-done.15.refs_1_
  75.8 2.5 shard_map.268.o_ref
  78.3 4.8 %shard_map.269 = (bf16[256,384]{1,0:T(8,128)(2,1)}, f32[256,3]{1,0:T(8,128)}, f32[2,64,1536]{2,1,0:T(8,128)}, bf16[2,64,1536]{2,1,0:T(8,128)(2,1)}) custom-call(bf16[256,384]{1,0:T(8,128)(2,1)} %get-tuple-element.145.q_ref, bf16[512,128]{1,0:T(8,128)(2,1)} %constant_dynamic-update-slice_fusion.seen_ref, bf16[512,128]{1,0:T(8,128)(2,1)} %collective-permute-done.14.other_ref, ...), custom_call_target="tpu_custom_call" | custom-call | tf_op jit(solution)/shard_map/pallas_call | solution.py:422
  83.2 2.3 collective-permute-done.17
  92.2 11.1 %collective-permute-done.19 = bf16[64,1536]{1,0:T(8,128)(2,1)S(1)} collective-permute-done((bf16[64,1536]{1,0:T(8,128)(2,1)S(1)}, bf16[64,1536]{1,0:T(8,128)(2,1)S(1)}, u32[]{:S(2)}, u32[]{:S(2)}) %collective-permute-start.19) | collective-permute-done | bytes 196640 | tf_op jit(solution)/shard_map/ppermute | solution.py:652
  103.3 1.7 collective-permute-start.25
  107.7 1.8 collective-permute-start.23
  109.5 2.0 collective-permute-done.25.refs_10_
  111.9 6.1 %collective-permute-done.23 = bf16[64,1536]{1,0:T(8,128)(2,1)S(1)} collective-permute-done((bf16[64,1536]{1,0:T(8,128)(2,1)S(1)}, bf16[64,1536]{1,0:T(8,128)(2,1)S(1)}, u32[]{:S(2)}, u32[]{:S(2)}) %collective-permute-start.23) | collective-permute-done | bytes 196640 | tf_op jit(solution)/shard_map/ppermute | solution.py:652
  119.6 3.4 collective-permute-start.30
  123.3 11.7 %collective-permute-done.30.refs_5_ = bf16[3,64,560]{2,1,0:T(8,128)(2,1)S(1)} collective-permute-done((bf16[3,64,560]{2,1,0:T(8,128)(2,1)S(1)}, bf16[3,64,560]{2,1,0:T(8,128)(2,1)S(1)}, u32[]{:S(2)}, u32[]{:S(2)}) %collective-permute-start.30) | collective-permute-done | bytes 215072 | tf_op jit(solution)/shard_map/ppermute | solution.py:652
  135.7 1.7 collective-permute-start.32
  137.5 6.0 %collective-permute-done.31 = bf16[128,1536]{1,0:T(8,128)(2,1)S(1)} collective-permute-done((bf16[128,1536]{1,0:T(8,128)(2,1)S(1)}, bf16[128,1536]{1,0:T(8,128)(2,1)S(1)}, u32[]{:S(2)}, u32[]{:S(2)}) %collective-permute-start.31) | collective-permute-done | bytes 393248 | tf_op jit(solution)/shard_map/ppermute | solution.py:652
  143.9 8.3 %collective-permute-done.38.refs_13_ = bf16[3,64,560]{2,1,0:T(8,128)(2,1)S(1)} collective-permute-done((bf16[3,64,560]{2,1,0:T(8,128)(2,1)S(1)}, bf16[3,64,560]{2,1,0:T(8,128)(2,1)S(1)}, u32[]{:S(2)}, u32[]{:S(2)}) %collective-permute-start.38) | collective-permute-done | bytes 215072 | tf_op jit(solution)/shard_map/ppermute | solution.py:652
  152.5 1.9 collective-permute-start.36
  154.3 1.7 collective-permute-start.37
  156.1 5.0 %collective-permute-done.39.refs_14_ = bf16[3,64,560]{2,1,0:T(8,128)(2,1)S(1)} collective-permute-done((bf16[3,64,560]{2,1,0:T(8,128)(2,1)S(1)}, bf16[3,64,560]{2,1,0:T(8,128)(2,1)S(1)}, u32[]{:S(2)}, u32[]{:S(2)}) %collective-permute-start.39) | collective-permute-done | bytes 215072 | tf_op jit(solution)/shard_map/ppermute | solution.py:652
  161.8 1.6 collective-permute-start.40
  163.4 2.9 collective-permute-done.37.refs_12_
  166.3 4.0 %collective-permute-done.40.refs_15_ = bf16[3,64,560]{2,1,0:T(8,128)(2,1)S(1)} collective-permute-done((bf16[3,64,560]{2,1,0:T(8,128)(2,1)S(1)}, bf16[3,64,560]{2,1,0:T(8,128)(2,1)S(1)}, u32[]{:S(2)}, u32[]{:S(2)}) %collective-permute-start.40) | collective-permute-done | bytes 215072 | tf_op jit(solution)/shard_map/ppermute | solution.py:652
  170.3 7.1 %shard_map.270 = (bf16[1536,560]{1,0:T(8,128)(2,1)}, bf16[1536,560]{1,0:T(8,128)(2,1)}, bf16[1536,560]{1,0:T(8,128)(2,1)}, bf16[512,560]{1,0:T(8,128)(2,1)S(1)},...) custom-call(bf16[512,1536]{1,0:T(8,128)(2,1)S(1)} %collective-permute-done.34.n2_ref.refs_, ...), custom_call_target="tpu_custom_call" | custom-call | tf_op jit(solution)/shard_map/pallas_call | solution.py:498
  184.6 6.8 %shard_map.271 = (bf16[512,560]{1,0:T(8,128)(2,1)S(1)}, bf16[512,560]{1,0:T(8,128)(2,1)S(1)}, bf16[512,560]{1,0:T(8,128)(2,1)S(1)}, f32[512,1536]{1,0:T(8,128)S(1)}) custom-call(bf16[512,1536]{1,0:T(8,128)(2,1)S(1)} %constant_dynamic-update-slice_fusion.4.n2_ref.refs_0_, bf16[512,1536]{1,0:T(8,128)(2,1)S(1)} %constant_dynamic-update-slice_fusion.9.cot_ref.refs_2_, ...), custom_call_target="tpu_custom_call" | custom-call | tf_op jit(solution)/shard_map/pallas_call | solution.py:515
  210.7 4.2 %shard_map.272 = (bf16[3,192,560]{2,1,0:T(8,128)(2,1)S(1)}, bf16[3,192,560]{2,1,0:T(8,128)(2,1)S(1)}, bf16[3,192,560]{2,1,0:T(8,128)(2,1)S(1)}, bf16[3,192,560]{2,1,0:T(8,128)(2,1)S(1)}) custom-call(bf16[512,1536]{1,0:T(8,128)(2,1)S(1)} %constant_dynamic-update-slice_fusion.4.n2_ref.refs_0_, bf16[512,1536]{1,0:T(8,128)(2,1)S(1)} %copy-done.3, ...), custom_call_target="tpu_custom_call" | custom-call | tf_op jit(solution)/shard_map/pallas_call | solution.py:557
  216.9 3.5 collective-permute-start.44
  222.5 5.3 %shard_map.273 = (bf16[3,192,560]{2,1,0:T(8,128)(2,1)S(1)}, bf16[3,192,560]{2,1,0:T(8,128)(2,1)S(1)}, bf16[3,192,560]{2,1,0:T(8,128)(2,1)S(1)}, bf16[3,192,560]{2,1,0:T(8,128)(2,1)}) custom-call(bf16[512,1536]{1,0:T(8,128)(2,1)S(1)} %constant_dynamic-update-slice_fusion.4.n2_ref.refs_0_, bf16[512,1536]{1,0:T(8,128)(2,1)S(1)} %copy-done.3, ...), custom_call_target="tpu_custom_call" | custom-call | tf_op jit(solution)/shard_map/pallas_call | solution.py:557
  227.9 1.8 collective-permute-done.44
  231.6 7.6 %collective-permute-done.46 = bf16[3,192,560]{2,1,0:T(8,128)(2,1)S(1)} collective-permute-done((bf16[3,192,560]{2,1,0:T(8,128)(2,1)S(1)}, bf16[3,192,560]{2,1,0:T(8,128)(2,1)S(1)}, u32[]{:S(2)}, u32[]{:S(2)}) %collective-permute-start.46) | collective-permute-done | bytes 645152 | tf_op jit(solution)/shard_map/ppermute | solution.py:652
  243.4 3.1 fusion.86
  249.6 6.7 %collective-permute-done.50 = bf16[3,192,560]{2,1,0:T(8,128)(2,1)S(1)} collective-permute-done((bf16[3,192,560]{2,1,0:T(8,128)(2,1)S(1)}, bf16[3,192,560]{2,1,0:T(8,128)(2,1)S(1)}, u32[]{:S(2)}, u32[]{:S(2)}) %collective-permute-start.50) | collective-permute-done | bytes 645152 | tf_op jit(solution)/shard_map/ppermute | solution.py:652
  267.8 7.7 %collective-permute-done.55 = f32[256,128]{1,0:T(8,128)S(1)} collective-permute-done((f32[256,128]{1,0:T(8,128)S(1)}, f32[256,128]{1,0:T(8,128)S(1)}, u32[]{:S(2)}, u32[]{:S(2)}) %collective-permute-start.55) | collective-permute-done | bytes 131104 | tf_op jit(solution)/shard_map/ppermute | solution.py:652
  279.5 3.0 shard_map.274
  283.6 2.2 add_convert_fusion.2
  285.8 4.8 %collective-permute-start.67 = (bf16[3,192,560]{2,1,0:T(8,128)(2,1)}, bf16[3,192,560]{2,1,0:T(8,128)(2,1)S(1)}, u32[]{:S(2)}, u32[]{:S(2)}) collective-permute-start(bf16[3,192,560]{2,1,0:T(8,128)(2,1)} %add_convert_fusion.1), channel_id=1, source_target_pairs={{0,16},{8,24},{16,0},{24,8},{1,17},{9,25},{17,1},{25,9},{2,18},{10... | collective-permute-start | bytes 1935368 | tf_op jit(solution)/shard_map/ppermute | solution.py:652
  290.6 2.8 shard_map.275
  297.2 2.6 fusion.21
  308.5 2.9 collective-permute-done.63
  314.0 13.4 %collective-permute-done.71 = f32[40,128]{1,0:T(8,128)S(1)} collective-permute-done((f32[40,128]{1,0:T(8,128)S(1)}, f32[40,128]{1,0:T(8,128)S(1)}, u32[]{:S(2)}, u32[]{:S(2)}) %collective-permute-start.71) | collective-permute-done | bytes 20512 | tf_op jit(solution)/shard_map/ppermute | solution.py:652
  327.8 3.4 collective-permute-done.72
  332.6 3.4 collective-permute-done.73
  336.4 1.9 collective-permute-start.53
  338.4 1.6 collective-permute-done.74
  344.1 12.8 %collective-permute-done.65 = bf16[2,192,512]{2,1,0:T(8,128)(2,1)S(1)} collective-permute-done((bf16[2,192,512]{2,1,0:T(8,128)(2,1)S(1)}, bf16[2,192,512]{2,1,0:T(8,128)(2,1)S(1)}, u32[]{:S(2)}, u32[]{:S(2)}) %collective-permute-start.65) | collective-permute-done | bytes 393248 | tf_op jit(solution)/shard_map/ppermute | solution.py:652
  358.1 2.7 collective-permute-start.66
  361.3 12.0 %collective-permute-done.66 = bf16[1,192,512]{2,1,0:T(8,128)(2,1)S(1)} collective-permute-done((bf16[1,192,512]{2,1,0:T(8,128)(2,1)S(1)}, bf16[1,192,512]{2,1,0:T(8,128)(2,1)S(1)}, u32[]{:S(2)}, u32[]{:S(2)}) %collective-permute-start.66) | collective-permute-done | bytes 196640 | tf_op jit(solution)/shard_map/ppermute | solution.py:652
  380.1 5.4 %collective-permute-done.58 = bf16[64,3072]{1,0:T(8,128)(2,1)S(1)} collective-permute-done((bf16[64,3072]{1,0:T(8,128)(2,1)S(1)}, bf16[64,3072]{1,0:T(8,128)(2,1)S(1)}, u32[]{:S(2)}, u32[]{:S(2)}) %collective-permute-start.58) | collective-permute-done | bytes 393248 | tf_op jit(solution)/shard_map/ppermute | solution.py:652
  385.8 1.7 collective-permute-done.77
  388.4 3.3 shard_map.276
  392.2 2.1 slice_convert_fusion
  (426 shorter events, 125.7 us)
Async XLA Ops:
  2.2 7.2 %collective-permute-start.1 = (bf16[2,64,128]{2,1,0:T(8,128)(2,1)}, bf16[2,64,128]{2,1,0:T(8,128)(2,1)S(1)}, u32[]{:S(2)}, u32[]{:S(2)}) collective-permute-start(bf16[2,64,128]{2,1,0:T(8,128)(2,1)} %get-tuple-element.130), channel_id=1, source_target_pairs={{0,2},{1,3},{2,0},{3,1},{4,6},{5,7},{6,4},{7,5},{8,10},{9,11},{10,... | collective-permute-start | bytes 98312 | tf_op jit(solution)/shard_map/ppermute | solution.py:652
  5.2 14.4 %collective-permute-start = (bf16[1,192,384]{2,1,0:T(8,128)(2,1)}, bf16[1,192,384]{2,1,0:T(8,128)(2,1)}, u32[]{:S(2)}, u32[]{:S(2)}) collective-permute-start(bf16[1,192,384]{2,1,0:T(8,128)(2,1)} %bitcast.158), channel_id=1, source_target_pairs={{0,16},{8,24},{16,0},{24,8},{1,17},{9,25},{17,1},{25,9},{2,18},{10... | collective-permute-start | bytes 442376 | tf_op jit(solution)/shard_map/ppermute | solution.py:652
  11.5 6.7 %collective-permute-start.7 = (bf16[1,256,128]{2,1,0:T(8,128)(2,1)S(1)}, bf16[1,256,128]{2,1,0:T(8,128)(2,1)}, u32[]{:S(2)}, u32[]{:S(2)}) collective-permute-start(bf16[1,256,128]{2,1,0:T(8,128)(2,1)S(1)} %maximum_bitcast_fusion.1), channel_id=1, source_target_pairs={{0,16},{8,24},{16,0},{24,8},{1,17},{9,25},{17,1},{25,9},{2,18},{10... | collective-permute-start | bytes 196616 | tf_op jit(solution)/shard_map/ppermute | solution.py:652
  20.5 13.1 %collective-permute-start.3 = (bf16[2,192,384]{2,1,0:T(8,128)(2,1)S(1)}, bf16[2,192,384]{2,1,0:T(8,128)(2,1)}, u32[]{:S(2)}, u32[]{:S(2)}) collective-permute-start(bf16[2,192,384]{2,1,0:T(8,128)(2,1)S(1)} %pad_maximum_fusion.4.refs_0_), channel_id=1, source_target_pairs={{0,8},{8,0},{16,24},{24,16},{1,9},{9,1},{17,25},{25,17},{2,10},{10... | collective-permute-start | bytes 884744 | tf_op jit(solution)/shard_map/ppermute | solution.py:652
  22.3 29.8 %collective-permute-start.10 = (bf16[2,192,384]{2,1,0:T(8,128)(2,1)S(1)}, bf16[2,192,384]{2,1,0:T(8,128)(2,1)}, u32[]{:S(2)}, u32[]{:S(2)}) collective-permute-start(bf16[2,192,384]{2,1,0:T(8,128)(2,1)S(1)} %pad_maximum_fusion.4.refs_0_), channel_id=1, source_target_pairs={{0,4},{4,0},{1,5},{5,1},{2,6},{6,2},{3,7},{7,3},{8,12},{12,8},{9,1... | collective-permute-start | bytes 884744 | tf_op jit(solution)/shard_map/ppermute | solution.py:652
  23.8 8.0 %collective-permute-start.5 = (bf16[1,192,384]{2,1,0:T(8,128)(2,1)S(1)}, bf16[1,192,384]{2,1,0:T(8,128)(2,1)S(1)}, u32[]{:S(2)}, u32[]{:S(2)}) collective-permute-start(bf16[1,192,384]{2,1,0:T(8,128)(2,1)S(1)} %bitcast.153), channel_id=1, source_target_pairs={{0,16},{8,24},{16,0},{24,8},{1,17},{9,25},{17,1},{25,9},{2,18},{10... | collective-permute-start | bytes 442376 | tf_op jit(solution)/shard_map/ppermute | solution.py:652
  26.3 14.1 %collective-permute-start.9 = (bf16[4,256,128]{2,1,0:T(8,128)(2,1)S(1)}, bf16[4,256,128]{2,1,0:T(8,128)(2,1)}, u32[]{:S(2)}, u32[]{:S(2)}) collective-permute-start(bf16[4,256,128]{2,1,0:T(8,128)(2,1)S(1)} %pad_maximum_fusion.6.refs_0_), channel_id=1, source_target_pairs={{0,4},{4,0},{1,5},{5,1},{2,6},{6,2},{3,7},{7,3},{8,12},{12,8},{9,1... | collective-permute-start | bytes 786440 | tf_op jit(solution)/shard_map/ppermute | solution.py:652
  33.7 18.4 %collective-permute-start.6 = (bf16[2,192,384]{2,1,0:T(8,128)(2,1)}, bf16[2,192,384]{2,1,0:T(8,128)(2,1)}, u32[]{:S(2)}, u32[]{:S(2)}) collective-permute-start(bf16[2,192,384]{2,1,0:T(8,128)(2,1)} %pad_maximum_fusion.5), channel_id=1, source_target_pairs={{0,8},{8,0},{16,24},{24,16},{1,9},{9,1},{17,25},{25,17},{2,10},{10... | collective-permute-start | bytes 884744 | tf_op jit(solution)/shard_map/ppermute | solution.py:652
  36.5 15.5 %collective-permute-start.11 = (bf16[2,192,384]{2,1,0:T(8,128)(2,1)}, bf16[2,192,384]{2,1,0:T(8,128)(2,1)}, u32[]{:S(2)}, u32[]{:S(2)}) collective-permute-start(bf16[2,192,384]{2,1,0:T(8,128)(2,1)} %collective-permute-done.3.refs_1_), channel_id=1, source_target_pairs={{0,4},{4,0},{1,5},{5,1},{2,6},{6,2},{3,7},{7,3},{8,12},{12,8},{9,1... | collective-permute-start | bytes 884744 | tf_op jit(solution)/shard_map/ppermute | solution.py:652
  39.3 12.8 %collective-permute-start.4 = (bf16[3,64,560]{2,1,0:T(8,128)(2,1)}, bf16[3,64,560]{2,1,0:T(8,128)(2,1)S(1)}, u32[]{:S(2)}, u32[]{:S(2)}) collective-permute-start(bf16[3,64,560]{2,1,0:T(8,128)(2,1)} %get-tuple-element.133), channel_id=1, source_target_pairs={{0,16},{8,24},{16,0},{24,8},{1,17},{9,25},{17,1},{25,9},{2,18},{10... | collective-permute-start | bytes 645128 | tf_op jit(solution)/shard_map/ppermute | solution.py:652
  61.1 7.9 %collective-permute-start.13 = (bf16[64,1536]{1,0:T(8,128)(2,1)S(1)}, bf16[64,1536]{1,0:T(8,128)(2,1)S(1)}, u32[]{:S(2)}, u32[]{:S(2)}) collective-permute-start(bf16[64,1536]{1,0:T(8,128)(2,1)S(1)} %copy-done.58), channel_id=1, source_target_pairs={{0,16},{8,24},{16,0},{24,8},{1,17},{9,25},{17,1},{25,9},{2,18},{10... | collective-permute-start | bytes 589832 | tf_op jit(solution)/shard_map/ppermute | solution.py:652
  62.4 13.4 %collective-permute-start.15 = (bf16[4,192,384]{2,1,0:T(8,128)(2,1)S(1)}, bf16[4,192,384]{2,1,0:T(8,128)(2,1)}, u32[]{:S(2)}, u32[]{:S(2)}) collective-permute-start(bf16[4,192,384]{2,1,0:T(8,128)(2,1)S(1)} %pad_maximum_fusion.1.refs_0_), channel_id=1, source_target_pairs={{0,4},{4,0},{1,5},{5,1},{2,6},{6,2},{3,7},{7,3},{8,12},{12,8},{9,1... | collective-permute-start | bytes 1769480 | tf_op jit(solution)/shard_map/ppermute | solution.py:652
  69.9 15.6 %collective-permute-start.17 = (bf16[128,1536]{1,0:T(8,128)(2,1)}, bf16[128,1536]{1,0:T(8,128)(2,1)}, u32[]{:S(2)}, u32[]{:S(2)}) collective-permute-start(bf16[128,1536]{1,0:T(8,128)(2,1)} %pad_maximum_fusion.2), channel_id=1, source_target_pairs={{0,8},{8,0},{16,24},{24,16},{1,9},{9,1},{17,25},{25,17},{2,10},{10... | collective-permute-start | bytes 1179656 | tf_op jit(solution)/shard_map/ppermute | solution.py:652
  70.5 12.7 %collective-permute-start.16 = (bf16[3,64,560]{2,1,0:T(8,128)(2,1)S(1)}, bf16[3,64,560]{2,1,0:T(8,128)(2,1)S(1)}, u32[]{:S(2)}, u32[]{:S(2)}) collective-permute-start(bf16[3,64,560]{2,1,0:T(8,128)(2,1)S(1)} %copy-done.47), channel_id=1, source_target_pairs={{0,16},{8,24},{16,0},{24,8},{1,17},{9,25},{17,1},{25,9},{2,18},{10... | collective-permute-start | bytes 645128 | tf_op jit(solution)/shard_map/ppermute | solution.py:652
  86.5 20.3 %collective-permute-start.20 = (bf16[3,64,560]{2,1,0:T(8,128)(2,1)S(1)}, bf16[3,64,560]{2,1,0:T(8,128)(2,1)S(1)}, u32[]{:S(2)}, u32[]{:S(2)}) collective-permute-start(bf16[3,64,560]{2,1,0:T(8,128)(2,1)S(1)} %copy-done.45), channel_id=1, source_target_pairs={{0,16},{8,24},{16,0},{24,8},{1,17},{9,25},{17,1},{25,9},{2,18},{10... | collective-permute-start | bytes 645128 | tf_op jit(solution)/shard_map/ppermute | solution.py:652
  87.7 19.9 %collective-permute-start.21 = (bf16[3,192,560]{2,1,0:T(8,128)(2,1)S(1)}, bf16[3,192,560]{2,1,0:T(8,128)(2,1)S(1)}, u32[]{:S(2)}, u32[]{:S(2)}) collective-permute-start(bf16[3,192,560]{2,1,0:T(8,128)(2,1)S(1)} %get-tuple-element.161.refs_0_), channel_id=1, source_target_pairs={{0,4},{4,0},{1,5},{5,1},{2,6},{6,2},{3,7},{7,3},{8,12},{12,8},{9,1... | collective-permute-start | bytes 1935368 | tf_op jit(solution)/shard_map/ppermute | solution.py:652
  87.7 19.9 %collective-permute-start.22 = (bf16[128,1536]{1,0:T(8,128)(2,1)}, bf16[128,1536]{1,0:T(8,128)(2,1)S(1)}, u32[]{:S(2)}, u32[]{:S(2)}) collective-permute-start(bf16[128,1536]{1,0:T(8,128)(2,1)} %pad_maximum_fusion.2), channel_id=1, source_target_pairs={{0,2},{1,3},{2,0},{3,1},{4,6},{5,7},{6,4},{7,5},{8,10},{9,11},{10,... | collective-permute-start | bytes 1179656 | tf_op jit(solution)/shard_map/ppermute | solution.py:652
  88.4 29.6 %collective-permute-start.24 = (bf16[3,192,560]{2,1,0:T(8,128)(2,1)}, bf16[3,192,560]{2,1,0:T(8,128)(2,1)S(1)}, u32[]{:S(2)}, u32[]{:S(2)}) collective-permute-start(bf16[3,192,560]{2,1,0:T(8,128)(2,1)} %get-tuple-element.165), channel_id=1, source_target_pairs={{0,8},{8,0},{16,24},{24,16},{1,9},{9,1},{17,25},{25,17},{2,10},{10... | collective-permute-start | bytes 1935368 | tf_op jit(solution)/shard_map/ppermute | solution.py:652
  89.8 13.5 %collective-permute-start.19 = (bf16[64,1536]{1,0:T(8,128)(2,1)S(1)}, bf16[64,1536]{1,0:T(8,128)(2,1)S(1)}, u32[]{:S(2)}, u32[]{:S(2)}) collective-permute-start(bf16[64,1536]{1,0:T(8,128)(2,1)S(1)} %fusion.41), channel_id=1, source_target_pairs={{0,2},{1,3},{2,0},{3,1},{4,6},{5,7},{6,4},{7,5},{8,10},{9,11},{10,... | collective-permute-start | bytes 589832 | tf_op jit(solution)/shard_map/ppermute | solution.py:652
  103.3 8.2 %collective-permute-start.25 = (bf16[3,64,560]{2,1,0:T(8,128)(2,1)S(1)}, bf16[3,64,560]{2,1,0:T(8,128)(2,1)S(1)}, u32[]{:S(2)}, u32[]{:S(2)}) collective-permute-start(bf16[3,64,560]{2,1,0:T(8,128)(2,1)S(1)} %collective-permute-done.4.refs_2_), channel_id=1, source_target_pairs={{0,4},{4,0},{1,5},{5,1},{2,6},{6,2},{3,7},{7,3},{8,12},{12,8},{9,1... | collective-permute-start | bytes 645128 | tf_op jit(solution)/shard_map/ppermute | solution.py:652
  106.8 11.2 %collective-permute-start.27 = (bf16[128,1536]{1,0:T(8,128)(2,1)}, bf16[128,1536]{1,0:T(8,128)(2,1)S(1)}, u32[]{:S(2)}, u32[]{:S(2)}) collective-permute-start(bf16[128,1536]{1,0:T(8,128)(2,1)} %collective-permute-done.17), channel_id=1, source_target_pairs={{0,2},{1,3},{2,0},{3,1},{4,6},{5,7},{6,4},{7,5},{8,10},{9,11},{10,... | collective-permute-start | bytes 1179656 | tf_op jit(solution)/shard_map/ppermute | solution.py:652
  107.7 10.4 %collective-permute-start.23 = (bf16[64,1536]{1,0:T(8,128)(2,1)S(1)}, bf16[64,1536]{1,0:T(8,128)(2,1)S(1)}, u32[]{:S(2)}, u32[]{:S(2)}) collective-permute-start(bf16[64,1536]{1,0:T(8,128)(2,1)S(1)} %multiply_convert_fusion), channel_id=1, source_target_pairs={{0,16},{8,24},{16,0},{24,8},{1,17},{9,25},{17,1},{25,9},{2,18},{10... | collective-permute-start | bytes 589832 | tf_op jit(solution)/shard_map/ppermute | solution.py:652
  111.5 7.2 %collective-permute-start.26 = (bf16[3,64,560]{2,1,0:T(8,128)(2,1)S(1)}, bf16[3,64,560]{2,1,0:T(8,128)(2,1)S(1)}, u32[]{:S(2)}, u32[]{:S(2)}) collective-permute-start(bf16[3,64,560]{2,1,0:T(8,128)(2,1)S(1)} %copy-done.35), channel_id=1, source_target_pairs={{0,4},{4,0},{1,5},{5,1},{2,6},{6,2},{3,7},{7,3},{8,12},{12,8},{9,1... | collective-permute-start | bytes 645128 | tf_op jit(solution)/shard_map/ppermute | solution.py:652
  118.7 16.2 %collective-permute-start.28 = (bf16[128,1536]{1,0:T(8,128)(2,1)S(1)}, bf16[128,1536]{1,0:T(8,128)(2,1)S(1)}, u32[]{:S(2)}, u32[]{:S(2)}) collective-permute-start(bf16[128,1536]{1,0:T(8,128)(2,1)S(1)} %get-tuple-element.169), channel_id=1, source_target_pairs={{0,8},{8,0},{16,24},{24,16},{1,9},{9,1},{17,25},{25,17},{2,10},{10... | collective-permute-start | bytes 1179656 | tf_op jit(solution)/shard_map/ppermute | solution.py:652
  118.8 18.7 %collective-permute-start.29 = (bf16[128,1536]{1,0:T(8,128)(2,1)S(1)}, bf16[128,1536]{1,0:T(8,128)(2,1)S(1)}, u32[]{:S(2)}, u32[]{:S(2)}) collective-permute-start(bf16[128,1536]{1,0:T(8,128)(2,1)S(1)} %get-tuple-element.169), channel_id=1, source_target_pairs={{0,2},{1,3},{2,0},{3,1},{4,6},{5,7},{6,4},{7,5},{8,10},{9,11},{10,... | collective-permute-start | bytes 1179656 | tf_op jit(solution)/shard_map/ppermute | solution.py:652
  119.6 15.4 %collective-permute-start.30 = (bf16[3,64,560]{2,1,0:T(8,128)(2,1)S(1)}, bf16[3,64,560]{2,1,0:T(8,128)(2,1)S(1)}, u32[]{:S(2)}, u32[]{:S(2)}) collective-permute-start(bf16[3,64,560]{2,1,0:T(8,128)(2,1)S(1)} %copy-done.43), channel_id=1, source_target_pairs={{0,24},{8,16},{16,8},{24,0},{1,25},{9,17},{17,9},{25,1},{2,26},{10... | collective-permute-start | bytes 645128 | tf_op jit(solution)/shard_map/ppermute | solution.py:652
  122.9 20.5 %collective-permute-start.33 = (bf16[3,192,560]{2,1,0:T(8,128)(2,1)S(1)}, bf16[3,192,560]{2,1,0:T(8,128)(2,1)S(1)}, u32[]{:S(2)}, u32[]{:S(2)}) collective-permute-start(bf16[3,192,560]{2,1,0:T(8,128)(2,1)S(1)} %collective-permute-done.24.refs_1_), channel_id=1, source_target_pairs={{0,4},{4,0},{1,5},{5,1},{2,6},{6,2},{3,7},{7,3},{8,12},{12,8},{9,1... | collective-permute-start | bytes 1935368 | tf_op jit(solution)/shard_map/ppermute | solution.py:652
  135.0 8.5 %collective-permute-start.31 = (bf16[128,1536]{1,0:T(8,128)(2,1)S(1)}, bf16[128,1536]{1,0:T(8,128)(2,1)S(1)}, u32[]{:S(2)}, u32[]{:S(2)}) collective-permute-start(bf16[128,1536]{1,0:T(8,128)(2,1)S(1)} %collective-permute-done.28), channel_id=1, source_target_pairs={{0,2},{1,3},{2,0},{3,1},{4,6},{5,7},{6,4},{7,5},{8,10},{9,11},{10,... | collective-permute-start | bytes 1179656 | tf_op jit(solution)/shard_map/ppermute | solution.py:652
  135.7 8.1 %collective-permute-start.32 = (bf16[3,64,560]{2,1,0:T(8,128)(2,1)S(1)}, bf16[3,64,560]{2,1,0:T(8,128)(2,1)S(1)}, u32[]{:S(2)}, u32[]{:S(2)}) collective-permute-start(bf16[3,64,560]{2,1,0:T(8,128)(2,1)S(1)} %copy-done.41), channel_id=1, source_target_pairs={{0,24},{8,16},{16,8},{24,0},{1,25},{9,17},{17,9},{25,1},{2,26},{10... | collective-permute-start | bytes 645128 | tf_op jit(solution)/shard_map/ppermute | solution.py:652
  137.4 32.9 %collective-permute-start.35 = (bf16[512,1536]{1,0:T(8,128)(2,1)S(1)}, bf16[512,1536]{1,0:T(8,128)(2,1)S(1)}, u32[]{:S(2)}, u32[]{:S(2)}) collective-permute-start(bf16[512,1536]{1,0:T(8,128)(2,1)S(1)} %constant_dynamic-update-slice_fusion.9.cot_ref.refs_2_), channel_id=1, source_target_pairs={{0,1},{1,0},{2,3},{3,2},{4,5},{5,4},{6,7},{7,6},{8,9},{9,8},{10,11... | collective-permute-start | bytes 4718600 | tf_op jit(solution)/shard_map/ppermute | solution.py:652
  143.8 26.5 %collective-permute-start.34 = (bf16[512,1536]{1,0:T(8,128)(2,1)S(1)}, bf16[512,1536]{1,0:T(8,128)(2,1)S(1)}, u32[]{:S(2)}, u32[]{:S(2)}) collective-permute-start(bf16[512,1536]{1,0:T(8,128)(2,1)S(1)} %constant_dynamic-update-slice_fusion.4.n2_ref.refs_0_), channel_id=1, source_target_pairs={{0,1},{1,0},{2,3},{3,2},{4,5},{5,4},{6,7},{7,6},{8,9},{9,8},{10,11... | collective-permute-start | bytes 4718600 | tf_op jit(solution)/shard_map/ppermute | solution.py:652
  143.8 8.4 %collective-permute-start.38 = (bf16[3,64,560]{2,1,0:T(8,128)(2,1)S(1)}, bf16[3,64,560]{2,1,0:T(8,128)(2,1)S(1)}, u32[]{:S(2)}, u32[]{:S(2)}) collective-permute-start(bf16[3,64,560]{2,1,0:T(8,128)(2,1)S(1)} %collective-permute-done.30.refs_5_), channel_id=1, source_target_pairs={{0,4},{4,0},{1,5},{5,1},{2,6},{6,2},{3,7},{7,3},{8,12},{12,8},{9,1... | collective-permute-start | bytes 645128 | tf_op jit(solution)/shard_map/ppermute | solution.py:652
  152.2 8.9 %collective-permute-start.39 = (bf16[3,64,560]{2,1,0:T(8,128)(2,1)S(1)}, bf16[3,64,560]{2,1,0:T(8,128)(2,1)S(1)}, u32[]{:S(2)}, u32[]{:S(2)}) collective-permute-start(bf16[3,64,560]{2,1,0:T(8,128)(2,1)S(1)} %collective-permute-done.32.refs_6_), channel_id=1, source_target_pairs={{0,4},{4,0},{1,5},{5,1},{2,6},{6,2},{3,7},{7,3},{8,12},{12,8},{9,1... | collective-permute-start | bytes 645128 | tf_op jit(solution)/shard_map/ppermute | solution.py:652
  152.5 9.3 %collective-permute-start.36 = (bf16[3,64,560]{2,1,0:T(8,128)(2,1)S(1)}, bf16[3,64,560]{2,1,0:T(8,128)(2,1)S(1)}, u32[]{:S(2)}, u32[]{:S(2)}) collective-permute-start(bf16[3,64,560]{2,1,0:T(8,128)(2,1)S(1)} %copy-done.39), channel_id=1, source_target_pairs={{0,24},{8,16},{16,8},{24,0},{1,25},{9,17},{17,9},{25,1},{2,26},{10... | collective-permute-start | bytes 645128 | tf_op jit(solution)/shard_map/ppermute | solution.py:652
  154.3 12.0 %collective-permute-start.37 = (bf16[3,64,560]{2,1,0:T(8,128)(2,1)S(1)}, bf16[3,64,560]{2,1,0:T(8,128)(2,1)S(1)}, u32[]{:S(2)}, u32[]{:S(2)}) collective-permute-start(bf16[3,64,560]{2,1,0:T(8,128)(2,1)S(1)} %collective-permute-done.20.refs_4_), channel_id=1, source_target_pairs={{0,4},{4,0},{1,5},{5,1},{2,6},{6,2},{3,7},{7,3},{8,12},{12,8},{9,1... | collective-permute-start | bytes 645128 | tf_op jit(solution)/shard_map/ppermute | solution.py:652
  161.8 8.5 %collective-permute-start.40 = (bf16[3,64,560]{2,1,0:T(8,128)(2,1)S(1)}, bf16[3,64,560]{2,1,0:T(8,128)(2,1)S(1)}, u32[]{:S(2)}, u32[]{:S(2)}) collective-permute-start(bf16[3,64,560]{2,1,0:T(8,128)(2,1)S(1)} %collective-permute-done.36.refs_7_), channel_id=1, source_target_pairs={{0,4},{4,0},{1,5},{5,1},{2,6},{6,2},{3,7},{7,3},{8,12},{12,8},{9,1... | collective-permute-start | bytes 645128 | tf_op jit(solution)/shard_map/ppermute | solution.py:652
  180.0 14.0 %collective-permute-start.41 = (bf16[512,1536]{1,0:T(8,128)(2,1)S(1)}, bf16[512,1536]{1,0:T(8,128)(2,1)S(1)}, u32[]{:S(2)}, u32[]{:S(2)}) collective-permute-start(bf16[512,1536]{1,0:T(8,128)(2,1)S(1)} %get-tuple-element.189), channel_id=1, source_target_pairs={{0,1},{1,0},{2,3},{3,2},{4,5},{5,4},{6,7},{7,6},{8,9},{9,8},{10,11... | collective-permute-start | bytes 4718600 | tf_op jit(solution)/shard_map/ppermute | solution.py:652
  196.3 19.4 %collective-permute-start.43 = (bf16[128,1536]{1,0:T(8,128)(2,1)}, bf16[128,1536]{1,0:T(8,128)(2,1)}, u32[]{:S(2)}, u32[]{:S(2)}) collective-permute-start(bf16[128,1536]{1,0:T(8,128)(2,1)} %get-tuple-element.271), channel_id=1, source_target_pairs={{0,2},{1,3},{2,0},{3,1},{4,6},{5,7},{6,4},{7,5},{8,10},{9,11},{10,... | collective-permute-start | bytes 1179656 | tf_op jit(solution)/shard_map/ppermute | solution.py:652
  215.0 12.9 %collective-permute-start.42 = (bf16[128,1536]{1,0:T(8,128)(2,1)S(1)}, bf16[128,1536]{1,0:T(8,128)(2,1)S(1)}, u32[]{:S(2)}, u32[]{:S(2)}) collective-permute-start(bf16[128,1536]{1,0:T(8,128)(2,1)S(1)} %copy-done.77), channel_id=1, source_target_pairs={{0,2},{1,3},{2,0},{3,1},{4,6},{5,7},{6,4},{7,5},{8,10},{9,11},{10,... | collective-permute-start | bytes 1179656 | tf_op jit(solution)/shard_map/ppermute | solution.py:652
  216.9 12.7 %collective-permute-start.44 = (bf16[128,1536]{1,0:T(8,128)(2,1)S(1)}, bf16[128,1536]{1,0:T(8,128)(2,1)S(1)}, u32[]{:S(2)}, u32[]{:S(2)}) collective-permute-start(bf16[128,1536]{1,0:T(8,128)(2,1)S(1)} %add_convert_fusion.5), channel_id=1, source_target_pairs={{0,8},{8,0},{16,24},{24,16},{1,9},{9,1},{17,25},{25,17},{2,10},{10... | collective-permute-start | bytes 1179656 | tf_op jit(solution)/shard_map/ppermute | solution.py:652
  221.0 18.1 %collective-permute-start.46 = (bf16[3,192,560]{2,1,0:T(8,128)(2,1)S(1)}, bf16[3,192,560]{2,1,0:T(8,128)(2,1)S(1)}, u32[]{:S(2)}, u32[]{:S(2)}) collective-permute-start(bf16[3,192,560]{2,1,0:T(8,128)(2,1)S(1)} %get-tuple-element.203), channel_id=1, source_target_pairs={{0,4},{4,0},{1,5},{5,1},{2,6},{6,2},{3,7},{7,3},{8,12},{12,8},{9,1... | collective-permute-start | bytes 1935368 | tf_op jit(solution)/shard_map/ppermute | solution.py:652
  229.9 11.4 %collective-permute-start.45 = (bf16[64,1536]{1,0:T(8,128)(2,1)S(1)}, bf16[64,1536]{1,0:T(8,128)(2,1)S(1)}, u32[]{:S(2)}, u32[]{:S(2)}) collective-permute-start(bf16[64,1536]{1,0:T(8,128)(2,1)S(1)} %slice.437), channel_id=1, source_target_pairs={{0,16},{8,24},{16,0},{24,8},{1,17},{9,25},{17,1},{25,9},{2,18},{10... | collective-permute-start | bytes 589832 | tf_op jit(solution)/shard_map/ppermute | solution.py:652
  239.1 17.1 %collective-permute-start.50 = (bf16[3,192,560]{2,1,0:T(8,128)(2,1)S(1)}, bf16[3,192,560]{2,1,0:T(8,128)(2,1)S(1)}, u32[]{:S(2)}, u32[]{:S(2)}) collective-permute-start(bf16[3,192,560]{2,1,0:T(8,128)(2,1)S(1)} %get-tuple-element.209), channel_id=1, source_target_pairs={{0,4},{4,0},{1,5},{5,1},{2,6},{6,2},{3,7},{7,3},{8,12},{12,8},{9,1... | collective-permute-start | bytes 1935368 | tf_op jit(solution)/shard_map/ppermute | solution.py:652
  248.4 10.5 %collective-permute-start.48 = (bf16[2,64,1536]{2,1,0:T(8,128)(2,1)S(1)}, bf16[2,64,1536]{2,1,0:T(8,128)(2,1)S(1)}, u32[]{:S(2)}, u32[]{:S(2)}) collective-permute-start(bf16[2,64,1536]{2,1,0:T(8,128)(2,1)S(1)} %maximum_select_fusion.4), channel_id=1, source_target_pairs={{0,1},{1,0},{2,3},{3,2},{4,5},{5,4},{6,7},{7,6},{8,9},{9,8},{10,11... | collective-permute-start | bytes 1179656 | tf_op jit(solution)/shard_map/ppermute | solution.py:652
  256.3 27.3 %collective-permute-start.61 = (bf16[3,192,560]{2,1,0:T(8,128)(2,1)}, bf16[3,192,560]{2,1,0:T(8,128)(2,1)}, u32[]{:S(2)}, u32[]{:S(2)}) collective-permute-start(bf16[3,192,560]{2,1,0:T(8,128)(2,1)} %get-tuple-element.222), channel_id=1, source_target_pairs={{0,4},{4,0},{1,5},{5,1},{2,6},{6,2},{3,7},{7,3},{8,12},{12,8},{9,1... | collective-permute-start | bytes 1935368 | tf_op jit(solution)/shard_map/ppermute | solution.py:652
  257.7 28.0 %collective-permute-start.62 = (bf16[3,192,560]{2,1,0:T(8,128)(2,1)}, bf16[3,192,560]{2,1,0:T(8,128)(2,1)S(1)}, u32[]{:S(2)}, u32[]{:S(2)}) collective-permute-start(bf16[3,192,560]{2,1,0:T(8,128)(2,1)} %add_convert_fusion.3), channel_id=1, source_target_pairs={{0,24},{8,16},{16,8},{24,0},{1,25},{9,17},{17,9},{25,1},{2,26},{10... | collective-permute-start | bytes 1935368 | tf_op jit(solution)/shard_map/ppermute | solution.py:652
  265.3 10.2 %collective-permute-start.55 = (f32[256,128]{1,0:T(8,128)S(1)}, f32[256,128]{1,0:T(8,128)S(1)}, u32[]{:S(2)}, u32[]{:S(2)}) collective-permute-start(f32[256,128]{1,0:T(8,128)S(1)} %slice.319), channel_id=1, source_target_pairs={{4,0},{5,1},{6,2},{7,3},{12,8},{13,9},{14,10},{15,11},{20,16},{21,... | collective-permute-start | bytes 393224 | tf_op jit(solution)/shard_map/ppermute | solution.py:652
  282.6 11.7 %collective-permute-start.56 = (bf16[2,64,1536]{2,1,0:T(8,128)(2,1)}, bf16[2,64,1536]{2,1,0:T(8,128)(2,1)}, u32[]{:S(2)}, u32[]{:S(2)}) collective-permute-start(bf16[2,64,1536]{2,1,0:T(8,128)(2,1)} %fusion.31), channel_id=1, source_target_pairs={{0,1},{1,0},{2,3},{3,2},{4,5},{5,4},{6,7},{7,6},{8,9},{9,8},{10,11... | collective-permute-start | bytes 1179656 | tf_op jit(solution)/shard_map/ppermute | solution.py:652
  285.8 87.6 %collective-permute-start.67 = (bf16[3,192,560]{2,1,0:T(8,128)(2,1)}, bf16[3,192,560]{2,1,0:T(8,128)(2,1)S(1)}, u32[]{:S(2)}, u32[]{:S(2)}) collective-permute-start(bf16[3,192,560]{2,1,0:T(8,128)(2,1)} %add_convert_fusion.1), channel_id=1, source_target_pairs={{0,16},{8,24},{16,0},{24,8},{1,17},{9,25},{17,1},{25,9},{2,18},{10... | collective-permute-start | bytes 1935368 | tf_op jit(solution)/shard_map/ppermute | solution.py:652
  293.4 12.1 %collective-permute-start.60 = (bf16[2,192,512]{2,1,0:T(8,128)(2,1)}, bf16[2,192,512]{2,1,0:T(8,128)(2,1)}, u32[]{:S(2)}, u32[]{:S(2)}) collective-permute-start(bf16[2,192,512]{2,1,0:T(8,128)(2,1)} %get-tuple-element.218), channel_id=1, source_target_pairs={{0,4},{4,0},{1,5},{5,1},{2,6},{6,2},{3,7},{7,3},{8,12},{12,8},{9,1... | collective-permute-start | bytes 1179656 | tf_op jit(solution)/shard_map/ppermute | solution.py:652
  296.3 6.4 %collective-permute-start.57 = (bf16[64,1536]{1,0:T(8,128)(2,1)}, bf16[64,1536]{1,0:T(8,128)(2,1)}, u32[]{:S(2)}, u32[]{:S(2)}) collective-permute-start(bf16[64,1536]{1,0:T(8,128)(2,1)} %fusion.42), channel_id=1, source_target_pairs={{0,2},{1,3},{2,0},{3,1},{4,6},{5,7},{6,4},{7,5},{8,10},{9,11},{10,... | collective-permute-start | bytes 589832 | tf_op jit(solution)/shard_map/ppermute | solution.py:652
  299.8 11.7 %collective-permute-start.63 = (bf16[2,192,512]{2,1,0:T(8,128)(2,1)}, bf16[2,192,512]{2,1,0:T(8,128)(2,1)}, u32[]{:S(2)}, u32[]{:S(2)}) collective-permute-start(bf16[2,192,512]{2,1,0:T(8,128)(2,1)} %get-tuple-element.225), channel_id=1, source_target_pairs={{0,4},{4,0},{1,5},{5,1},{2,6},{6,2},{3,7},{7,3},{8,12},{12,8},{9,1... | collective-permute-start | bytes 1179656 | tf_op jit(solution)/shard_map/ppermute | solution.py:652
  306.9 29.3 %collective-permute-start.52 = (bf16[256,1536]{1,0:T(8,128)(2,1)S(1)}, bf16[256,1536]{1,0:T(8,128)(2,1)S(1)}, u32[]{:S(2)}, u32[]{:S(2)}) collective-permute-start(bf16[256,1536]{1,0:T(8,128)(2,1)S(1)} %pad_maximum_fusion), channel_id=1, source_target_pairs={{0,2},{1,3},{2,0},{3,1},{4,6},{5,7},{6,4},{7,5},{8,10},{9,11},{10,... | collective-permute-start | bytes 2359304 | tf_op jit(solution)/shard_map/ppermute | solution.py:652
  307.8 30.4 %collective-permute-start.64 = (bf16[3,192,560]{2,1,0:T(8,128)(2,1)}, bf16[3,192,560]{2,1,0:T(8,128)(2,1)S(1)}, u32[]{:S(2)}, u32[]{:S(2)}) collective-permute-start(bf16[3,192,560]{2,1,0:T(8,128)(2,1)} %add_convert_fusion.2), channel_id=1, source_target_pairs={{0,8},{8,0},{16,24},{24,16},{1,9},{9,1},{17,25},{25,17},{2,10},{10... | collective-permute-start | bytes 1935368 | tf_op jit(solution)/shard_map/ppermute | solution.py:652
  308.5 34.5 %collective-permute-start.75 = (bf16[4,192,384]{2,1,0:T(8,128)(2,1)}, bf16[4,192,384]{2,1,0:T(8,128)(2,1)S(1)}, u32[]{:S(2)}, u32[]{:S(2)}) collective-permute-start(bf16[4,192,384]{2,1,0:T(8,128)(2,1)} %get-tuple-element.236), channel_id=1, source_target_pairs={{0,4},{4,0},{1,5},{5,1},{2,6},{6,2},{3,7},{7,3},{8,12},{12,8},{9,1... | collective-permute-start | bytes 1769480 | tf_op jit(solution)/shard_map/ppermute | solution.py:652
  311.5 15.9 %collective-permute-start.71 = (f32[40,128]{1,0:T(8,128)S(1)}, f32[40,128]{1,0:T(8,128)S(1)}, u32[]{:S(2)}, u32[]{:S(2)}) collective-permute-start(f32[40,128]{1,0:T(8,128)S(1)} %fusion.115), channel_id=1, source_target_pairs={{0,2},{1,3},{2,0},{3,1},{4,6},{5,7},{6,4},{7,5},{8,10},{9,11},{10,... | collective-permute-start | bytes 61448 | tf_op jit(solution)/shard_map/ppermute | solution.py:652
  336.4 21.7 %collective-permute-start.53 = (bf16[128,1536]{1,0:T(8,128)(2,1)S(1)}, bf16[128,1536]{1,0:T(8,128)(2,1)S(1)}, u32[]{:S(2)}, u32[]{:S(2)}) collective-permute-start(bf16[128,1536]{1,0:T(8,128)(2,1)S(1)} %fusion.19), channel_id=1, source_target_pairs={{0,8},{8,0},{16,24},{24,16},{1,9},{9,1},{17,25},{25,17},{2,10},{10... | collective-permute-start | bytes 1179656 | tf_op jit(solution)/shard_map/ppermute | solution.py:652
  338.2 18.7 %collective-permute-start.65 = (bf16[2,192,512]{2,1,0:T(8,128)(2,1)S(1)}, bf16[2,192,512]{2,1,0:T(8,128)(2,1)S(1)}, u32[]{:S(2)}, u32[]{:S(2)}) collective-permute-start(bf16[2,192,512]{2,1,0:T(8,128)(2,1)S(1)} %add_convert_fusion.4), channel_id=1, source_target_pairs={{0,8},{8,0},{16,24},{24,16},{1,9},{9,1},{17,25},{25,17},{2,10},{10... | collective-permute-start | bytes 1179656 | tf_op jit(solution)/shard_map/ppermute | solution.py:652
  343.1 34.6 %collective-permute-start.76 = (bf16[2,192,384]{2,1,0:T(8,128)(2,1)S(1)}, bf16[2,192,384]{2,1,0:T(8,128)(2,1)S(1)}, u32[]{:S(2)}, u32[]{:S(2)}) collective-permute-start(bf16[2,192,384]{2,1,0:T(8,128)(2,1)S(1)} %add_convert_fusion.8), channel_id=1, source_target_pairs={{0,8},{8,0},{16,24},{24,16},{1,9},{9,1},{17,25},{25,17},{2,10},{10... | collective-permute-start | bytes 884744 | tf_op jit(solution)/shard_map/ppermute | solution.py:652
  343.3 44.9 %collective-permute-start.78 = (bf16[3,192,560]{2,1,0:T(8,128)(2,1)S(1)}, bf16[3,192,560]{2,1,0:T(8,128)(2,1)S(1)}, u32[]{:S(2)}, u32[]{:S(2)}) collective-permute-start(bf16[3,192,560]{2,1,0:T(8,128)(2,1)S(1)} %copy-done.37), channel_id=1, source_target_pairs={{0,4},{4,0},{1,5},{5,1},{2,6},{6,2},{3,7},{7,3},{8,12},{12,8},{9,1... | collective-permute-start | bytes 1935368 | tf_op jit(solution)/shard_map/ppermute | solution.py:652
  358.1 15.2 %collective-permute-start.66 = (bf16[1,192,512]{2,1,0:T(8,128)(2,1)S(1)}, bf16[1,192,512]{2,1,0:T(8,128)(2,1)S(1)}, u32[]{:S(2)}, u32[]{:S(2)}) collective-permute-start(bf16[1,192,512]{2,1,0:T(8,128)(2,1)S(1)} %slice.435), channel_id=1, source_target_pairs={{0,16},{8,24},{16,0},{24,8},{1,17},{9,25},{17,1},{25,9},{2,18},{10... | collective-permute-start | bytes 589832 | tf_op jit(solution)/shard_map/ppermute | solution.py:652
  361.0 14.4 %collective-permute-start.54 = (bf16[64,1536]{1,0:T(8,128)(2,1)S(1)}, bf16[64,1536]{1,0:T(8,128)(2,1)S(1)}, u32[]{:S(2)}, u32[]{:S(2)}) collective-permute-start(bf16[64,1536]{1,0:T(8,128)(2,1)S(1)} %slice.436), channel_id=1, source_target_pairs={{0,16},{8,24},{16,0},{24,8},{1,17},{9,25},{17,1},{25,9},{2,18},{10... | collective-permute-start | bytes 589832 | tf_op jit(solution)/shard_map/ppermute | solution.py:652
  376.3 9.3 %collective-permute-start.58 = (bf16[64,3072]{1,0:T(8,128)(2,1)S(1)}, bf16[64,3072]{1,0:T(8,128)(2,1)S(1)}, u32[]{:S(2)}, u32[]{:S(2)}) collective-permute-start(bf16[64,3072]{1,0:T(8,128)(2,1)S(1)} %pad_maximum_fusion.3), channel_id=1, source_target_pairs={{0,2},{1,3},{2,0},{3,1},{4,6},{5,7},{6,4},{7,5},{8,10},{9,11},{10,... | collective-permute-start | bytes 1179656 | tf_op jit(solution)/shard_map/ppermute | solution.py:652
  377.8 9.6 %collective-permute-start.77 = (bf16[1,192,384]{2,1,0:T(8,128)(2,1)S(1)}, bf16[1,192,384]{2,1,0:T(8,128)(2,1)S(1)}, u32[]{:S(2)}, u32[]{:S(2)}) collective-permute-start(bf16[1,192,384]{2,1,0:T(8,128)(2,1)S(1)} %slice.438), channel_id=1, source_target_pairs={{0,16},{8,24},{16,0},{24,8},{1,17},{9,25},{17,1},{25,9},{2,18},{10... | collective-permute-start | bytes 442376 | tf_op jit(solution)/shard_map/ppermute | solution.py:652
  (105 other events, 987.0 us)

commit v3 on v2

--- a/solution.py
+++ b/solution.py
@@ -175,10 +175,9 @@
     (QUERY, XB): [(O_ALL, (Z, 2))],
     (W_Z, (2, 0)): [(QUERY, (Z, 1))],
     (O_ALL, (Z, 1)): [(QUERY, (Z, 1))],
-    PROJECT: [(W_Z, (2, 0)), (O_ALL, (Z, 1))],
+    PROJECT: [(O_ALL, (Z, 1))],
     (COT, (Z, 2)): [(QUERY, XB)],
     (O_ALL, X): [(QUERY, XB)],
-    KV_ACT_C: [(COT, (Z, 2))],
     (W_Z, (2, 1)): [KV_ACT_X],
     (COT, (Z, 1)): [KV_ACT_X],
     (W_X, (2, 0)): [BRANCH_Y],
@@ -232,6 +231,7 @@
     (G_X, 0): [(OUT, X)],
     (OUT, GRAD): [KV_GRAD_C],
     KV_DONE_Y: [(G_Z, 2)],
+    HEADS: [(W_Z, (2, 0))],
 }
 
 

time: 400 us -> 395 us (0.988)
  waiting for transfers between devices: 171 us -> 160 us
  starting transfers between devices: 81.6 us -> 88.8 us
    ppermute x79, waiting for transfers between devices: 171 us -> 160 us  [move(): makers[name] = lambda: lax.ppermute(tied(name, maker()), *links[link])]
    ppermute x79, starting transfers between devices: 81.6 us -> 88.8 us  [move(): makers[name] = lambda: lax.ppermute(tied(name, maker()), *links[link])]
    unnamed x189 -> x197, local copies, waits for them, and re-layouts: 27.3 us -> 27.5 us
  transfers between devices with their start and end apart: 79 -> 79, of which waited for: 42 -> 40; matrix products, arithmetic and copies ran while one was open for 16% -> 15% of each run, Pallas kernels for 9% -> 11%
where the time goes in v3:
time: 395 us; the launch traced here: 390 us
  waiting for transfers between devices  160 us (41%)
  starting transfers between devices  88.8 us (22%)
  Pallas kernels  51.4 us (13%)
  other arithmetic  41 us (10%)
  local copies, waits for them, and re-layouts  36.6 us (9%)
  matrix products  9.85 us (2%)
    ppermute x79, waiting for transfers between devices, move(): makers[name] = lambda: lax.ppermute(tied(name, maker()), *links[link])  160 us
    ppermute x79, starting transfers between devices, move(): makers[name] = lambda: lax.ppermute(tied(name, maker()), *links[link])  88.8 us
    unnamed x197, local copies, waits for them, and re-layouts  27.5 us
    pallas_call x2, Pallas kernels, weight_grads(): pl.pallas_call(kernel, cost_estimate=CHEAP, out_shape=[jax.ShapeDtypeStru...  9.47 us
  transfers between devices with their start and end apart: 79, of which 40 were waited for; matrix products, arithmetic and copies ran while one was open for 15% of the time, Pallas kernels for 11%

profile of v3, /device:TPU:0, one launch (start us, length us, event | category | flops | bytes accessed | tf_op | source)
XLA Modules:
  0.0 389.7 jit_solution(17710667311920710331)
XLA Ops:
  0.7 4.1 %collective-permute-start = (bf16[1,192,384]{2,1,0:T(8,128)(2,1)}, bf16[1,192,384]{2,1,0:T(8,128)(2,1)}, u32[]{:S(2)}, u32[]{:S(2)}) collective-permute-start(bf16[1,192,384]{2,1,0:T(8,128)(2,1)} %bitcast.158), channel_id=1, source_target_pairs={{0,16},{8,24},{16,0},{24,8},{1,17},{9,25},{17,1},{25,9},{2,18},{10... | collective-permute-start | bytes 442376 | tf_op jit(solution)/shard_map/ppermute | solution.py:652
  7.7 1.6 constant_dynamic-update-slice_fusion.13
  14.9 2.0 shard_map.267
  17.0 2.2 collective-permute-done.6
  21.4 1.8 collective-permute-start.2
  25.6 2.4 collective-permute-done.7
  30.4 1.7 collective-permute-done.1
  34.1 2.2 collective-permute-start.3
  40.1 2.0 shard_map.264
  42.2 2.3 collective-permute-done.3
  44.4 2.5 shard_map.265.w_ref
  47.0 3.7 shard_map.266
  50.7 4.7 %collective-permute-start.11 = (bf16[256,128]{1,0:T(8,128)(2,1)}, bf16[256,128]{1,0:T(8,128)(2,1)S(1)}, u32[]{:S(2)}, u32[]{:S(2)}) collective-permute-start(bf16[256,128]{1,0:T(8,128)(2,1)} %get-tuple-element.143), channel_id=1, source_target_pairs={{0,4},{1,5},{2,6},{3,7},{8,12},{9,13},{10,14},{11,15},{16,20},{17,... | collective-permute-start | bytes 196616 | tf_op jit(solution)/shard_map/ppermute | solution.py:652
  55.4 2.6 collective-permute-start.16
  59.2 5.1 %collective-permute-done.16 = bf16[64,1536]{1,0:T(8,128)(2,1)S(1)} collective-permute-done((bf16[64,1536]{1,0:T(8,128)(2,1)S(1)}, bf16[64,1536]{1,0:T(8,128)(2,1)S(1)}, u32[]{:S(2)}, u32[]{:S(2)}) %collective-permute-start.16) | collective-permute-done | bytes 196640 | tf_op jit(solution)/shard_map/ppermute | solution.py:652
  65.8 3.5 collective-permute-start.15
  71.0 2.5 shard_map.268.o_ref
  73.6 4.8 %shard_map.269 = (bf16[256,384]{1,0:T(8,128)(2,1)}, f32[256,3]{1,0:T(8,128)}, f32[2,64,1536]{2,1,0:T(8,128)}, bf16[2,64,1536]{2,1,0:T(8,128)(2,1)}) custom-call(bf16[256,384]{1,0:T(8,128)(2,1)} %get-tuple-element.142.q_ref, bf16[512,128]{1,0:T(8,128)(2,1)} %copy-done.68, bf16[512,128]{1,0:T(8,128)(2,1)} %copy-done.80, f32[256,512]{1,0:T(8,128)} %add_select_fusion.mask_ref, ...), custom_call_target="tpu_custom_call" | custom-call | tf_op jit(solution)/shard_map/pallas_call | solution.py:422
  78.4 2.8 collective-permute-done.15.refs_3_
  83.9 2.5 collective-permute-start.24
  89.5 8.9 %collective-permute-done.19 = bf16[64,1536]{1,0:T(8,128)(2,1)S(1)} collective-permute-done((bf16[64,1536]{1,0:T(8,128)(2,1)S(1)}, bf16[64,1536]{1,0:T(8,128)(2,1)S(1)}, u32[]{:S(2)}, u32[]{:S(2)}) %collective-permute-start.19) | collective-permute-done | bytes 196640 | tf_op jit(solution)/shard_map/ppermute | solution.py:652
  98.3 1.7 collective-permute-start.25
  103.4 2.6 collective-permute-start.23
  107.2 6.9 %collective-permute-done.23 = bf16[64,1536]{1,0:T(8,128)(2,1)S(1)} collective-permute-done((bf16[64,1536]{1,0:T(8,128)(2,1)S(1)}, bf16[64,1536]{1,0:T(8,128)(2,1)S(1)}, u32[]{:S(2)}, u32[]{:S(2)}) %collective-permute-start.23) | collective-permute-done | bytes 196640 | tf_op jit(solution)/shard_map/ppermute | solution.py:652
  114.2 1.8 collective-permute-start.28
  117.6 1.7 collective-permute-start.30
  119.6 10.8 %collective-permute-done.30.refs_5_ = bf16[3,64,560]{2,1,0:T(8,128)(2,1)S(1)} collective-permute-done((bf16[3,64,560]{2,1,0:T(8,128)(2,1)S(1)}, bf16[3,64,560]{2,1,0:T(8,128)(2,1)S(1)}, u32[]{:S(2)}, u32[]{:S(2)}) %collective-permute-start.30) | collective-permute-done | bytes 215072 | tf_op jit(solution)/shard_map/ppermute | solution.py:652
  132.0 2.1 collective-permute-start.32
  134.2 4.7 %collective-permute-done.31 = bf16[128,1536]{1,0:T(8,128)(2,1)S(1)} collective-permute-done((bf16[128,1536]{1,0:T(8,128)(2,1)S(1)}, bf16[128,1536]{1,0:T(8,128)(2,1)S(1)}, u32[]{:S(2)}, u32[]{:S(2)}) %collective-permute-start.31) | collective-permute-done | bytes 393248 | tf_op jit(solution)/shard_map/ppermute | solution.py:652
  140.2 8.2 %collective-permute-done.38.refs_13_ = bf16[3,64,560]{2,1,0:T(8,128)(2,1)S(1)} collective-permute-done((bf16[3,64,560]{2,1,0:T(8,128)(2,1)S(1)}, bf16[3,64,560]{2,1,0:T(8,128)(2,1)S(1)}, u32[]{:S(2)}, u32[]{:S(2)}) %collective-permute-start.38) | collective-permute-done | bytes 215072 | tf_op jit(solution)/shard_map/ppermute | solution.py:652
  148.7 2.1 collective-permute-start.36
  150.8 1.7 collective-permute-start.37
  152.5 4.8 %collective-permute-done.39.refs_14_ = bf16[3,64,560]{2,1,0:T(8,128)(2,1)S(1)} collective-permute-done((bf16[3,64,560]{2,1,0:T(8,128)(2,1)S(1)}, bf16[3,64,560]{2,1,0:T(8,128)(2,1)S(1)}, u32[]{:S(2)}, u32[]{:S(2)}) %collective-permute-start.39) | collective-permute-done | bytes 215072 | tf_op jit(solution)/shard_map/ppermute | solution.py:652
  158.0 1.7 collective-permute-start.40
  159.7 2.9 collective-permute-done.37.refs_12_
  162.6 4.0 %collective-permute-done.40.refs_15_ = bf16[3,64,560]{2,1,0:T(8,128)(2,1)S(1)} collective-permute-done((bf16[3,64,560]{2,1,0:T(8,128)(2,1)S(1)}, bf16[3,64,560]{2,1,0:T(8,128)(2,1)S(1)}, u32[]{:S(2)}, u32[]{:S(2)}) %collective-permute-start.40) | collective-permute-done | bytes 215072 | tf_op jit(solution)/shard_map/ppermute | solution.py:652
  166.6 7.1 %shard_map.270 = (bf16[1536,560]{1,0:T(8,128)(2,1)}, bf16[1536,560]{1,0:T(8,128)(2,1)}, bf16[1536,560]{1,0:T(8,128)(2,1)}, bf16[512,560]{1,0:T(8,128)(2,1)S(1)},...) custom-call(bf16[512,1536]{1,0:T(8,128)(2,1)S(1)} %collective-permute-done.34.n2_ref.refs_, ...), custom_call_target="tpu_custom_call" | custom-call | tf_op jit(solution)/shard_map/pallas_call | solution.py:498
  180.9 6.8 %shard_map.271 = (bf16[512,560]{1,0:T(8,128)(2,1)S(1)}, bf16[512,560]{1,0:T(8,128)(2,1)S(1)}, bf16[512,560]{1,0:T(8,128)(2,1)S(1)}, f32[512,1536]{1,0:T(8,128)S(1)}) custom-call(bf16[512,1536]{1,0:T(8,128)(2,1)S(1)} %constant_dynamic-update-slice_fusion.4.n2_ref.refs_0_, bf16[512,1536]{1,0:T(8,128)(2,1)S(1)} %constant_dynamic-update-slice_fusion.9.cot_ref.refs_2_, ...), custom_call_target="tpu_custom_call" | custom-call | tf_op jit(solution)/shard_map/pallas_call | solution.py:515
  206.3 4.2 %shard_map.272 = (bf16[3,192,560]{2,1,0:T(8,128)(2,1)S(1)}, bf16[3,192,560]{2,1,0:T(8,128)(2,1)S(1)}, bf16[3,192,560]{2,1,0:T(8,128)(2,1)S(1)}, bf16[3,192,560]{2,1,0:T(8,128)(2,1)S(1)}) custom-call(bf16[512,1536]{1,0:T(8,128)(2,1)S(1)} %constant_dynamic-update-slice_fusion.4.n2_ref.refs_0_, bf16[512,1536]{1,0:T(8,128)(2,1)S(1)} %copy-done.3, ...), custom_call_target="tpu_custom_call" | custom-call | tf_op jit(solution)/shard_map/pallas_call | solution.py:557
  213.3 2.4 collective-permute-start.44
  217.8 5.3 %shard_map.273 = (bf16[3,192,560]{2,1,0:T(8,128)(2,1)S(1)}, bf16[3,192,560]{2,1,0:T(8,128)(2,1)S(1)}, bf16[3,192,560]{2,1,0:T(8,128)(2,1)S(1)}, bf16[3,192,560]{2,1,0:T(8,128)(2,1)}) custom-call(bf16[512,1536]{1,0:T(8,128)(2,1)S(1)} %constant_dynamic-update-slice_fusion.4.n2_ref.refs_0_, bf16[512,1536]{1,0:T(8,128)(2,1)S(1)} %copy-done.3, ...), custom_call_target="tpu_custom_call" | custom-call | tf_op jit(solution)/shard_map/pallas_call | solution.py:557
  223.1 1.8 collective-permute-done.44
  225.2 1.8 collective-permute-start.45
  227.2 7.1 %collective-permute-done.46 = bf16[3,192,560]{2,1,0:T(8,128)(2,1)S(1)} collective-permute-done((bf16[3,192,560]{2,1,0:T(8,128)(2,1)S(1)}, bf16[3,192,560]{2,1,0:T(8,128)(2,1)S(1)}, u32[]{:S(2)}, u32[]{:S(2)}) %collective-permute-start.46) | collective-permute-done | bytes 645152 | tf_op jit(solution)/shard_map/ppermute | solution.py:652
  238.6 3.1 fusion.86
  244.8 6.7 %collective-permute-done.50 = bf16[3,192,560]{2,1,0:T(8,128)(2,1)S(1)} collective-permute-done((bf16[3,192,560]{2,1,0:T(8,128)(2,1)S(1)}, bf16[3,192,560]{2,1,0:T(8,128)(2,1)S(1)}, u32[]{:S(2)}, u32[]{:S(2)}) %collective-permute-start.50) | collective-permute-done | bytes 645152 | tf_op jit(solution)/shard_map/ppermute | solution.py:652
  263.4 7.4 %collective-permute-done.55 = f32[256,128]{1,0:T(8,128)S(1)} collective-permute-done((f32[256,128]{1,0:T(8,128)S(1)}, f32[256,128]{1,0:T(8,128)S(1)}, u32[]{:S(2)}, u32[]{:S(2)}) %collective-permute-start.55) | collective-permute-done | bytes 131104 | tf_op jit(solution)/shard_map/ppermute | solution.py:652
  274.8 3.0 shard_map.274
  278.9 2.2 add_convert_fusion.2
  281.1 4.8 %collective-permute-start.67 = (bf16[3,192,560]{2,1,0:T(8,128)(2,1)}, bf16[3,192,560]{2,1,0:T(8,128)(2,1)S(1)}, u32[]{:S(2)}, u32[]{:S(2)}) collective-permute-start(bf16[3,192,560]{2,1,0:T(8,128)(2,1)} %add_convert_fusion.1), channel_id=1, source_target_pairs={{0,16},{8,24},{16,0},{24,8},{1,17},{9,25},{17,1},{25,9},{2,18},{10... | collective-permute-start | bytes 1935368 | tf_op jit(solution)/shard_map/ppermute | solution.py:652
  285.9 2.9 shard_map.275
  292.6 2.6 fusion.21
  303.7 3.1 collective-permute-done.63
  309.5 13.1 %collective-permute-done.71 = f32[40,128]{1,0:T(8,128)S(1)} collective-permute-done((f32[40,128]{1,0:T(8,128)S(1)}, f32[40,128]{1,0:T(8,128)S(1)}, u32[]{:S(2)}, u32[]{:S(2)}) %collective-permute-start.71) | collective-permute-done | bytes 20512 | tf_op jit(solution)/shard_map/ppermute | solution.py:652
  322.7 3.8 collective-permute-done.72
  328.0 3.3 collective-permute-done.73
  331.7 1.9 collective-permute-start.53
  339.0 13.2 %collective-permute-done.65 = bf16[2,192,512]{2,1,0:T(8,128)(2,1)S(1)} collective-permute-done((bf16[2,192,512]{2,1,0:T(8,128)(2,1)S(1)}, bf16[2,192,512]{2,1,0:T(8,128)(2,1)S(1)}, u32[]{:S(2)}, u32[]{:S(2)}) %collective-permute-start.65) | collective-permute-done | bytes 393248 | tf_op jit(solution)/shard_map/ppermute | solution.py:652
  353.4 3.1 collective-permute-start.66
  356.8 11.9 %collective-permute-done.66 = bf16[1,192,512]{2,1,0:T(8,128)(2,1)S(1)} collective-permute-done((bf16[1,192,512]{2,1,0:T(8,128)(2,1)S(1)}, bf16[1,192,512]{2,1,0:T(8,128)(2,1)S(1)}, u32[]{:S(2)}, u32[]{:S(2)}) %collective-permute-start.66) | collective-permute-done | bytes 196640 | tf_op jit(solution)/shard_map/ppermute | solution.py:652
  375.5 5.3 %collective-permute-done.58 = bf16[64,3072]{1,0:T(8,128)(2,1)S(1)} collective-permute-done((bf16[64,3072]{1,0:T(8,128)(2,1)S(1)}, bf16[64,3072]{1,0:T(8,128)(2,1)S(1)}, u32[]{:S(2)}, u32[]{:S(2)}) %collective-permute-start.58) | collective-permute-done | bytes 393248 | tf_op jit(solution)/shard_map/ppermute | solution.py:652
  381.0 1.7 collective-permute-done.77
  383.6 3.3 shard_map.276
  387.4 2.1 slice_convert_fusion
  (434 shorter events, 128.8 us)
Async XLA Ops:
  0.7 19.7 %collective-permute-start = (bf16[1,192,384]{2,1,0:T(8,128)(2,1)}, bf16[1,192,384]{2,1,0:T(8,128)(2,1)}, u32[]{:S(2)}, u32[]{:S(2)}) collective-permute-start(bf16[1,192,384]{2,1,0:T(8,128)(2,1)} %bitcast.158), channel_id=1, source_target_pairs={{0,16},{8,24},{16,0},{24,8},{1,17},{9,25},{17,1},{25,9},{2,18},{10... | collective-permute-start | bytes 442376 | tf_op jit(solution)/shard_map/ppermute | solution.py:652
  20.0 7.9 %collective-permute-start.7 = (bf16[2,256,128]{2,1,0:T(8,128)(2,1)S(1)}, bf16[2,256,128]{2,1,0:T(8,128)(2,1)S(1)}, u32[]{:S(2)}, u32[]{:S(2)}) collective-permute-start(bf16[2,256,128]{2,1,0:T(8,128)(2,1)S(1)} %pad_maximum_fusion.8), channel_id=1, source_target_pairs={{0,8},{8,0},{16,24},{24,16},{1,9},{9,1},{17,25},{25,17},{2,10},{10... | collective-permute-start | bytes 393224 | tf_op jit(solution)/shard_map/ppermute | solution.py:652
  21.4 12.7 %collective-permute-start.2 = (bf16[2,192,384]{2,1,0:T(8,128)(2,1)S(1)}, bf16[2,192,384]{2,1,0:T(8,128)(2,1)}, u32[]{:S(2)}, u32[]{:S(2)}) collective-permute-start(bf16[2,192,384]{2,1,0:T(8,128)(2,1)S(1)} %pad_maximum_fusion.5.refs_0_), channel_id=1, source_target_pairs={{0,8},{8,0},{16,24},{24,16},{1,9},{9,1},{17,25},{25,17},{2,10},{10... | collective-permute-start | bytes 884744 | tf_op jit(solution)/shard_map/ppermute | solution.py:652
  23.2 21.2 %collective-permute-start.9 = (bf16[2,192,384]{2,1,0:T(8,128)(2,1)S(1)}, bf16[2,192,384]{2,1,0:T(8,128)(2,1)}, u32[]{:S(2)}, u32[]{:S(2)}) collective-permute-start(bf16[2,192,384]{2,1,0:T(8,128)(2,1)S(1)} %pad_maximum_fusion.5.refs_0_), channel_id=1, source_target_pairs={{0,4},{4,0},{1,5},{5,1},{2,6},{6,2},{3,7},{7,3},{8,12},{12,8},{9,1... | collective-permute-start | bytes 884744 | tf_op jit(solution)/shard_map/ppermute | solution.py:652
  24.7 7.4 %collective-permute-start.1 = (bf16[1,192,384]{2,1,0:T(8,128)(2,1)S(1)}, bf16[1,192,384]{2,1,0:T(8,128)(2,1)S(1)}, u32[]{:S(2)}, u32[]{:S(2)}) collective-permute-start(bf16[1,192,384]{2,1,0:T(8,128)(2,1)S(1)} %bitcast.152), channel_id=1, source_target_pairs={{0,16},{8,24},{16,0},{24,8},{1,17},{9,25},{17,1},{25,9},{2,18},{10... | collective-permute-start | bytes 442376 | tf_op jit(solution)/shard_map/ppermute | solution.py:652
  28.9 11.3 %collective-permute-start.8 = (bf16[4,256,128]{2,1,0:T(8,128)(2,1)S(1)}, bf16[4,256,128]{2,1,0:T(8,128)(2,1)}, u32[]{:S(2)}, u32[]{:S(2)}) collective-permute-start(bf16[4,256,128]{2,1,0:T(8,128)(2,1)S(1)} %pad_maximum_fusion.6.refs_0_), channel_id=1, source_target_pairs={{0,4},{4,0},{1,5},{5,1},{2,6},{6,2},{3,7},{7,3},{8,12},{12,8},{9,1... | collective-permute-start | bytes 786440 | tf_op jit(solution)/shard_map/ppermute | solution.py:652
  34.1 10.3 %collective-permute-start.3 = (bf16[2,192,384]{2,1,0:T(8,128)(2,1)}, bf16[2,192,384]{2,1,0:T(8,128)(2,1)}, u32[]{:S(2)}, u32[]{:S(2)}) collective-permute-start(bf16[2,192,384]{2,1,0:T(8,128)(2,1)} %pad_maximum_fusion.4), channel_id=1, source_target_pairs={{0,8},{8,0},{16,24},{24,16},{1,9},{9,1},{17,25},{25,17},{2,10},{10... | collective-permute-start | bytes 884744 | tf_op jit(solution)/shard_map/ppermute | solution.py:652
  36.4 8.1 %collective-permute-start.10 = (bf16[2,192,384]{2,1,0:T(8,128)(2,1)}, bf16[2,192,384]{2,1,0:T(8,128)(2,1)}, u32[]{:S(2)}, u32[]{:S(2)}) collective-permute-start(bf16[2,192,384]{2,1,0:T(8,128)(2,1)} %collective-permute-done.2.refs_1_), channel_id=1, source_target_pairs={{0,4},{4,0},{1,5},{5,1},{2,6},{6,2},{3,7},{7,3},{8,12},{12,8},{9,1... | collective-permute-start | bytes 884744 | tf_op jit(solution)/shard_map/ppermute | solution.py:652
  39.1 31.3 %collective-permute-start.13 = (bf16[3,64,560]{2,1,0:T(8,128)(2,1)}, bf16[3,64,560]{2,1,0:T(8,128)(2,1)S(1)}, u32[]{:S(2)}, u32[]{:S(2)}) collective-permute-start(bf16[3,64,560]{2,1,0:T(8,128)(2,1)} %get-tuple-element.146), channel_id=1, source_target_pairs={{0,16},{8,24},{16,0},{24,8},{1,17},{9,25},{17,1},{25,9},{2,18},{10... | collective-permute-start | bytes 645128 | tf_op jit(solution)/shard_map/ppermute | solution.py:652
  50.7 8.5 %collective-permute-start.11 = (bf16[256,128]{1,0:T(8,128)(2,1)}, bf16[256,128]{1,0:T(8,128)(2,1)S(1)}, u32[]{:S(2)}, u32[]{:S(2)}) collective-permute-start(bf16[256,128]{1,0:T(8,128)(2,1)} %get-tuple-element.143), channel_id=1, source_target_pairs={{0,4},{1,5},{2,6},{3,7},{8,12},{9,13},{10,14},{11,15},{16,20},{17,... | collective-permute-start | bytes 196616 | tf_op jit(solution)/shard_map/ppermute | solution.py:652
  55.4 8.9 %collective-permute-start.16 = (bf16[64,1536]{1,0:T(8,128)(2,1)S(1)}, bf16[64,1536]{1,0:T(8,128)(2,1)S(1)}, u32[]{:S(2)}, u32[]{:S(2)}) collective-permute-start(bf16[64,1536]{1,0:T(8,128)(2,1)S(1)} %copy-done.58), channel_id=1, source_target_pairs={{0,16},{8,24},{16,0},{24,8},{1,17},{9,25},{17,1},{25,9},{2,18},{10... | collective-permute-start | bytes 589832 | tf_op jit(solution)/shard_map/ppermute | solution.py:652
  59.1 11.9 %collective-permute-start.14 = (bf16[4,192,384]{2,1,0:T(8,128)(2,1)S(1)}, bf16[4,192,384]{2,1,0:T(8,128)(2,1)}, u32[]{:S(2)}, u32[]{:S(2)}) collective-permute-start(bf16[4,192,384]{2,1,0:T(8,128)(2,1)S(1)} %pad_maximum_fusion.1.refs_0_), channel_id=1, source_target_pairs={{0,4},{4,0},{1,5},{5,1},{2,6},{6,2},{3,7},{7,3},{8,12},{12,8},{9,1... | collective-permute-start | bytes 1769480 | tf_op jit(solution)/shard_map/ppermute | solution.py:652
  65.2 16.0 %collective-permute-start.17 = (bf16[128,1536]{1,0:T(8,128)(2,1)}, bf16[128,1536]{1,0:T(8,128)(2,1)}, u32[]{:S(2)}, u32[]{:S(2)}) collective-permute-start(bf16[128,1536]{1,0:T(8,128)(2,1)} %pad_maximum_fusion.2), channel_id=1, source_target_pairs={{0,8},{8,0},{16,24},{24,16},{1,9},{9,1},{17,25},{25,17},{2,10},{10... | collective-permute-start | bytes 1179656 | tf_op jit(solution)/shard_map/ppermute | solution.py:652
  65.8 15.4 %collective-permute-start.15 = (bf16[3,64,560]{2,1,0:T(8,128)(2,1)S(1)}, bf16[3,64,560]{2,1,0:T(8,128)(2,1)S(1)}, u32[]{:S(2)}, u32[]{:S(2)}) collective-permute-start(bf16[3,64,560]{2,1,0:T(8,128)(2,1)S(1)} %copy-done.47), channel_id=1, source_target_pairs={{0,16},{8,24},{16,0},{24,8},{1,17},{9,25},{17,1},{25,9},{2,18},{10... | collective-permute-start | bytes 645128 | tf_op jit(solution)/shard_map/ppermute | solution.py:652
  82.2 19.6 %collective-permute-start.20 = (bf16[3,64,560]{2,1,0:T(8,128)(2,1)S(1)}, bf16[3,64,560]{2,1,0:T(8,128)(2,1)S(1)}, u32[]{:S(2)}, u32[]{:S(2)}) collective-permute-start(bf16[3,64,560]{2,1,0:T(8,128)(2,1)S(1)} %copy-done.45), channel_id=1, source_target_pairs={{0,16},{8,24},{16,0},{24,8},{1,17},{9,25},{17,1},{25,9},{2,18},{10... | collective-permute-start | bytes 645128 | tf_op jit(solution)/shard_map/ppermute | solution.py:652
  82.3 21.1 %collective-permute-start.21 = (bf16[3,192,560]{2,1,0:T(8,128)(2,1)S(1)}, bf16[3,192,560]{2,1,0:T(8,128)(2,1)S(1)}, u32[]{:S(2)}, u32[]{:S(2)}) collective-permute-start(bf16[3,192,560]{2,1,0:T(8,128)(2,1)S(1)} %get-tuple-element.161.refs_0_), channel_id=1, source_target_pairs={{0,4},{4,0},{1,5},{5,1},{2,6},{6,2},{3,7},{7,3},{8,12},{12,8},{9,1... | collective-permute-start | bytes 1935368 | tf_op jit(solution)/shard_map/ppermute | solution.py:652
  82.4 21.0 %collective-permute-start.22 = (bf16[128,1536]{1,0:T(8,128)(2,1)}, bf16[128,1536]{1,0:T(8,128)(2,1)S(1)}, u32[]{:S(2)}, u32[]{:S(2)}) collective-permute-start(bf16[128,1536]{1,0:T(8,128)(2,1)} %pad_maximum_fusion.2), channel_id=1, source_target_pairs={{0,2},{1,3},{2,0},{3,1},{4,6},{5,7},{6,4},{7,5},{8,10},{9,11},{10,... | collective-permute-start | bytes 1179656 | tf_op jit(solution)/shard_map/ppermute | solution.py:652
  83.9 30.2 %collective-permute-start.24 = (bf16[3,192,560]{2,1,0:T(8,128)(2,1)}, bf16[3,192,560]{2,1,0:T(8,128)(2,1)S(1)}, u32[]{:S(2)}, u32[]{:S(2)}) collective-permute-start(bf16[3,192,560]{2,1,0:T(8,128)(2,1)} %get-tuple-element.165), channel_id=1, source_target_pairs={{0,8},{8,0},{16,24},{24,16},{1,9},{9,1},{17,25},{25,17},{2,10},{10... | collective-permute-start | bytes 1935368 | tf_op jit(solution)/shard_map/ppermute | solution.py:652
  87.8 10.5 %collective-permute-start.19 = (bf16[64,1536]{1,0:T(8,128)(2,1)S(1)}, bf16[64,1536]{1,0:T(8,128)(2,1)S(1)}, u32[]{:S(2)}, u32[]{:S(2)}) collective-permute-start(bf16[64,1536]{1,0:T(8,128)(2,1)S(1)} %fusion.41), channel_id=1, source_target_pairs={{0,2},{1,3},{2,0},{3,1},{4,6},{5,7},{6,4},{7,5},{8,10},{9,11},{10,... | collective-permute-start | bytes 589832 | tf_op jit(solution)/shard_map/ppermute | solution.py:652
  98.3 8.1 %collective-permute-start.25 = (bf16[3,64,560]{2,1,0:T(8,128)(2,1)S(1)}, bf16[3,64,560]{2,1,0:T(8,128)(2,1)S(1)}, u32[]{:S(2)}, u32[]{:S(2)}) collective-permute-start(bf16[3,64,560]{2,1,0:T(8,128)(2,1)S(1)} %collective-permute-done.13.refs_2_), channel_id=1, source_target_pairs={{0,4},{4,0},{1,5},{5,1},{2,6},{6,2},{3,7},{7,3},{8,12},{12,8},{9,1... | collective-permute-start | bytes 645128 | tf_op jit(solution)/shard_map/ppermute | solution.py:652
  101.8 12.4 %collective-permute-start.27 = (bf16[128,1536]{1,0:T(8,128)(2,1)}, bf16[128,1536]{1,0:T(8,128)(2,1)S(1)}, u32[]{:S(2)}, u32[]{:S(2)}) collective-permute-start(bf16[128,1536]{1,0:T(8,128)(2,1)} %collective-permute-done.17), channel_id=1, source_target_pairs={{0,2},{1,3},{2,0},{3,1},{4,6},{5,7},{6,4},{7,5},{8,10},{9,11},{10,... | collective-permute-start | bytes 1179656 | tf_op jit(solution)/shard_map/ppermute | solution.py:652
  103.4 10.7 %collective-permute-start.23 = (bf16[64,1536]{1,0:T(8,128)(2,1)S(1)}, bf16[64,1536]{1,0:T(8,128)(2,1)S(1)}, u32[]{:S(2)}, u32[]{:S(2)}) collective-permute-start(bf16[64,1536]{1,0:T(8,128)(2,1)S(1)} %multiply_convert_fusion), channel_id=1, source_target_pairs={{0,16},{8,24},{16,0},{24,8},{1,17},{9,25},{17,1},{25,9},{2,18},{10... | collective-permute-start | bytes 589832 | tf_op jit(solution)/shard_map/ppermute | solution.py:652
  106.4 7.7 %collective-permute-start.26 = (bf16[3,64,560]{2,1,0:T(8,128)(2,1)S(1)}, bf16[3,64,560]{2,1,0:T(8,128)(2,1)S(1)}, u32[]{:S(2)}, u32[]{:S(2)}) collective-permute-start(bf16[3,64,560]{2,1,0:T(8,128)(2,1)S(1)} %copy-done.35), channel_id=1, source_target_pairs={{0,4},{4,0},{1,5},{5,1},{2,6},{6,2},{3,7},{7,3},{8,12},{12,8},{9,1... | collective-permute-start | bytes 645128 | tf_op jit(solution)/shard_map/ppermute | solution.py:652
  114.2 16.3 %collective-permute-start.28 = (bf16[128,1536]{1,0:T(8,128)(2,1)S(1)}, bf16[128,1536]{1,0:T(8,128)(2,1)S(1)}, u32[]{:S(2)}, u32[]{:S(2)}) collective-permute-start(bf16[128,1536]{1,0:T(8,128)(2,1)S(1)} %get-tuple-element.169), channel_id=1, source_target_pairs={{0,8},{8,0},{16,24},{24,16},{1,9},{9,1},{17,25},{25,17},{2,10},{10... | collective-permute-start | bytes 1179656 | tf_op jit(solution)/shard_map/ppermute | solution.py:652
  116.0 18.1 %collective-permute-start.29 = (bf16[128,1536]{1,0:T(8,128)(2,1)S(1)}, bf16[128,1536]{1,0:T(8,128)(2,1)S(1)}, u32[]{:S(2)}, u32[]{:S(2)}) collective-permute-start(bf16[128,1536]{1,0:T(8,128)(2,1)S(1)} %get-tuple-element.169), channel_id=1, source_target_pairs={{0,2},{1,3},{2,0},{3,1},{4,6},{5,7},{6,4},{7,5},{8,10},{9,11},{10,... | collective-permute-start | bytes 1179656 | tf_op jit(solution)/shard_map/ppermute | solution.py:652
  117.6 12.8 %collective-permute-start.30 = (bf16[3,64,560]{2,1,0:T(8,128)(2,1)S(1)}, bf16[3,64,560]{2,1,0:T(8,128)(2,1)S(1)}, u32[]{:S(2)}, u32[]{:S(2)}) collective-permute-start(bf16[3,64,560]{2,1,0:T(8,128)(2,1)S(1)} %copy-done.43), channel_id=1, source_target_pairs={{0,24},{8,16},{16,8},{24,0},{1,25},{9,17},{17,9},{25,1},{2,26},{10... | collective-permute-start | bytes 645128 | tf_op jit(solution)/shard_map/ppermute | solution.py:652
  119.3 19.6 %collective-permute-start.33 = (bf16[3,192,560]{2,1,0:T(8,128)(2,1)S(1)}, bf16[3,192,560]{2,1,0:T(8,128)(2,1)S(1)}, u32[]{:S(2)}, u32[]{:S(2)}) collective-permute-start(bf16[3,192,560]{2,1,0:T(8,128)(2,1)S(1)} %collective-permute-done.24.refs_1_), channel_id=1, source_target_pairs={{0,4},{4,0},{1,5},{5,1},{2,6},{6,2},{3,7},{7,3},{8,12},{12,8},{9,1... | collective-permute-start | bytes 1935368 | tf_op jit(solution)/shard_map/ppermute | solution.py:652
  130.4 8.4 %collective-permute-start.31 = (bf16[128,1536]{1,0:T(8,128)(2,1)S(1)}, bf16[128,1536]{1,0:T(8,128)(2,1)S(1)}, u32[]{:S(2)}, u32[]{:S(2)}) collective-permute-start(bf16[128,1536]{1,0:T(8,128)(2,1)S(1)} %collective-permute-done.28), channel_id=1, source_target_pairs={{0,2},{1,3},{2,0},{3,1},{4,6},{5,7},{6,4},{7,5},{8,10},{9,11},{10,... | collective-permute-start | bytes 1179656 | tf_op jit(solution)/shard_map/ppermute | solution.py:652
  132.0 8.1 %collective-permute-start.32 = (bf16[3,64,560]{2,1,0:T(8,128)(2,1)S(1)}, bf16[3,64,560]{2,1,0:T(8,128)(2,1)S(1)}, u32[]{:S(2)}, u32[]{:S(2)}) collective-permute-start(bf16[3,64,560]{2,1,0:T(8,128)(2,1)S(1)} %copy-done.41), channel_id=1, source_target_pairs={{0,24},{8,16},{16,8},{24,0},{1,25},{9,17},{17,9},{25,1},{2,26},{10... | collective-permute-start | bytes 645128 | tf_op jit(solution)/shard_map/ppermute | solution.py:652
  134.1 32.5 %collective-permute-start.35 = (bf16[512,1536]{1,0:T(8,128)(2,1)S(1)}, bf16[512,1536]{1,0:T(8,128)(2,1)S(1)}, u32[]{:S(2)}, u32[]{:S(2)}) collective-permute-start(bf16[512,1536]{1,0:T(8,128)(2,1)S(1)} %constant_dynamic-update-slice_fusion.9.cot_ref.refs_2_), channel_id=1, source_target_pairs={{0,1},{1,0},{2,3},{3,2},{4,5},{5,4},{6,7},{7,6},{8,9},{9,8},{10,11... | collective-permute-start | bytes 4718600 | tf_op jit(solution)/shard_map/ppermute | solution.py:652
  140.1 26.5 %collective-permute-start.34 = (bf16[512,1536]{1,0:T(8,128)(2,1)S(1)}, bf16[512,1536]{1,0:T(8,128)(2,1)S(1)}, u32[]{:S(2)}, u32[]{:S(2)}) collective-permute-start(bf16[512,1536]{1,0:T(8,128)(2,1)S(1)} %constant_dynamic-update-slice_fusion.4.n2_ref.refs_0_), channel_id=1, source_target_pairs={{0,1},{1,0},{2,3},{3,2},{4,5},{5,4},{6,7},{7,6},{8,9},{9,8},{10,11... | collective-permute-start | bytes 4718600 | tf_op jit(solution)/shard_map/ppermute | solution.py:652
  140.1 8.4 %collective-permute-start.38 = (bf16[3,64,560]{2,1,0:T(8,128)(2,1)S(1)}, bf16[3,64,560]{2,1,0:T(8,128)(2,1)S(1)}, u32[]{:S(2)}, u32[]{:S(2)}) collective-permute-start(bf16[3,64,560]{2,1,0:T(8,128)(2,1)S(1)} %collective-permute-done.30.refs_5_), channel_id=1, source_target_pairs={{0,4},{4,0},{1,5},{5,1},{2,6},{6,2},{3,7},{7,3},{8,12},{12,8},{9,1... | collective-permute-start | bytes 645128 | tf_op jit(solution)/shard_map/ppermute | solution.py:652
  148.4 8.9 %collective-permute-start.39 = (bf16[3,64,560]{2,1,0:T(8,128)(2,1)S(1)}, bf16[3,64,560]{2,1,0:T(8,128)(2,1)S(1)}, u32[]{:S(2)}, u32[]{:S(2)}) collective-permute-start(bf16[3,64,560]{2,1,0:T(8,128)(2,1)S(1)} %collective-permute-done.32.refs_6_), channel_id=1, source_target_pairs={{0,4},{4,0},{1,5},{5,1},{2,6},{6,2},{3,7},{7,3},{8,12},{12,8},{9,1... | collective-permute-start | bytes 645128 | tf_op jit(solution)/shard_map/ppermute | solution.py:652
  148.7 9.3 %collective-permute-start.36 = (bf16[3,64,560]{2,1,0:T(8,128)(2,1)S(1)}, bf16[3,64,560]{2,1,0:T(8,128)(2,1)S(1)}, u32[]{:S(2)}, u32[]{:S(2)}) collective-permute-start(bf16[3,64,560]{2,1,0:T(8,128)(2,1)S(1)} %copy-done.39), channel_id=1, source_target_pairs={{0,24},{8,16},{16,8},{24,0},{1,25},{9,17},{17,9},{25,1},{2,26},{10... | collective-permute-start | bytes 645128 | tf_op jit(solution)/shard_map/ppermute | solution.py:652
  150.8 11.8 %collective-permute-start.37 = (bf16[3,64,560]{2,1,0:T(8,128)(2,1)S(1)}, bf16[3,64,560]{2,1,0:T(8,128)(2,1)S(1)}, u32[]{:S(2)}, u32[]{:S(2)}) collective-permute-start(bf16[3,64,560]{2,1,0:T(8,128)(2,1)S(1)} %collective-permute-done.20.refs_4_), channel_id=1, source_target_pairs={{0,4},{4,0},{1,5},{5,1},{2,6},{6,2},{3,7},{7,3},{8,12},{12,8},{9,1... | collective-permute-start | bytes 645128 | tf_op jit(solution)/shard_map/ppermute | solution.py:652
  158.0 8.6 %collective-permute-start.40 = (bf16[3,64,560]{2,1,0:T(8,128)(2,1)S(1)}, bf16[3,64,560]{2,1,0:T(8,128)(2,1)S(1)}, u32[]{:S(2)}, u32[]{:S(2)}) collective-permute-start(bf16[3,64,560]{2,1,0:T(8,128)(2,1)S(1)} %collective-permute-done.36.refs_7_), channel_id=1, source_target_pairs={{0,4},{4,0},{1,5},{5,1},{2,6},{6,2},{3,7},{7,3},{8,12},{12,8},{9,1... | collective-permute-start | bytes 645128 | tf_op jit(solution)/shard_map/ppermute | solution.py:652
  176.2 14.0 %collective-permute-start.41 = (bf16[512,1536]{1,0:T(8,128)(2,1)S(1)}, bf16[512,1536]{1,0:T(8,128)(2,1)S(1)}, u32[]{:S(2)}, u32[]{:S(2)}) collective-permute-start(bf16[512,1536]{1,0:T(8,128)(2,1)S(1)} %get-tuple-element.189), channel_id=1, source_target_pairs={{0,1},{1,0},{2,3},{3,2},{4,5},{5,4},{6,7},{7,6},{8,9},{9,8},{10,11... | collective-permute-start | bytes 4718600 | tf_op jit(solution)/shard_map/ppermute | solution.py:652
  192.7 19.4 %collective-permute-start.43 = (bf16[128,1536]{1,0:T(8,128)(2,1)}, bf16[128,1536]{1,0:T(8,128)(2,1)}, u32[]{:S(2)}, u32[]{:S(2)}) collective-permute-start(bf16[128,1536]{1,0:T(8,128)(2,1)} %get-tuple-element.271), channel_id=1, source_target_pairs={{0,2},{1,3},{2,0},{3,1},{4,6},{5,7},{6,4},{7,5},{8,10},{9,11},{10,... | collective-permute-start | bytes 1179656 | tf_op jit(solution)/shard_map/ppermute | solution.py:652
  210.5 12.6 %collective-permute-start.42 = (bf16[128,1536]{1,0:T(8,128)(2,1)S(1)}, bf16[128,1536]{1,0:T(8,128)(2,1)S(1)}, u32[]{:S(2)}, u32[]{:S(2)}) collective-permute-start(bf16[128,1536]{1,0:T(8,128)(2,1)S(1)} %copy-done.81), channel_id=1, source_target_pairs={{0,2},{1,3},{2,0},{3,1},{4,6},{5,7},{6,4},{7,5},{8,10},{9,11},{10,... | collective-permute-start | bytes 1179656 | tf_op jit(solution)/shard_map/ppermute | solution.py:652
  213.3 11.7 %collective-permute-start.44 = (bf16[128,1536]{1,0:T(8,128)(2,1)S(1)}, bf16[128,1536]{1,0:T(8,128)(2,1)S(1)}, u32[]{:S(2)}, u32[]{:S(2)}) collective-permute-start(bf16[128,1536]{1,0:T(8,128)(2,1)S(1)} %add_convert_fusion.5), channel_id=1, source_target_pairs={{0,8},{8,0},{16,24},{24,16},{1,9},{9,1},{17,25},{25,17},{2,10},{10... | collective-permute-start | bytes 1179656 | tf_op jit(solution)/shard_map/ppermute | solution.py:652
  216.2 18.1 %collective-permute-start.46 = (bf16[3,192,560]{2,1,0:T(8,128)(2,1)S(1)}, bf16[3,192,560]{2,1,0:T(8,128)(2,1)S(1)}, u32[]{:S(2)}, u32[]{:S(2)}) collective-permute-start(bf16[3,192,560]{2,1,0:T(8,128)(2,1)S(1)} %get-tuple-element.203), channel_id=1, source_target_pairs={{0,4},{4,0},{1,5},{5,1},{2,6},{6,2},{3,7},{7,3},{8,12},{12,8},{9,1... | collective-permute-start | bytes 1935368 | tf_op jit(solution)/shard_map/ppermute | solution.py:652
  225.2 11.4 %collective-permute-start.45 = (bf16[64,1536]{1,0:T(8,128)(2,1)S(1)}, bf16[64,1536]{1,0:T(8,128)(2,1)S(1)}, u32[]{:S(2)}, u32[]{:S(2)}) collective-permute-start(bf16[64,1536]{1,0:T(8,128)(2,1)S(1)} %slice.437), channel_id=1, source_target_pairs={{0,16},{8,24},{16,0},{24,8},{1,17},{9,25},{17,1},{25,9},{2,18},{10... | collective-permute-start | bytes 589832 | tf_op jit(solution)/shard_map/ppermute | solution.py:652
  234.4 17.2 %collective-permute-start.50 = (bf16[3,192,560]{2,1,0:T(8,128)(2,1)S(1)}, bf16[3,192,560]{2,1,0:T(8,128)(2,1)S(1)}, u32[]{:S(2)}, u32[]{:S(2)}) collective-permute-start(bf16[3,192,560]{2,1,0:T(8,128)(2,1)S(1)} %get-tuple-element.209), channel_id=1, source_target_pairs={{0,4},{4,0},{1,5},{5,1},{2,6},{6,2},{3,7},{7,3},{8,12},{12,8},{9,1... | collective-permute-start | bytes 1935368 | tf_op jit(solution)/shard_map/ppermute | solution.py:652
  243.7 10.8 %collective-permute-start.48 = (bf16[2,64,1536]{2,1,0:T(8,128)(2,1)S(1)}, bf16[2,64,1536]{2,1,0:T(8,128)(2,1)S(1)}, u32[]{:S(2)}, u32[]{:S(2)}) collective-permute-start(bf16[2,64,1536]{2,1,0:T(8,128)(2,1)S(1)} %maximum_select_fusion.4), channel_id=1, source_target_pairs={{0,1},{1,0},{2,3},{3,2},{4,5},{5,4},{6,7},{7,6},{8,9},{9,8},{10,11... | collective-permute-start | bytes 1179656 | tf_op jit(solution)/shard_map/ppermute | solution.py:652
  251.5 27.4 %collective-permute-start.61 = (bf16[3,192,560]{2,1,0:T(8,128)(2,1)}, bf16[3,192,560]{2,1,0:T(8,128)(2,1)}, u32[]{:S(2)}, u32[]{:S(2)}) collective-permute-start(bf16[3,192,560]{2,1,0:T(8,128)(2,1)} %get-tuple-element.222), channel_id=1, source_target_pairs={{0,4},{4,0},{1,5},{5,1},{2,6},{6,2},{3,7},{7,3},{8,12},{12,8},{9,1... | collective-permute-start | bytes 1935368 | tf_op jit(solution)/shard_map/ppermute | solution.py:652
  253.0 28.1 %collective-permute-start.62 = (bf16[3,192,560]{2,1,0:T(8,128)(2,1)}, bf16[3,192,560]{2,1,0:T(8,128)(2,1)S(1)}, u32[]{:S(2)}, u32[]{:S(2)}) collective-permute-start(bf16[3,192,560]{2,1,0:T(8,128)(2,1)} %add_convert_fusion.3), channel_id=1, source_target_pairs={{0,24},{8,16},{16,8},{24,0},{1,25},{9,17},{17,9},{25,1},{2,26},{10... | collective-permute-start | bytes 1935368 | tf_op jit(solution)/shard_map/ppermute | solution.py:652
  260.9 9.9 %collective-permute-start.55 = (f32[256,128]{1,0:T(8,128)S(1)}, f32[256,128]{1,0:T(8,128)S(1)}, u32[]{:S(2)}, u32[]{:S(2)}) collective-permute-start(f32[256,128]{1,0:T(8,128)S(1)} %slice.319), channel_id=1, source_target_pairs={{4,0},{5,1},{6,2},{7,3},{12,8},{13,9},{14,10},{15,11},{20,16},{21,... | collective-permute-start | bytes 393224 | tf_op jit(solution)/shard_map/ppermute | solution.py:652
  277.9 11.2 %collective-permute-start.56 = (bf16[2,64,1536]{2,1,0:T(8,128)(2,1)}, bf16[2,64,1536]{2,1,0:T(8,128)(2,1)}, u32[]{:S(2)}, u32[]{:S(2)}) collective-permute-start(bf16[2,64,1536]{2,1,0:T(8,128)(2,1)} %fusion.31), channel_id=1, source_target_pairs={{0,1},{1,0},{2,3},{3,2},{4,5},{5,4},{6,7},{7,6},{8,9},{9,8},{10,11... | collective-permute-start | bytes 1179656 | tf_op jit(solution)/shard_map/ppermute | solution.py:652
  281.1 87.7 %collective-permute-start.67 = (bf16[3,192,560]{2,1,0:T(8,128)(2,1)}, bf16[3,192,560]{2,1,0:T(8,128)(2,1)S(1)}, u32[]{:S(2)}, u32[]{:S(2)}) collective-permute-start(bf16[3,192,560]{2,1,0:T(8,128)(2,1)} %add_convert_fusion.1), channel_id=1, source_target_pairs={{0,16},{8,24},{16,0},{24,8},{1,17},{9,25},{17,1},{25,9},{2,18},{10... | collective-permute-start | bytes 1935368 | tf_op jit(solution)/shard_map/ppermute | solution.py:652
  288.8 12.0 %collective-permute-start.60 = (bf16[2,192,512]{2,1,0:T(8,128)(2,1)}, bf16[2,192,512]{2,1,0:T(8,128)(2,1)}, u32[]{:S(2)}, u32[]{:S(2)}) collective-permute-start(bf16[2,192,512]{2,1,0:T(8,128)(2,1)} %get-tuple-element.218), channel_id=1, source_target_pairs={{0,4},{4,0},{1,5},{5,1},{2,6},{6,2},{3,7},{7,3},{8,12},{12,8},{9,1... | collective-permute-start | bytes 1179656 | tf_op jit(solution)/shard_map/ppermute | solution.py:652
  291.1 7.0 %collective-permute-start.57 = (bf16[64,1536]{1,0:T(8,128)(2,1)}, bf16[64,1536]{1,0:T(8,128)(2,1)}, u32[]{:S(2)}, u32[]{:S(2)}) collective-permute-start(bf16[64,1536]{1,0:T(8,128)(2,1)} %fusion.42), channel_id=1, source_target_pairs={{0,2},{1,3},{2,0},{3,1},{4,6},{5,7},{6,4},{7,5},{8,10},{9,11},{10,... | collective-permute-start | bytes 589832 | tf_op jit(solution)/shard_map/ppermute | solution.py:652
  295.2 11.6 %collective-permute-start.63 = (bf16[2,192,512]{2,1,0:T(8,128)(2,1)}, bf16[2,192,512]{2,1,0:T(8,128)(2,1)}, u32[]{:S(2)}, u32[]{:S(2)}) collective-permute-start(bf16[2,192,512]{2,1,0:T(8,128)(2,1)} %get-tuple-element.225), channel_id=1, source_target_pairs={{0,4},{4,0},{1,5},{5,1},{2,6},{6,2},{3,7},{7,3},{8,12},{12,8},{9,1... | collective-permute-start | bytes 1179656 | tf_op jit(solution)/shard_map/ppermute | solution.py:652
  302.1 29.4 %collective-permute-start.52 = (bf16[256,1536]{1,0:T(8,128)(2,1)S(1)}, bf16[256,1536]{1,0:T(8,128)(2,1)S(1)}, u32[]{:S(2)}, u32[]{:S(2)}) collective-permute-start(bf16[256,1536]{1,0:T(8,128)(2,1)S(1)} %pad_maximum_fusion), channel_id=1, source_target_pairs={{0,2},{1,3},{2,0},{3,1},{4,6},{5,7},{6,4},{7,5},{8,10},{9,11},{10,... | collective-permute-start | bytes 2359304 | tf_op jit(solution)/shard_map/ppermute | solution.py:652
  303.6 29.9 %collective-permute-start.64 = (bf16[3,192,560]{2,1,0:T(8,128)(2,1)}, bf16[3,192,560]{2,1,0:T(8,128)(2,1)S(1)}, u32[]{:S(2)}, u32[]{:S(2)}) collective-permute-start(bf16[3,192,560]{2,1,0:T(8,128)(2,1)} %add_convert_fusion.2), channel_id=1, source_target_pairs={{0,8},{8,0},{16,24},{24,16},{1,9},{9,1},{17,25},{25,17},{2,10},{10... | collective-permute-start | bytes 1935368 | tf_op jit(solution)/shard_map/ppermute | solution.py:652
  303.6 34.6 %collective-permute-start.75 = (bf16[4,192,384]{2,1,0:T(8,128)(2,1)}, bf16[4,192,384]{2,1,0:T(8,128)(2,1)S(1)}, u32[]{:S(2)}, u32[]{:S(2)}) collective-permute-start(bf16[4,192,384]{2,1,0:T(8,128)(2,1)} %get-tuple-element.236), channel_id=1, source_target_pairs={{0,4},{4,0},{1,5},{5,1},{2,6},{6,2},{3,7},{7,3},{8,12},{12,8},{9,1... | collective-permute-start | bytes 1769480 | tf_op jit(solution)/shard_map/ppermute | solution.py:652
  306.8 15.8 %collective-permute-start.71 = (f32[40,128]{1,0:T(8,128)S(1)}, f32[40,128]{1,0:T(8,128)S(1)}, u32[]{:S(2)}, u32[]{:S(2)}) collective-permute-start(f32[40,128]{1,0:T(8,128)S(1)} %fusion.115), channel_id=1, source_target_pairs={{0,2},{1,3},{2,0},{3,1},{4,6},{5,7},{6,4},{7,5},{8,10},{9,11},{10,... | collective-permute-start | bytes 61448 | tf_op jit(solution)/shard_map/ppermute | solution.py:652
  331.7 21.7 %collective-permute-start.53 = (bf16[128,1536]{1,0:T(8,128)(2,1)S(1)}, bf16[128,1536]{1,0:T(8,128)(2,1)S(1)}, u32[]{:S(2)}, u32[]{:S(2)}) collective-permute-start(bf16[128,1536]{1,0:T(8,128)(2,1)S(1)} %fusion.19), channel_id=1, source_target_pairs={{0,8},{8,0},{16,24},{24,16},{1,9},{9,1},{17,25},{25,17},{2,10},{10... | collective-permute-start | bytes 1179656 | tf_op jit(solution)/shard_map/ppermute | solution.py:652
  333.5 18.7 %collective-permute-start.65 = (bf16[2,192,512]{2,1,0:T(8,128)(2,1)S(1)}, bf16[2,192,512]{2,1,0:T(8,128)(2,1)S(1)}, u32[]{:S(2)}, u32[]{:S(2)}) collective-permute-start(bf16[2,192,512]{2,1,0:T(8,128)(2,1)S(1)} %add_convert_fusion.4), channel_id=1, source_target_pairs={{0,8},{8,0},{16,24},{24,16},{1,9},{9,1},{17,25},{25,17},{2,10},{10... | collective-permute-start | bytes 1179656 | tf_op jit(solution)/shard_map/ppermute | solution.py:652
  338.3 34.7 %collective-permute-start.76 = (bf16[2,192,384]{2,1,0:T(8,128)(2,1)S(1)}, bf16[2,192,384]{2,1,0:T(8,128)(2,1)S(1)}, u32[]{:S(2)}, u32[]{:S(2)}) collective-permute-start(bf16[2,192,384]{2,1,0:T(8,128)(2,1)S(1)} %add_convert_fusion.8), channel_id=1, source_target_pairs={{0,8},{8,0},{16,24},{24,16},{1,9},{9,1},{17,25},{25,17},{2,10},{10... | collective-permute-start | bytes 884744 | tf_op jit(solution)/shard_map/ppermute | solution.py:652
  338.6 44.8 %collective-permute-start.78 = (bf16[3,192,560]{2,1,0:T(8,128)(2,1)S(1)}, bf16[3,192,560]{2,1,0:T(8,128)(2,1)S(1)}, u32[]{:S(2)}, u32[]{:S(2)}) collective-permute-start(bf16[3,192,560]{2,1,0:T(8,128)(2,1)S(1)} %copy-done.37), channel_id=1, source_target_pairs={{0,4},{4,0},{1,5},{5,1},{2,6},{6,2},{3,7},{7,3},{8,12},{12,8},{9,1... | collective-permute-start | bytes 1935368 | tf_op jit(solution)/shard_map/ppermute | solution.py:652
  353.4 15.3 %collective-permute-start.66 = (bf16[1,192,512]{2,1,0:T(8,128)(2,1)S(1)}, bf16[1,192,512]{2,1,0:T(8,128)(2,1)S(1)}, u32[]{:S(2)}, u32[]{:S(2)}) collective-permute-start(bf16[1,192,512]{2,1,0:T(8,128)(2,1)S(1)} %slice.435), channel_id=1, source_target_pairs={{0,16},{8,24},{16,0},{24,8},{1,17},{9,25},{17,1},{25,9},{2,18},{10... | collective-permute-start | bytes 589832 | tf_op jit(solution)/shard_map/ppermute | solution.py:652
  356.7 14.1 %collective-permute-start.54 = (bf16[64,1536]{1,0:T(8,128)(2,1)S(1)}, bf16[64,1536]{1,0:T(8,128)(2,1)S(1)}, u32[]{:S(2)}, u32[]{:S(2)}) collective-permute-start(bf16[64,1536]{1,0:T(8,128)(2,1)S(1)} %slice.436), channel_id=1, source_target_pairs={{0,16},{8,24},{16,0},{24,8},{1,17},{9,25},{17,1},{25,9},{2,18},{10... | collective-permute-start | bytes 589832 | tf_op jit(solution)/shard_map/ppermute | solution.py:652
  371.6 9.1 %collective-permute-start.58 = (bf16[64,3072]{1,0:T(8,128)(2,1)S(1)}, bf16[64,3072]{1,0:T(8,128)(2,1)S(1)}, u32[]{:S(2)}, u32[]{:S(2)}) collective-permute-start(bf16[64,3072]{1,0:T(8,128)(2,1)S(1)} %pad_maximum_fusion.3), channel_id=1, source_target_pairs={{0,2},{1,3},{2,0},{3,1},{4,6},{5,7},{6,4},{7,5},{8,10},{9,11},{10,... | collective-permute-start | bytes 1179656 | tf_op jit(solution)/shard_map/ppermute | solution.py:652
  373.2 9.5 %collective-permute-start.77 = (bf16[1,192,384]{2,1,0:T(8,128)(2,1)S(1)}, bf16[1,192,384]{2,1,0:T(8,128)(2,1)S(1)}, u32[]{:S(2)}, u32[]{:S(2)}) collective-permute-start(bf16[1,192,384]{2,1,0:T(8,128)(2,1)S(1)} %slice.438), channel_id=1, source_target_pairs={{0,16},{8,24},{16,0},{24,8},{1,17},{9,25},{17,1},{25,9},{2,18},{10... | collective-permute-start | bytes 442376 | tf_op jit(solution)/shard_map/ppermute | solution.py:652
  (109 other events, 1002.6 us)
